TPU v7x, 512 devices: a whole 4x8x8 slice. The times are simulated.
512 devices in a mesh: section: 4 (over y_lo, core), dp: 128 (over y_hi, x, z).
Axes of the slice: x: 4, y: 8 (y_hi: 4, y_lo: 2; y = y_hi * 2 + y_lo), z: 8, core: 2. Of those that a mesh axis runs over, the one named last changes fastest.
Arguments:
- student: bfloat16 [65536, 1024], P(('section', 'dp')), may hold values from -6 to 6
- teacher: bfloat16 [65536, 1024], P(('section', 'dp')), may hold values from -6 to 6
Outputs:
- student_grad: bfloat16 [65536, 1024], P(('section', 'dp'))
All inputs are finite; a program needn't handle non-finite values.
Results may differ from a plain program's by a relative error of at most 0.017.
Values may be sent and summed in bfloat16 or wider, within the bound.
No kernel may reach another device: no remote copies, remote signals or barrier semaphores. Data moves between devices by JAX's collectives and lax.ppermute only.
A program may use at most 64 MiB of HBM per device.

v0:
```python
import jax
import jax.numpy as jnp
from jax import lax
from jax.sharding import PartitionSpec as P

D = 1024
STEPS = 3


def from_behind(block, axis, distance):
    devices = range(lax.axis_size(axis))
    route = [((i - distance) % len(devices), i) for i in devices]
    return lax.ppermute(block, axis, route)


def unit_rows(rows):
    values = rows.astype(jnp.float32)
    inverse = lax.rsqrt(jnp.sum(values * values, axis=1, keepdims=True) + 1e-06)
    return ((values * inverse).astype(jnp.bfloat16), inverse)


def pair_weights(unit_s, unit_t, whole):
    contract = (((1,), (1,)), ((), ()))
    diff = lax.dot_general(unit_s, whole[0], contract, preferred_element_type=jnp.float32)
    diff = diff - lax.dot_general(unit_t, whole[1], contract, preferred_element_type=jnp.float32)
    return diff.astype(jnp.bfloat16)


def on_device(student, teacher):
    unit_s, inv_s = unit_rows(student)
    unit_t, unused = unit_rows(teacher)
    stacked = jnp.stack([unit_s, unit_t])
    moving = lax.all_gather(stacked, "section", axis=1, tiled=True)
    own_sum = jnp.zeros(unit_s.shape, jnp.float32)
    carried = None
    returned = None
    for step in range(STEPS):
        whole = moving
        weights = pair_weights(unit_s, unit_t, whole)
        forward = jnp.dot(weights, whole[0], preferred_element_type=jnp.float32)
        own_sum = own_sum + forward
        term = lax.dot_general(
            weights, unit_s, (((0,), (0,)), ((), ())), preferred_element_type=jnp.float32
        )
        carried = term if step == 0 else carried + term
        if step + 1 < STEPS:
            carried = from_behind(carried.astype(jnp.bfloat16), "dp", 1).astype(carried.dtype)
        if step + 1 < STEPS:
            moving = from_behind(moving, "dp", 1)
    returned = from_behind(carried.astype(jnp.bfloat16), "dp", 1 - STEPS).astype(carried.dtype)
    total = own_sum + lax.psum_scatter(
        returned.astype(jnp.bfloat16), "section", scatter_dimension=0, tiled=True
    ).astype(jnp.float32)
    unit_f = unit_s.astype(jnp.float32)
    along = jnp.sum(unit_f * total, axis=1, keepdims=True)
    return (D / 2.0 * inv_s * (total - unit_f * along)).astype(jnp.bfloat16)


def solution(mesh):
    placed = (P(("section", "dp"), None), P(("section", "dp"), None))
    return jax.shard_map(
        on_device, mesh=mesh, in_specs=placed, out_specs=P(("section", "dp"), None), check_vma=False
    )
```

profile of v0, /device:TPU:1, one launch (start us, length us, event | category | flops | bytes accessed | tf_op | source)
XLA Modules:
  0.0 433.7 jit_solution(16704419531291109098)
XLA Ops:
  6.5 0.0 copy-start
  6.5 0.0 all-gather.2.cloned.1.call-start
  6.5 1.1 fusion.10
  7.7 1.1 fusion.8
  8.8 0.0 copy-start.1
  8.8 1.2 fusion.19
  10.0 0.9 pad_maximum_fusion
  10.9 0.0 all-gather.2.cloned.1.call-update
  10.9 0.0 reduce-scatter.2.cloned.1.call-start
  10.9 40.5 %all-gather.2.cloned.1.call-done = bf16[2,512,1024]{2,1,0:T(8,128)(2,1)} async-done(((bf16[2,128,1024]{2,1,0:T(8,128)(2,1)}), bf16[2,512,1024]{2,1,0:T(8,128)(2,1)}) %all-gather.2.cloned.1.call-update) | async-done | bytes 2097168 | tf_op jit(solution)/shard_map/all_gather | solution.py:33
  51.4 3.3 collective-permute-start
  54.7 54.4 %collective-permute-done = bf16[2,512,1024]{2,1,0:T(8,128)(2,1)S(1)} collective-permute-done((bf16[2,512,1024]{2,1,0:T(8,128)(2,1)}, bf16[2,512,1024]{2,1,0:T(8,128)(2,1)S(1)}, u32[]{:S(2)}, u32[]{:S(2)}) %collective-permute-start) | collective-permute-done | bytes 2097184 | tf_op jit(solution)/shard_map/ppermute | solution.py:13
  109.1 0.0 copy-start.5
  109.1 1.9 collective-permute-start.1
  111.0 0.0 copy-done
  111.0 1.7 fusion.7
  112.7 0.0 copy-done.1
  112.8 1.7 fusion.1
  114.5 0.5 convolution_convert_fusion
  115.0 1.9 collective-permute-start.2
  116.9 0.5 fusion.5
  117.4 0.0 copy-done.5
  117.4 0.5 fusion.2
  117.9 103.9 %collective-permute-done.2 = bf16[512,1024]{1,0:T(8,128)(2,1)S(1)} collective-permute-done((bf16[512,1024]{1,0:T(8,128)(2,1)S(1)}, bf16[512,1024]{1,0:T(8,128)(2,1)S(1)}, u32[]{:S(2)}, u32[]{:S(2)}) %collective-permute-start.2) | collective-permute-done | bytes 1048608 | tf_op jit(solution)/shard_map/ppermute | solution.py:13
  221.8 0.5 add_convert_fusion.1
  222.3 1.9 collective-permute-start.3
  224.3 0.0 collective-permute-done.1
  224.3 0.0 copy-start.3
  224.3 0.5 fusion.4
  224.8 0.5 fusion.3
  225.3 0.5 fusion.20
  225.8 0.0 copy-done.3
  225.8 40.3 %collective-permute-done.3 = bf16[512,1024]{1,0:T(8,128)(2,1)S(1)} collective-permute-done((bf16[512,1024]{1,0:T(8,128)(2,1)S(1)}, bf16[512,1024]{1,0:T(8,128)(2,1)S(1)}, u32[]{:S(2)}, u32[]{:S(2)}) %collective-permute-start.3) | collective-permute-done | bytes 1048608 | tf_op jit(solution)/shard_map/ppermute | solution.py:13
  266.1 0.4 add_convert_fusion
  266.5 1.9 collective-permute-start.4
  268.4 26.9 %collective-permute-done.4 = bf16[512,1024]{1,0:T(8,128)(2,1)S(1)} collective-permute-done((bf16[512,1024]{1,0:T(8,128)(2,1)S(1)}, bf16[512,1024]{1,0:T(8,128)(2,1)S(1)}, u32[]{:S(2)}, u32[]{:S(2)}) %collective-permute-start.4) | collective-permute-done | bytes 1048608 | tf_op jit(solution)/shard_map/ppermute | solution.py:13
  295.3 0.0 copy-start.2
  295.3 1.0 copy-done.2
  296.3 0.0 reduce-scatter.2.cloned.1.call-update
  296.3 0.0 copy-start.4
  296.3 1.7 fusion.6
  298.0 1.5 convolution_add_fusion.1
  299.6 125.0 %reduce-scatter.2.cloned.1.call-done = bf16[128,1024]{1,0:T(8,128)(2,1)} async-done(((bf16[512,1024]{1,0:T(8,128)(2,1)}), bf16[128,1024]{1,0:T(8,128)(2,1)}) %reduce-scatter.2.cloned.1.call-update) | async-done | bytes 262160 | tf_op jit(solution)/shard_map/reduce_scatter | solution.py:51
  424.6 0.0 copy-done.4
  424.6 1.4 fusion.12
  425.9 0.9 fusion.15
  (2 shorter events, 0.0 us)
Async XLA Ops:
  6.5 104.5 %copy-start = (bf16[128,1024]{1,0:T(8,128)(2,1)S(1)}, bf16[128,1024]{1,0:T(8,128)(2,1)}, u32[]{:S(2)}) copy-start(bf16[128,1024]{1,0:T(8,128)(2,1)} %param.2) | copy-start | bytes 786436
  6.5 44.9 %all-gather.2.cloned.1.call-start = ((), (), s32[]{:S(2)}) async-start(), calls=%async_computation.1 | async-start | bytes 2621440 | tf_op jit(solution)/shard_map/all_gather | solution.py:33
  8.8 104.0 %copy-start.1 = (bf16[128,1024]{1,0:T(8,128)(2,1)S(1)}, bf16[128,1024]{1,0:T(8,128)(2,1)}, u32[]{:S(2)}) copy-start(bf16[128,1024]{1,0:T(8,128)(2,1)} %param.3) | copy-start | bytes 786436
  10.9 413.7 %reduce-scatter.2.cloned.1.call-start = ((), (), s32[]{:S(2)}) async-start(), calls=%async_computation.2 | async-start | bytes 1310720 | tf_op jit(solution)/shard_map/reduce_scatter | solution.py:51
  51.4 57.7 %collective-permute-start = (bf16[2,512,1024]{2,1,0:T(8,128)(2,1)}, bf16[2,512,1024]{2,1,0:T(8,128)(2,1)S(1)}, u32[]{:S(2)}, u32[]{:S(2)}) collective-permute-start(bf16[2,512,1024]{2,1,0:T(8,128)(2,1)} %all-gather.2.cloned.1.call-done), channel_id=1, source_target_pairs={{127,0},{0,1},{1,2},{2,3},{3,4},{4,5},{5,6},{6,7},{7,8},{8,9},{9,1... | collective-permute-start | bytes 6291464 | tf_op jit(solution)/shard_map/ppermute | solution.py:13
  109.1 8.3 %copy-start.5 = (bf16[2,512,1024]{2,1,0:T(8,128)(2,1)}, bf16[2,512,1024]{2,1,0:T(8,128)(2,1)S(1)}, u32[]{:S(2)}) copy-start(bf16[2,512,1024]{2,1,0:T(8,128)(2,1)S(1)} %collective-permute-done) | copy-start | bytes 6291460
  109.1 115.2 %collective-permute-start.1 = (bf16[2,512,1024]{2,1,0:T(8,128)(2,1)S(1)}, bf16[2,512,1024]{2,1,0:T(8,128)(2,1)S(1)}, u32[]{:S(2)}, u32[]{:S(2)}) collective-permute-start(bf16[2,512,1024]{2,1,0:T(8,128)(2,1)S(1)} %collective-permute-done), channel_id=1, source_target_pairs={{127,0},{0,1},{1,2},{2,3},{3,4},{4,5},{5,6},{6,7},{7,8},{8,9},{9,1... | collective-permute-start | bytes 6291464 | tf_op jit(solution)/shard_map/ppermute | solution.py:13
  115.0 106.9 %collective-permute-start.2 = (bf16[512,1024]{1,0:T(8,128)(2,1)S(1)}, bf16[512,1024]{1,0:T(8,128)(2,1)S(1)}, u32[]{:S(2)}, u32[]{:S(2)}) collective-permute-start(bf16[512,1024]{1,0:T(8,128)(2,1)S(1)} %convolution_convert_fusion), channel_id=1, source_target_pairs={{127,0},{0,1},{1,2},{2,3},{3,4},{4,5},{5,6},{6,7},{7,8},{8,9},{9,1... | collective-permute-start | bytes 3145736 | tf_op jit(solution)/shard_map/ppermute | solution.py:13
  222.3 43.8 %collective-permute-start.3 = (bf16[512,1024]{1,0:T(8,128)(2,1)S(1)}, bf16[512,1024]{1,0:T(8,128)(2,1)S(1)}, u32[]{:S(2)}, u32[]{:S(2)}) collective-permute-start(bf16[512,1024]{1,0:T(8,128)(2,1)S(1)} %add_convert_fusion.1), channel_id=1, source_target_pairs={{127,0},{0,1},{1,2},{2,3},{3,4},{4,5},{5,6},{6,7},{7,8},{8,9},{9,1... | collective-permute-start | bytes 3145736 | tf_op jit(solution)/shard_map/ppermute | solution.py:13
  224.3 1.5 copy-start.3
  266.5 28.8 %collective-permute-start.4 = (bf16[512,1024]{1,0:T(8,128)(2,1)S(1)}, bf16[512,1024]{1,0:T(8,128)(2,1)S(1)}, u32[]{:S(2)}, u32[]{:S(2)}) collective-permute-start(bf16[512,1024]{1,0:T(8,128)(2,1)S(1)} %add_convert_fusion), channel_id=1, source_target_pairs={{2,0},{3,1},{4,2},{5,3},{6,4},{7,5},{8,6},{9,7},{10,8},{11,9},{12,... | collective-permute-start | bytes 3145736 | tf_op jit(solution)/shard_map/ppermute | solution.py:13
  295.3 1.0 copy-start.2
  296.3 128.3 %copy-start.4 = (bf16[2,512,1024]{2,1,0:T(8,128)(2,1)S(1)}, bf16[2,512,1024]{2,1,0:T(8,128)(2,1)}, u32[]{:S(2)}) copy-start(bf16[2,512,1024]{2,1,0:T(8,128)(2,1)} %copy-done.3) | copy-start | bytes 6291460
Sparse Core Ops, SparseCore 0:
  11.0 40.3 all-gather.1
  296.4 128.1 reduce-scatter.1
where the time goes:
time: 434 us
  waiting for transfers between devices  391 us (90%)
  between operations  13.6 us (3%)
  matrix products  11.5 us (3%)
  starting transfers between devices  11 us (3%)
  other arithmetic  5.57 us (1%)
    ppermute x5, waiting for transfers between devices, from_behind(): return lax.ppermute(block, axis, route)  225 us
    reduce_scatter x1, waiting for transfers between devices, on_device(): lax.psum_scatter(returned.astype(jnp.bfloat16), 'section', scatter_dimens...  125 us
    all_gather x1, waiting for transfers between devices, on_device(): moving = lax.all_gather(stacked, 'section', axis=1, tiled=True)  40.5 us
    ppermute x5, starting transfers between devices, from_behind(): return lax.ppermute(block, axis, route)  10.9 us
  transfers between devices with their start and end apart: 7, of which 6 were waited for; matrix products, arithmetic and copies ran while one was open for 2% of the time, Pallas kernels for 0%

commit v1 on v0

v1 whole, which is shorter than its diff:
```python
import jax
import jax.numpy as jnp
from jax import lax
from jax.experimental import pallas as pl
from jax.experimental.pallas import tpu as pltpu
from jax.sharding import PartitionSpec as P

D = 1024
ROWS = 128
N_SECTION = 4
N_DP = 128
RUN = 32
F32 = jnp.float32
BF16 = jnp.bfloat16
VMEM = pl.BlockSpec(memory_space=pltpu.VMEM)
ROW_BY_ROW = (((1,), (1,)), ((), ()))


def route(block, target):
    pairs = []
    for q in range(N_SECTION):
        for d in range(N_DP):
            goal = target(q, d)
            if goal is not None:
                pairs.append((q * N_DP + d, goal[0] * N_DP + goal[1] % N_DP))
    return lax.ppermute(block, ("section", "dp"), pairs)


def to_core(q, d):
    return q ^ 1, d


def to_y(q, d):
    return q ^ 2, d


def along(q, d):
    return q, d + 1 - 2 * (q % 2)


def along_inside(q, d):
    last = RUN - 1 if q % 2 == 0 else 0
    return None if d % RUN == last else along(q, d)


def across(q, d):
    if q % 2 == 0:
        return (q, d + 2) if d % RUN == RUN - 2 else None
    return (q, d - 2) if d % RUN == 1 else None


def call(kernel, out_shape, flops, *operands):
    size = sum(x.size * x.dtype.itemsize for x in operands)
    return pl.pallas_call(
        kernel,
        out_shape=out_shape,
        in_specs=[VMEM] * len(operands),
        out_specs=jax.tree.map(lambda _: VMEM, out_shape),
        cost_estimate=pl.CostEstimate(flops=flops, bytes_accessed=size, transcendentals=0),
        compiler_params=pltpu.CompilerParams(vmem_limit_bytes=40 * 2**20),
    )(*operands)


def unit_kernel(s_ref, t_ref, unit_ref, inv_ref):
    for i, ref in enumerate((s_ref, t_ref)):
        values = ref[...].astype(F32)
        inverse = lax.rsqrt(jnp.sum(values * values, axis=1, keepdims=True) + 1e-06)
        unit_ref[i * ROWS : (i + 1) * ROWS, :] = (values * inverse).astype(BF16)
        if i == 0:
            inv_ref[...] = inverse


def add_terms(group, rows, factor):
    s_rows, t_rows = rows[:ROWS], rows[ROWS:]
    terms = []
    for part in group:
        diff = lax.dot_general(part[:ROWS], s_rows, ROW_BY_ROW, preferred_element_type=F32)
        diff = diff - lax.dot_general(part[ROWS:], t_rows, ROW_BY_ROW, preferred_element_type=F32)
        weights = (factor * diff).astype(BF16)
        terms.append(jnp.dot(weights, s_rows, preferred_element_type=F32))
    return terms


def first_kernel(own, sib, far, cross, one_a, one_b, sum_ref):
    group = [own[...], sib[...], far[...], cross[...]]
    total = add_terms(group, own[...], 2.0)
    for rows in (one_a, one_b):
        total = [x + y for x, y in zip(total, add_terms(group, rows[...], 1.0))]
    for i, x in enumerate(total):
        sum_ref[i * ROWS : (i + 1) * ROWS, :] = x


def second_kernel(own, sib, far, cross, two_a, two_b, sum_ref, keep_ref, send_ref):
    group = [own[...], sib[...], far[...], cross[...]]
    total = [sum_ref[i * ROWS : (i + 1) * ROWS, :] for i in range(4)]
    for rows in (two_a, two_b):
        total = [x + y for x, y in zip(total, add_terms(group, rows[...], 1.0))]
    keep_ref[:ROWS, :] = total[0]
    keep_ref[ROWS:, :] = total[2]
    send_ref[:ROWS, :] = total[1].astype(BF16)
    send_ref[ROWS:, :] = total[3].astype(BF16)


def far_kernel(keep, got, send_ref):
    send_ref[...] = (keep[ROWS:, :] + got[ROWS:, :].astype(F32)).astype(BF16)


def last_kernel(unit, inv, keep, got, got_far, out_ref):
    total = keep[:ROWS, :] + got[:ROWS, :].astype(F32) + got_far[...].astype(F32)
    unit_f = unit[:ROWS, :].astype(F32)
    along_unit = jnp.sum(unit_f * total, axis=1, keepdims=True)
    out_ref[...] = (D / 2.0 * inv[...] * (total - unit_f * along_unit)).astype(BF16)


def on_device(student, teacher):
    shape = jax.ShapeDtypeStruct
    own, inv = call(
        unit_kernel, (shape((2 * ROWS, D), BF16), shape((ROWS, 1), F32)), 10 * ROWS * D, student, teacher
    )
    one_a = route(own, along)
    sib = route(own, to_core)
    direct_a = route(own, across)
    far = route(own, to_y)
    one_b = route(sib, along)
    direct_b = route(sib, across)
    two_a = route(one_a, along_inside)
    two_b = route(one_b, along_inside)
    cross = route(far, to_core)
    core = lax.axis_index("section") % 2
    place = lax.axis_index("dp") % RUN
    at_start = place == jnp.where(core == 0, 0, RUN - 1)
    two_a = jnp.where(at_start, direct_a, two_a)
    two_b = jnp.where(at_start, direct_b, two_b)
    gram = 2 * 3 * 4 * ROWS * ROWS * D
    partial = call(first_kernel, shape((4 * ROWS, D), F32), 3 * gram, own, sib, far, cross, one_a, one_b)
    keep, send = call(
        second_kernel,
        (shape((2 * ROWS, D), F32), shape((2 * ROWS, D), BF16)),
        2 * gram,
        own, sib, far, cross, two_a, two_b, partial,
    )
    got = route(send, to_core)
    send_far = call(far_kernel, shape((ROWS, D), BF16), ROWS * D, keep, got)
    got_far = route(send_far, to_y)
    return call(last_kernel, shape((ROWS, D), BF16), 8 * ROWS * D, own, inv, keep, got, got_far)


def solution(mesh):
    placed = (P(("section", "dp"), None), P(("section", "dp"), None))
    return jax.shard_map(
        on_device, mesh=mesh, in_specs=placed, out_specs=P(("section", "dp"), None), check_vma=False
    )
```

time: 434 us -> 95.3 us (0.22)
  waiting for transfers between devices: 391 us -> 43.8 us
  starting transfers between devices: 11 us -> 39.6 us
  between operations: 13.6 us -> 0.17 us
  matrix products: 11.5 us -> 0 us
  Pallas kernels: 0 us -> 7.19 us
    ppermute x5 -> x11, waiting for transfers between devices: 225 us -> 43.8 us  [route(): return lax.ppermute(block, ('section', 'dp'), pairs)]
    reduce_scatter x1 -> x0, waiting for transfers between devices: 125 us -> none  [on_device(): lax.psum_scatter(returned.astype(jnp.bfloat16), 'section', scatter_dimens...]
    all_gather x1 -> x0, waiting for transfers between devices: 40.5 us -> none  [on_device(): moving = lax.all_gather(stacked, 'section', axis=1, tiled=True)]
    ppermute x5 -> x11, starting transfers between devices: 10.9 us -> 39.6 us  [route(): return lax.ppermute(block, ('section', 'dp'), pairs)]
    dot_general x12 -> x0, matrix products: 11.5 us -> none  [the longest x3 4.56 us: on_device(): forward = jnp.dot(weights, whole[0], preferred_element_type=jnp.float32)]
    pallas_call x0 -> x5, Pallas kernels: none -> 7.19 us  [call(): pl.pallas_call(kernel, out_shape=out_shape, in_specs=[VMEM] * len(operand...]
  transfers between devices with their start and end apart: 7 -> 11, of which waited for: 6 -> 6; matrix products, arithmetic and copies ran while one was open for 2% -> 1% of each run, Pallas kernels for 0% -> 4%
where the time goes in v1:
time: 95.3 us; the launch traced here: 94.8 us
  waiting for transfers between devices  43.8 us (46%)
  starting transfers between devices  39.6 us (42%)
  Pallas kernels  7.19 us (8%)
  other arithmetic  2.2 us (2%)
  local copies, waits for them, and re-layouts  1.9 us (2%)
    ppermute x11, waiting for transfers between devices, route(): return lax.ppermute(block, ('section', 'dp'), pairs)  43.8 us
    ppermute x11, starting transfers between devices, route(): return lax.ppermute(block, ('section', 'dp'), pairs)  39.6 us
    pallas_call x5, Pallas kernels, call(): pl.pallas_call(kernel, out_shape=out_shape, in_specs=[VMEM] * len(operand...  7.19 us
  transfers between devices with their start and end apart: 11, of which 6 were waited for; matrix products, arithmetic and copies ran while one was open for 1% of the time, Pallas kernels for 4%

profile of v1, /device:TPU:1, one launch (start us, length us, event | category | flops | bytes accessed | tf_op | source)
XLA Modules:
  0.0 94.8 jit_solution(17252969872226383967)
XLA Ops:
  0.0 0.0 copy-start
  0.0 0.9 copy-done
  1.0 0.0 copy-start.1
  1.0 0.9 copy-done.1
  1.9 0.2 shard_map.28
  2.1 8.8 %collective-permute-start = (bf16[256,1024]{1,0:T(8,128)(2,1)S(1)}, bf16[256,1024]{1,0:T(8,128)(2,1)S(1)}, u32[]{:S(2)}, u32[]{:S(2)}) collective-permute-start(bf16[256,1024]{1,0:T(8,128)(2,1)S(1)} %get-tuple-element.9.own.unit), channel_id=1, source_target_pairs={{0,128},{1,129},{2,130},{3,131},{4,132},{5,133},{6,134},{7,135},{8... | collective-permute-start | bytes 1572872 | tf_op jit(solution)/shard_map/ppermute | solution.py:26
  10.9 1.9 %collective-permute-start.1 = (bf16[256,1024]{1,0:T(8,128)(2,1)S(1)}, bf16[256,1024]{1,0:T(8,128)(2,1)S(1)}, u32[]{:S(2)}, u32[]{:S(2)}) collective-permute-start(bf16[256,1024]{1,0:T(8,128)(2,1)S(1)} %get-tuple-element.9.own.unit), channel_id=1, source_target_pairs={{0,256},{1,257},{2,258},{3,259},{4,260},{5,261},{6,262},{7,263},{8... | collective-permute-start | bytes 1572872 | tf_op jit(solution)/shard_map/ppermute | solution.py:26
  12.8 11.6 %collective-permute-start.4 = (bf16[256,1024]{1,0:T(8,128)(2,1)S(1)}, bf16[256,1024]{1,0:T(8,128)(2,1)S(1)}, u32[]{:S(2)}, u32[]{:S(2)}) collective-permute-start(bf16[256,1024]{1,0:T(8,128)(2,1)S(1)} %get-tuple-element.9.own.unit), channel_id=1, source_target_pairs={{0,1},{1,2},{2,3},{3,4},{4,5},{5,6},{6,7},{7,8},{8,9},{9,10},{10,1... | collective-permute-start | bytes 1572872 | tf_op jit(solution)/shard_map/ppermute | solution.py:26
  24.4 0.0 collective-permute-done.sib
  24.4 2.2 %collective-permute-start.7 = (bf16[256,1024]{1,0:T(8,128)(2,1)S(1)}, bf16[256,1024]{1,0:T(8,128)(2,1)S(1)}, u32[]{:S(2)}, u32[]{:S(2)}) collective-permute-start(bf16[256,1024]{1,0:T(8,128)(2,1)S(1)} %collective-permute-done.sib), channel_id=1, source_target_pairs={{0,1},{1,2},{2,3},{3,4},{4,5},{5,6},{6,7},{7,8},{8,9},{9,10},{10,1... | collective-permute-start | bytes 1572872 | tf_op jit(solution)/shard_map/ppermute | solution.py:26
  26.6 0.0 collective-permute-done.1.far
  26.6 2.6 %collective-permute-start.2 = (bf16[256,1024]{1,0:T(8,128)(2,1)S(1)}, bf16[256,1024]{1,0:T(8,128)(2,1)S(1)}, u32[]{:S(2)}, u32[]{:S(2)}) collective-permute-start(bf16[256,1024]{1,0:T(8,128)(2,1)S(1)} %collective-permute-done.1.far), channel_id=1, source_target_pairs={{0,128},{1,129},{2,130},{3,131},{4,132},{5,133},{6,134},{7,135},{8... | collective-permute-start | bytes 1572872 | tf_op jit(solution)/shard_map/ppermute | solution.py:26
  29.2 1.5 %collective-permute-start.3 = (bf16[256,1024]{1,0:T(8,128)(2,1)S(1)}, bf16[256,1024]{1,0:T(8,128)(2,1)}, u32[]{:S(2)}, u32[]{:S(2)}) collective-permute-start(bf16[256,1024]{1,0:T(8,128)(2,1)S(1)} %get-tuple-element.9.own.unit), channel_id=1, source_target_pairs={{30,32},{62,64},{94,96},{126,0},{129,255},{161,159},{193,191},{225... | collective-permute-start | bytes 1572872 | tf_op jit(solution)/shard_map/ppermute | solution.py:26
  30.7 8.9 %collective-permute-done.4.one_a = bf16[256,1024]{1,0:T(8,128)(2,1)S(1)} collective-permute-done((bf16[256,1024]{1,0:T(8,128)(2,1)S(1)}, bf16[256,1024]{1,0:T(8,128)(2,1)S(1)}, u32[]{:S(2)}, u32[]{:S(2)}) %collective-permute-start.4) | collective-permute-done | bytes 524320 | tf_op jit(solution)/shard_map/ppermute | solution.py:26
  39.6 1.3 %collective-permute-start.5 = (bf16[256,1024]{1,0:T(8,128)(2,1)S(1)}, bf16[256,1024]{1,0:T(8,128)(2,1)}, u32[]{:S(2)}, u32[]{:S(2)}) collective-permute-start(bf16[256,1024]{1,0:T(8,128)(2,1)S(1)} %collective-permute-done.4.one_a), channel_id=1, source_target_pairs={{0,1},{1,2},{2,3},{3,4},{4,5},{5,6},{6,7},{7,8},{8,9},{9,10},{10,1... | collective-permute-start | bytes 1572872 | tf_op jit(solution)/shard_map/ppermute | solution.py:26
  40.9 1.5 %collective-permute-start.6 = (bf16[256,1024]{1,0:T(8,128)(2,1)S(1)}, bf16[256,1024]{1,0:T(8,128)(2,1)}, u32[]{:S(2)}, u32[]{:S(2)}) collective-permute-start(bf16[256,1024]{1,0:T(8,128)(2,1)S(1)} %collective-permute-done.sib), channel_id=1, source_target_pairs={{30,32},{62,64},{94,96},{126,0},{129,255},{161,159},{193,191},{225... | collective-permute-start | bytes 1572872 | tf_op jit(solution)/shard_map/ppermute | solution.py:26
  42.4 3.0 %collective-permute-done.7.one_b = bf16[256,1024]{1,0:T(8,128)(2,1)S(1)} collective-permute-done((bf16[256,1024]{1,0:T(8,128)(2,1)S(1)}, bf16[256,1024]{1,0:T(8,128)(2,1)S(1)}, u32[]{:S(2)}, u32[]{:S(2)}) %collective-permute-start.7) | collective-permute-done | bytes 524320 | tf_op jit(solution)/shard_map/ppermute | solution.py:26
  45.4 1.3 %collective-permute-start.8 = (bf16[256,1024]{1,0:T(8,128)(2,1)S(1)}, bf16[256,1024]{1,0:T(8,128)(2,1)}, u32[]{:S(2)}, u32[]{:S(2)}) collective-permute-start(bf16[256,1024]{1,0:T(8,128)(2,1)S(1)} %collective-permute-done.7.one_b), channel_id=1, source_target_pairs={{0,1},{1,2},{2,3},{3,4},{4,5},{5,6},{6,7},{7,8},{8,9},{9,10},{10,1... | collective-permute-start | bytes 1572872 | tf_op jit(solution)/shard_map/ppermute | solution.py:26
  46.7 0.0 collective-permute-done.2.cross
  46.7 3.4 %shard_map.29.sum_ref = f32[512,1024]{1,0:T(8,128)S(1)} custom-call(bf16[256,1024]{1,0:T(8,128)(2,1)S(1)} %get-tuple-element.9.own.unit, bf16[256,1024]{1,0:T(8,128)(2,1)S(1)} %collective-permute-done.sib, bf16[256,1024]{1,0:T(8,128)(2,1)S(1)} %collective-permute-done.1.far, bf16[256,1024]{1,0:T(8,128)(2,1)S(1)} %collective-permute-done.2.cross, ...), custom_call_target="tpu_custom_call" | custom-call | flops 1207959552 | bytes 3145728 | tf_op jit(solution)/shard_map/pallas_call | solution.py:54
  50.1 0.0 collective-permute-done.3
  50.1 19.4 %collective-permute-done.5 = bf16[256,1024]{1,0:T(8,128)(2,1)} collective-permute-done((bf16[256,1024]{1,0:T(8,128)(2,1)S(1)}, bf16[256,1024]{1,0:T(8,128)(2,1)}, u32[]{:S(2)}, u32[]{:S(2)}) %collective-permute-start.5) | collective-permute-done | bytes 524320 | tf_op jit(solution)/shard_map/ppermute | solution.py:26
  69.5 1.1 %broadcast_select_fusion.1.two_a = bf16[256,1024]{1,0:T(8,128)(2,1)S(1)} fusion(bf16[256,1024]{1,0:T(8,128)(2,1)} %collective-permute-done.3, bf16[256,1024]{1,0:T(8,128)(2,1)} %collective-permute-done.5, pred[]{:T(512)S(6)} %eq.10), kind=kLoop, calls=%fused_computation.1 | loop fusion | flops 262144 | bytes 1572865 | tf_op jit(solution)/shard_map/jit(_where)/select_n | solution.py:132
  70.6 0.0 collective-permute-done.6
  70.6 4.4 %collective-permute-done.8 = bf16[256,1024]{1,0:T(8,128)(2,1)} collective-permute-done((bf16[256,1024]{1,0:T(8,128)(2,1)S(1)}, bf16[256,1024]{1,0:T(8,128)(2,1)}, u32[]{:S(2)}, u32[]{:S(2)}) %collective-permute-start.8) | collective-permute-done | bytes 524320 | tf_op jit(solution)/shard_map/ppermute | solution.py:26
  75.0 1.1 %broadcast_select_fusion.two_b = bf16[256,1024]{1,0:T(8,128)(2,1)S(1)} fusion(bf16[256,1024]{1,0:T(8,128)(2,1)} %collective-permute-done.6, bf16[256,1024]{1,0:T(8,128)(2,1)} %collective-permute-done.8, pred[]{:T(512)S(6)} %eq.10), kind=kLoop, calls=%fused_computation | loop fusion | flops 262144 | bytes 1572865 | tf_op jit(solution)/shard_map/jit(_where)/select_n | solution.py:133
  76.1 2.6 %shard_map.30 = (f32[256,1024]{1,0:T(8,128)S(1)}, bf16[256,1024]{1,0:T(8,128)(2,1)S(1)}) custom-call(bf16[256,1024]{1,0:T(8,128)(2,1)S(1)} %get-tuple-element.9.own.unit, bf16[256,1024]{1,0:T(8,128)(2,1)S(1)} %collective-permute-done.sib, bf16[256,1024]{1,0:T(8,128)(2,1)S(1)} %collective-permute-done.1.far, ...), custom_call_target="tpu_custom_call" | custom-call | flops 805306368 | bytes 5242880 | tf_op jit(solution)/shard_map/pallas_call | solution.py:54
  78.7 2.4 %collective-permute-start.9 = (bf16[256,1024]{1,0:T(8,128)(2,1)S(1)}, bf16[256,1024]{1,0:T(8,128)(2,1)S(1)}, u32[]{:S(2)}, u32[]{:S(2)}) collective-permute-start(bf16[256,1024]{1,0:T(8,128)(2,1)S(1)} %get-tuple-element.12), channel_id=1, source_target_pairs={{0,128},{1,129},{2,130},{3,131},{4,132},{5,133},{6,134},{7,135},{8... | collective-permute-start | bytes 1572872 | tf_op jit(solution)/shard_map/ppermute | solution.py:26
  81.2 1.5 %collective-permute-done.9.got = bf16[256,1024]{1,0:T(8,128)(2,1)S(1)} collective-permute-done((bf16[256,1024]{1,0:T(8,128)(2,1)S(1)}, bf16[256,1024]{1,0:T(8,128)(2,1)S(1)}, u32[]{:S(2)}, u32[]{:S(2)}) %collective-permute-start.9) | collective-permute-done | bytes 524320 | tf_op jit(solution)/shard_map/ppermute | solution.py:26
  82.7 4.6 %collective-permute-start.10 = (bf16[128,1024]{1,0:T(8,128)(2,1)S(1)}, bf16[128,1024]{1,0:T(8,128)(2,1)S(1)}, u32[]{:S(2)}, u32[]{:S(2)}) collective-permute-start(bf16[128,1024]{1,0:T(8,128)(2,1)S(1)} %shard_map.31), channel_id=1, source_target_pairs={{0,256},{1,257},{2,258},{3,259},{4,260},{5,261},{6,262},{7,263},{8... | collective-permute-start | bytes 786440 | tf_op jit(solution)/shard_map/ppermute | solution.py:26
  87.3 6.5 %collective-permute-done.10.got_far = bf16[128,1024]{1,0:T(8,128)(2,1)S(1)} collective-permute-done((bf16[128,1024]{1,0:T(8,128)(2,1)S(1)}, bf16[128,1024]{1,0:T(8,128)(2,1)S(1)}, u32[]{:S(2)}, u32[]{:S(2)}) %collective-permute-start.10) | collective-permute-done | bytes 262176 | tf_op jit(solution)/shard_map/ppermute | solution.py:26
  93.9 1.0 %shard_map.32 = bf16[128,1024]{1,0:T(8,128)(2,1)} custom-call(bf16[256,1024]{1,0:T(8,128)(2,1)S(1)} %get-tuple-element.9.own.unit, f32[128,1]{1,0:T(8,128)S(1)} %get-tuple-element.10.inv, f32[256,1024]{1,0:T(8,128)S(1)} %get-tuple-element.11.keep, bf16[256,1024]{1,0:T(8,128)(2,1)S(1)} %collective-permute-done.9.got, ...), custom_call_target="tpu_custom_call" | custom-call | flops 1048576 | bytes 2359808 | tf_op jit(solution)/shard_map/pallas_call | solution.py:54
  (1 shorter events, 0.0 us)
Async XLA Ops:
  0.0 0.9 %copy-start = (bf16[128,1024]{1,0:T(8,128)(2,1)S(1)}, bf16[128,1024]{1,0:T(8,128)(2,1)}, u32[]{:S(2)}) copy-start(bf16[128,1024]{1,0:T(8,128)(2,1)} %s_ref.1) | copy-start | bytes 786436
  1.0 0.9 %copy-start.1 = (bf16[128,1024]{1,0:T(8,128)(2,1)S(1)}, bf16[128,1024]{1,0:T(8,128)(2,1)}, u32[]{:S(2)}) copy-start(bf16[128,1024]{1,0:T(8,128)(2,1)} %t_ref.1) | copy-start | bytes 786436
  2.1 22.3 %collective-permute-start = (bf16[256,1024]{1,0:T(8,128)(2,1)S(1)}, bf16[256,1024]{1,0:T(8,128)(2,1)S(1)}, u32[]{:S(2)}, u32[]{:S(2)}) collective-permute-start(bf16[256,1024]{1,0:T(8,128)(2,1)S(1)} %get-tuple-element.9.own.unit), channel_id=1, source_target_pairs={{0,128},{1,129},{2,130},{3,131},{4,132},{5,133},{6,134},{7,135},{8... | collective-permute-start | bytes 1572872 | tf_op jit(solution)/shard_map/ppermute | solution.py:26
  10.9 15.7 %collective-permute-start.1 = (bf16[256,1024]{1,0:T(8,128)(2,1)S(1)}, bf16[256,1024]{1,0:T(8,128)(2,1)S(1)}, u32[]{:S(2)}, u32[]{:S(2)}) collective-permute-start(bf16[256,1024]{1,0:T(8,128)(2,1)S(1)} %get-tuple-element.9.own.unit), channel_id=1, source_target_pairs={{0,256},{1,257},{2,258},{3,259},{4,260},{5,261},{6,262},{7,263},{8... | collective-permute-start | bytes 1572872 | tf_op jit(solution)/shard_map/ppermute | solution.py:26
  12.8 26.8 %collective-permute-start.4 = (bf16[256,1024]{1,0:T(8,128)(2,1)S(1)}, bf16[256,1024]{1,0:T(8,128)(2,1)S(1)}, u32[]{:S(2)}, u32[]{:S(2)}) collective-permute-start(bf16[256,1024]{1,0:T(8,128)(2,1)S(1)} %get-tuple-element.9.own.unit), channel_id=1, source_target_pairs={{0,1},{1,2},{2,3},{3,4},{4,5},{5,6},{6,7},{7,8},{8,9},{9,10},{10,1... | collective-permute-start | bytes 1572872 | tf_op jit(solution)/shard_map/ppermute | solution.py:26
  24.4 21.0 %collective-permute-start.7 = (bf16[256,1024]{1,0:T(8,128)(2,1)S(1)}, bf16[256,1024]{1,0:T(8,128)(2,1)S(1)}, u32[]{:S(2)}, u32[]{:S(2)}) collective-permute-start(bf16[256,1024]{1,0:T(8,128)(2,1)S(1)} %collective-permute-done.sib), channel_id=1, source_target_pairs={{0,1},{1,2},{2,3},{3,4},{4,5},{5,6},{6,7},{7,8},{8,9},{9,10},{10,1... | collective-permute-start | bytes 1572872 | tf_op jit(solution)/shard_map/ppermute | solution.py:26
  26.6 20.1 %collective-permute-start.2 = (bf16[256,1024]{1,0:T(8,128)(2,1)S(1)}, bf16[256,1024]{1,0:T(8,128)(2,1)S(1)}, u32[]{:S(2)}, u32[]{:S(2)}) collective-permute-start(bf16[256,1024]{1,0:T(8,128)(2,1)S(1)} %collective-permute-done.1.far), channel_id=1, source_target_pairs={{0,128},{1,129},{2,130},{3,131},{4,132},{5,133},{6,134},{7,135},{8... | collective-permute-start | bytes 1572872 | tf_op jit(solution)/shard_map/ppermute | solution.py:26
  29.2 20.9 %collective-permute-start.3 = (bf16[256,1024]{1,0:T(8,128)(2,1)S(1)}, bf16[256,1024]{1,0:T(8,128)(2,1)}, u32[]{:S(2)}, u32[]{:S(2)}) collective-permute-start(bf16[256,1024]{1,0:T(8,128)(2,1)S(1)} %get-tuple-element.9.own.unit), channel_id=1, source_target_pairs={{30,32},{62,64},{94,96},{126,0},{129,255},{161,159},{193,191},{225... | collective-permute-start | bytes 1572872 | tf_op jit(solution)/shard_map/ppermute | solution.py:26
  39.6 29.9 %collective-permute-start.5 = (bf16[256,1024]{1,0:T(8,128)(2,1)S(1)}, bf16[256,1024]{1,0:T(8,128)(2,1)}, u32[]{:S(2)}, u32[]{:S(2)}) collective-permute-start(bf16[256,1024]{1,0:T(8,128)(2,1)S(1)} %collective-permute-done.4.one_a), channel_id=1, source_target_pairs={{0,1},{1,2},{2,3},{3,4},{4,5},{5,6},{6,7},{7,8},{8,9},{9,10},{10,1... | collective-permute-start | bytes 1572872 | tf_op jit(solution)/shard_map/ppermute | solution.py:26
  40.9 29.7 %collective-permute-start.6 = (bf16[256,1024]{1,0:T(8,128)(2,1)S(1)}, bf16[256,1024]{1,0:T(8,128)(2,1)}, u32[]{:S(2)}, u32[]{:S(2)}) collective-permute-start(bf16[256,1024]{1,0:T(8,128)(2,1)S(1)} %collective-permute-done.sib), channel_id=1, source_target_pairs={{30,32},{62,64},{94,96},{126,0},{129,255},{161,159},{193,191},{225... | collective-permute-start | bytes 1572872 | tf_op jit(solution)/shard_map/ppermute | solution.py:26
  45.4 29.7 %collective-permute-start.8 = (bf16[256,1024]{1,0:T(8,128)(2,1)S(1)}, bf16[256,1024]{1,0:T(8,128)(2,1)}, u32[]{:S(2)}, u32[]{:S(2)}) collective-permute-start(bf16[256,1024]{1,0:T(8,128)(2,1)S(1)} %collective-permute-done.7.one_b), channel_id=1, source_target_pairs={{0,1},{1,2},{2,3},{3,4},{4,5},{5,6},{6,7},{7,8},{8,9},{9,10},{10,1... | collective-permute-start | bytes 1572872 | tf_op jit(solution)/shard_map/ppermute | solution.py:26
  78.7 3.9 %collective-permute-start.9 = (bf16[256,1024]{1,0:T(8,128)(2,1)S(1)}, bf16[256,1024]{1,0:T(8,128)(2,1)S(1)}, u32[]{:S(2)}, u32[]{:S(2)}) collective-permute-start(bf16[256,1024]{1,0:T(8,128)(2,1)S(1)} %get-tuple-element.12), channel_id=1, source_target_pairs={{0,128},{1,129},{2,130},{3,131},{4,132},{5,133},{6,134},{7,135},{8... | collective-permute-start | bytes 1572872 | tf_op jit(solution)/shard_map/ppermute | solution.py:26
  82.7 11.2 %collective-permute-start.10 = (bf16[128,1024]{1,0:T(8,128)(2,1)S(1)}, bf16[128,1024]{1,0:T(8,128)(2,1)S(1)}, u32[]{:S(2)}, u32[]{:S(2)}) collective-permute-start(bf16[128,1024]{1,0:T(8,128)(2,1)S(1)} %shard_map.31), channel_id=1, source_target_pairs={{0,256},{1,257},{2,258},{3,259},{4,260},{5,261},{6,262},{7,263},{8... | collective-permute-start | bytes 786440 | tf_op jit(solution)/shard_map/ppermute | solution.py:26

commit v2 on v1

v2 whole, which is shorter than its diff:
```python
import jax
import jax.numpy as jnp
from jax import lax
from jax.experimental import pallas as pl
from jax.experimental.pallas import tpu as pltpu
from jax.sharding import PartitionSpec as P

D = 1024
ROWS = 128
N_SECTION = 4
N_DP = 128
RUN = 32
F32 = jnp.float32
BF16 = jnp.bfloat16
C1 = 400000000
C2 = 800000000
C3 = 1
C4 = 400000000
C5 = 400000000
C6 = 800000000
C7 = 400000000
C9 = 100000000
C10 = 100000000
C12 = 400000000
C11 = 800000000
C8 = 800000000
VMEM = pl.BlockSpec(memory_space=pltpu.VMEM)
ROW_BY_ROW = (((1,), (1,)), ((), ()))


def route(block, target):
    pairs = []
    for q in range(N_SECTION):
        for d in range(N_DP):
            goal = target(q, d)
            if goal is not None:
                pairs.append((q * N_DP + d, goal[0] * N_DP + goal[1] % N_DP))
    return lax.ppermute(block, ("section", "dp"), pairs)


def to_core(q, d):
    return q ^ 1, d


def to_y(q, d):
    return q ^ 2, d


def along(q, d):
    return q, d + 1 - 2 * (q % 2)


def along_inside(q, d):
    last = RUN - 1 if q % 2 == 0 else 0
    return None if d % RUN == last else along(q, d)


def across(q, d):
    if q % 2 == 0:
        return (q, d + 2) if d % RUN == RUN - 2 else None
    return (q, d - 2) if d % RUN == 1 else None


def aside(q, d):
    if q % 2 == 1:
        return (q ^ 1, d - 24) if d % RUN in (RUN - 2, RUN - 1) else None
    return (q ^ 1, d + 24) if d % RUN in (0, 1) else None


def from_aside(q, d):
    if q % 2 == 0:
        return {7: (q, d + 25), 6: (q ^ 1, d + 26)}.get(d % RUN)
    return {RUN - 8: (q, d - 25), RUN - 7: (q ^ 1, d - 26)}.get(d % RUN)


def call(kernel, out_shape, flops, *operands):
    size = sum(x.size * x.dtype.itemsize for x in operands)
    return pl.pallas_call(
        kernel,
        out_shape=out_shape,
        in_specs=[pl.BlockSpec(memory_space=pltpu.SMEM) if x.ndim == 1 else VMEM for x in operands],
        out_specs=jax.tree.map(lambda _: VMEM, out_shape),
        cost_estimate=pl.CostEstimate(flops=flops, bytes_accessed=size, transcendentals=0),
        compiler_params=pltpu.CompilerParams(vmem_limit_bytes=40 * 2**20),
    )(*operands)


def unit_kernel(s_hbm, t_hbm, unit_ref, inv_ref, s_ref, t_ref, sems):
    copies = [
        pltpu.make_async_copy(src, dst, sems.at[i])
        for i, (src, dst) in enumerate(((s_hbm, s_ref), (t_hbm, t_ref)))
    ]
    for copy in copies:
        copy.start()
    for i, ref in enumerate((s_ref, t_ref)):
        copies[i].wait()
        values = ref[...].astype(F32)
        inverse = lax.rsqrt(jnp.sum(values * values, axis=1, keepdims=True) + 1e-06)
        unit_ref[i * ROWS : (i + 1) * ROWS, :] = (values * inverse).astype(BF16)
        if i == 0:
            inv_ref[...] = inverse


def unit_rows(student, teacher):
    return pl.pallas_call(
        unit_kernel,
        out_shape=(jax.ShapeDtypeStruct((2 * ROWS, D), BF16), jax.ShapeDtypeStruct((ROWS, 1), F32)),
        in_specs=[pl.BlockSpec(memory_space=pl.ANY)] * 2,
        out_specs=(VMEM, VMEM),
        scratch_shapes=[pltpu.VMEM((ROWS, D), BF16)] * 2 + [pltpu.SemaphoreType.DMA((2,))],
        cost_estimate=pl.CostEstimate(flops=10 * ROWS * D, bytes_accessed=4 * ROWS * D, transcendentals=0),
        compiler_params=pltpu.CompilerParams(vmem_limit_bytes=40 * 2**20),
    )(student, teacher)


def stack(blocks, part):
    return jnp.concatenate([x[part * ROWS : (part + 1) * ROWS, :] for x in blocks], axis=0)


def terms(parts, rows, own_first):
    s_rows, t_rows = stack(rows, 0), stack(rows, 1)
    diff = lax.dot_general(stack(parts, 0), s_rows, ROW_BY_ROW, preferred_element_type=F32)
    diff = diff - lax.dot_general(stack(parts, 1), t_rows, ROW_BY_ROW, preferred_element_type=F32)
    if own_first:
        diff = jnp.concatenate([2.0 * diff[:, :ROWS], diff[:, ROWS:]], axis=1)
    return jnp.dot(diff.astype(BF16), s_rows, preferred_element_type=F32)


def hold_kernel(block, out_ref):
    out_ref[...] = block[...]


def mix_kernel(flag, one_b, near_b, direct, next_ref, extra_ref):
    at_end = flag[0] == 1
    none = jnp.zeros_like(near_b)
    next_ref[...] = one_b[...] + jnp.where(at_end, near_b[...], none)
    extra_ref[...] = direct[...] + jnp.where(at_end, none, near_b[...])


def first_kernel(one, other, own, one_a, one_b, two_a, sum_ref):
    sum_ref[...] = terms([one, other], [own, one_a, one_b, two_a], True)


def final_kernel(one, other, two, extra, old_ref, keep_ref, send_ref):
    total = old_ref[...] + terms([one, other], [two, extra], False)
    keep_ref[...] = total[:ROWS, :]
    send_ref[...] = total[ROWS:, :].astype(BF16)


def far_kernel(keep, got, send_ref):
    send_ref[...] = (keep[...] + got[...].astype(F32)).astype(BF16)


def last_kernel(unit, inv, keep, got, got_far, out_ref):
    total = keep[...] + got[...].astype(F32) + got_far[...].astype(F32)
    unit_f = unit[:ROWS, :].astype(F32)
    along_unit = jnp.sum(unit_f * total, axis=1, keepdims=True)
    out_ref[...] = (D / 2.0 * inv[...] * (total - unit_f * along_unit)).astype(BF16)


def after(block, *others):
    return lax.optimization_barrier((block, *others))[0]


def hold(block, cost):
    return call(hold_kernel, jax.ShapeDtypeStruct(block.shape, block.dtype), cost, block)


def on_device(student, teacher):
    shape = jax.ShapeDtypeStruct
    quarter_f, quarter_h = shape((ROWS, D), F32), shape((ROWS, D), BF16)
    half, both = shape((2 * ROWS, D), F32), shape((2 * ROWS, D), BF16)
    gram = 2 * 3 * 2 * ROWS * ROWS * D
    own, inv = unit_rows(student, teacher)
    one_a = hold(route(own, along), C9)
    spread = route(own, aside)
    direct = hold(route(own, across), C11)
    far = hold(route(own, to_y), C6)
    sib = route(own, to_core)
    one_b = route(sib, along_inside)
    near_b = hold(route(spread, from_aside), C12)
    core = lax.axis_index("section") % 2
    place = lax.axis_index("dp") % RUN
    flag = (place == core * (RUN - 1)).astype(jnp.int32).reshape(1)
    one_b, extra = call(mix_kernel, (both, both), C1, flag, after(one_b, far), near_b, direct)
    two_a = hold(route(one_a, along_inside), C5)
    two_b = hold(route(one_b, along_inside), C2)
    near_sum = call(first_kernel, half, C8, own, sib, own, one_a, after(one_b, far), two_a)
    cross = route(after(far, one_b), to_core)
    away_sum = call(first_kernel, half, 0, far, cross, own, one_a, one_b, two_a)
    keep_far, send_far = call(
        final_kernel, (quarter_f, quarter_h), C4, far, cross, two_b, extra, away_sum
    )
    got_far = route(send_far, to_core)
    send_far = call(far_kernel, quarter_h, ROWS * D, keep_far, got_far)
    got_far = hold(route(send_far, to_y), C10)
    keep, send = call(final_kernel, (quarter_f, quarter_h), gram, own, sib, two_b, extra, near_sum)
    got = route(after(send, send_far), to_core)
    return call(last_kernel, quarter_h, 8 * ROWS * D, own, inv, keep, got, got_far)


def solution(mesh):
    placed = (P(("section", "dp"), None), P(("section", "dp"), None))
    return jax.shard_map(
        on_device, mesh=mesh, in_specs=placed, out_specs=P(("section", "dp"), None), check_vma=False
    )
```

time: 95.3 us -> 79.6 us (0.84)
  waiting for transfers between devices: 43.8 us -> 31.5 us
  other arithmetic: 2.2 us -> 0 us
    ppermute x11 -> x13, waiting for transfers between devices: 43.8 us -> 31.5 us  [route(): return lax.ppermute(block, ('section', 'dp'), pairs)]
    select_n x2 -> x0, other arithmetic: 2.2 us -> none  [the longest x1 1.1 us: on_device(): two_a = jnp.where(at_start, direct_a, two_a)]
    pallas_call x5 -> x15, Pallas kernels: 7.19 us -> 6.32 us  [the longest x14 5.99 us: call(): pl.pallas_call(kernel, out_shape=out_shape, in_specs=[pl.BlockSpec(memory...]
    ppermute x11 -> x13, starting transfers between devices: 39.6 us -> 39.1 us  [route(): return lax.ppermute(block, ('section', 'dp'), pairs)]
  transfers between devices with their start and end apart: 11 -> 13, of which waited for: 6 -> 7; matrix products, arithmetic and copies ran while one was open for 1% -> 0% of each run, Pallas kernels for 4% -> 4%
where the time goes in v2:
time: 79.6 us; the launch traced here: 79.1 us
  starting transfers between devices  39.1 us (49%)
  waiting for transfers between devices  31.5 us (40%)
  Pallas kernels  6.32 us (8%)
  local copies, waits for them, and re-layouts  1.9 us (2%)
    ppermute x13, starting transfers between devices, route(): return lax.ppermute(block, ('section', 'dp'), pairs)  39.1 us
    ppermute x13, waiting for transfers between devices, route(): return lax.ppermute(block, ('section', 'dp'), pairs)  31.5 us
    pallas_call x14, Pallas kernels, call(): pl.pallas_call(kernel, out_shape=out_shape, in_specs=[pl.BlockSpec(memory...  5.99 us
    unnamed x4, local copies, waits for them, and re-layouts  1.9 us
  transfers between devices with their start and end apart: 13, of which 7 were waited for; matrix products, arithmetic and copies ran while one was open for 0% of the time, Pallas kernels for 4%

profile of v2, /device:TPU:1, one launch (start us, length us, event | category | flops | bytes accessed | tf_op | source)
XLA Modules:
  0.0 79.1 jit_solution(16238869108922029020)
XLA Ops:
  0.0 0.0 copy-start
  0.0 0.9 %copy-done = bf16[128,1024]{1,0:T(8,128)(2,1)S(1)} copy-done((bf16[128,1024]{1,0:T(8,128)(2,1)S(1)}, bf16[128,1024]{1,0:T(8,128)(2,1)}, u32[]{:S(2)}) %copy-start) | copy-done | bytes 262168
  1.0 0.0 copy-start.1
  1.0 0.9 %copy-done.1 = bf16[128,1024]{1,0:T(8,128)(2,1)S(1)} copy-done((bf16[128,1024]{1,0:T(8,128)(2,1)S(1)}, bf16[128,1024]{1,0:T(8,128)(2,1)}, u32[]{:S(2)}) %copy-start.1) | copy-done | bytes 262168
  1.9 0.3 shard_map.28
  2.2 8.8 %collective-permute-start = (bf16[256,1024]{1,0:T(8,128)(2,1)S(1)}, bf16[256,1024]{1,0:T(8,128)(2,1)S(1)}, u32[]{:S(2)}, u32[]{:S(2)}) collective-permute-start(bf16[256,1024]{1,0:T(8,128)(2,1)S(1)} %get-tuple-element.17.one.own.unit), channel_id=1, source_target_pairs={{0,128},{1,129},{2,130},{3,131},{4,132},{5,133},{6,134},{7,135},{8... | collective-permute-start | bytes 1572872 | tf_op jit(solution)/shard_map/ppermute | solution.py:38
  11.0 1.5 %collective-permute-start.3 = (bf16[256,1024]{1,0:T(8,128)(2,1)S(1)}, bf16[256,1024]{1,0:T(8,128)(2,1)}, u32[]{:S(2)}, u32[]{:S(2)}) collective-permute-start(bf16[256,1024]{1,0:T(8,128)(2,1)S(1)} %get-tuple-element.17.one.own.unit), channel_id=1, source_target_pairs={{0,152},{1,153},{32,184},{33,185},{64,216},{65,217},{96,248},{97,2... | collective-permute-start | bytes 1572872 | tf_op jit(solution)/shard_map/ppermute | solution.py:38
  12.5 12.5 %collective-permute-start.7 = (bf16[256,1024]{1,0:T(8,128)(2,1)S(1)}, bf16[256,1024]{1,0:T(8,128)(2,1)S(1)}, u32[]{:S(2)}, u32[]{:S(2)}) collective-permute-start(bf16[256,1024]{1,0:T(8,128)(2,1)S(1)} %get-tuple-element.17.one.own.unit), channel_id=1, source_target_pairs={{0,1},{1,2},{2,3},{3,4},{4,5},{5,6},{6,7},{7,8},{8,9},{9,10},{10,1... | collective-permute-start | bytes 1572872 | tf_op jit(solution)/shard_map/ppermute | solution.py:38
  25.0 2.3 %collective-permute-start.2 = (bf16[256,1024]{1,0:T(8,128)(2,1)S(1)}, bf16[256,1024]{1,0:T(8,128)(2,1)S(1)}, u32[]{:S(2)}, u32[]{:S(2)}) collective-permute-start(bf16[256,1024]{1,0:T(8,128)(2,1)S(1)} %get-tuple-element.17.one.own.unit), channel_id=1, source_target_pairs={{0,256},{1,257},{2,258},{3,259},{4,260},{5,261},{6,262},{7,263},{8... | collective-permute-start | bytes 1572872 | tf_op jit(solution)/shard_map/ppermute | solution.py:38
  27.3 0.7 collective-permute-start.5
  28.0 0.0 collective-permute-done.other
  28.1 1.3 %collective-permute-start.1 = (bf16[256,1024]{1,0:T(8,128)(2,1)S(1)}, bf16[256,1024]{1,0:T(8,128)(2,1)S(1)}, u32[]{:S(2)}, u32[]{:S(2)}) collective-permute-start(bf16[256,1024]{1,0:T(8,128)(2,1)S(1)} %collective-permute-done.other), channel_id=1, source_target_pairs={{0,1},{1,2},{2,3},{3,4},{4,5},{5,6},{6,7},{7,8},{8,9},{9,10},{10,1... | collective-permute-start | bytes 1572872 | tf_op jit(solution)/shard_map/ppermute | solution.py:38
  29.4 0.0 collective-permute-done.3
  29.4 1.3 %collective-permute-start.4 = (bf16[256,1024]{1,0:T(8,128)(2,1)}, bf16[256,1024]{1,0:T(8,128)(2,1)}, u32[]{:S(2)}, u32[]{:S(2)}) collective-permute-start(bf16[256,1024]{1,0:T(8,128)(2,1)} %collective-permute-done.3), channel_id=1, source_target_pairs={{6,160},{7,32},{38,192},{39,64},{70,224},{71,96},{102,128},{103,0}... | collective-permute-start | bytes 1572872 | tf_op jit(solution)/shard_map/ppermute | solution.py:38
  30.7 3.7 %collective-permute-done.7.block = bf16[256,1024]{1,0:T(8,128)(2,1)S(1)} collective-permute-done((bf16[256,1024]{1,0:T(8,128)(2,1)S(1)}, bf16[256,1024]{1,0:T(8,128)(2,1)S(1)}, u32[]{:S(2)}, u32[]{:S(2)}) %collective-permute-start.7) | collective-permute-done | bytes 524320 | tf_op jit(solution)/shard_map/ppermute | solution.py:38
  34.5 1.3 %collective-permute-start.8 = (bf16[256,1024]{1,0:T(8,128)(2,1)S(1)}, bf16[256,1024]{1,0:T(8,128)(2,1)S(1)}, u32[]{:S(2)}, u32[]{:S(2)}) collective-permute-start(bf16[256,1024]{1,0:T(8,128)(2,1)S(1)} %shard_map.34.one_a), channel_id=1, source_target_pairs={{0,1},{1,2},{2,3},{3,4},{4,5},{5,6},{6,7},{7,8},{8,9},{9,10},{10,1... | collective-permute-start | bytes 1572872 | tf_op jit(solution)/shard_map/ppermute | solution.py:38
  35.8 8.7 %collective-permute-done.2.block = bf16[256,1024]{1,0:T(8,128)(2,1)S(1)} collective-permute-done((bf16[256,1024]{1,0:T(8,128)(2,1)S(1)}, bf16[256,1024]{1,0:T(8,128)(2,1)S(1)}, u32[]{:S(2)}, u32[]{:S(2)}) %collective-permute-start.2) | collective-permute-done | bytes 524320 | tf_op jit(solution)/shard_map/ppermute | solution.py:38
  44.5 0.0 collective-permute-done.5.block
  44.6 0.6 collective-permute-done.1.one_b
  45.1 6.8 %collective-permute-done.4.block = bf16[256,1024]{1,0:T(8,128)(2,1)} collective-permute-done((bf16[256,1024]{1,0:T(8,128)(2,1)}, bf16[256,1024]{1,0:T(8,128)(2,1)}, u32[]{:S(2)}, u32[]{:S(2)}) %collective-permute-start.4) | collective-permute-done | bytes 524320 | tf_op jit(solution)/shard_map/ppermute | solution.py:38
  52.0 1.1 %shard_map.30.near_b = bf16[256,1024]{1,0:T(8,128)(2,1)S(1)} custom-call(bf16[256,1024]{1,0:T(8,128)(2,1)} %collective-permute-done.4.block), custom_call_target="tpu_custom_call" | custom-call | flops 400000000 | bytes 524288 | tf_op jit(solution)/shard_map/pallas_call | solution.py:78
  53.0 0.1 shard_map.32
  53.2 1.3 %collective-permute-start.6 = (bf16[256,1024]{1,0:T(8,128)(2,1)S(1)}, bf16[256,1024]{1,0:T(8,128)(2,1)S(1)}, u32[]{:S(2)}, u32[]{:S(2)}) collective-permute-start(bf16[256,1024]{1,0:T(8,128)(2,1)S(1)} %get-tuple-element.22.one_b), channel_id=1, source_target_pairs={{0,1},{1,2},{2,3},{3,4},{4,5},{5,6},{6,7},{7,8},{8,9},{9,10},{10,1... | collective-permute-start | bytes 1572872 | tf_op jit(solution)/shard_map/ppermute | solution.py:38
  54.5 2.3 %collective-permute-start.9 = (bf16[256,1024]{1,0:T(8,128)(2,1)S(1)}, bf16[256,1024]{1,0:T(8,128)(2,1)S(1)}, u32[]{:S(2)}, u32[]{:S(2)}) collective-permute-start(bf16[256,1024]{1,0:T(8,128)(2,1)S(1)} %shard_map.29.one), channel_id=1, source_target_pairs={{0,128},{1,129},{2,130},{3,131},{4,132},{5,133},{6,134},{7,135},{8... | collective-permute-start | bytes 1572872 | tf_op jit(solution)/shard_map/ppermute | solution.py:38
  56.8 0.0 collective-permute-done.8.block
  56.8 6.3 %collective-permute-done.6.block = bf16[256,1024]{1,0:T(8,128)(2,1)S(1)} collective-permute-done((bf16[256,1024]{1,0:T(8,128)(2,1)S(1)}, bf16[256,1024]{1,0:T(8,128)(2,1)S(1)}, u32[]{:S(2)}, u32[]{:S(2)}) %collective-permute-start.6) | collective-permute-done | bytes 524320 | tf_op jit(solution)/shard_map/ppermute | solution.py:38
  63.1 0.0 collective-permute-done.9.other
  63.2 1.1 %shard_map.38.old_ref = f32[256,1024]{1,0:T(8,128)S(1)} custom-call(bf16[256,1024]{1,0:T(8,128)(2,1)S(1)} %shard_map.29.one, bf16[256,1024]{1,0:T(8,128)(2,1)S(1)} %collective-permute-done.9.other, bf16[256,1024]{1,0:T(8,128)(2,1)S(1)} %get-tuple-element.17.one.own.unit, bf16[256,1024]{1,0:T(8,128)(2,1)S(1)} %shard_map.34.one_a, ...), custom_call_target="tpu_custom_call" | custom-call | bytes 3145728 | tf_op jit(solution)/shard_map/pallas_call | solution.py:78
  64.3 0.7 shard_map.39
  65.0 1.9 %collective-permute-start.10 = (bf16[128,1024]{1,0:T(8,128)(2,1)S(1)}, bf16[128,1024]{1,0:T(8,128)(2,1)S(1)}, u32[]{:S(2)}, u32[]{:S(2)}) collective-permute-start(bf16[128,1024]{1,0:T(8,128)(2,1)S(1)} %get-tuple-element.27), channel_id=1, source_target_pairs={{0,128},{1,129},{2,130},{3,131},{4,132},{5,133},{6,134},{7,135},{8... | collective-permute-start | bytes 786440 | tf_op jit(solution)/shard_map/ppermute | solution.py:38
  66.9 1.1 %shard_map.36.old_ref = f32[256,1024]{1,0:T(8,128)S(1)} custom-call(bf16[256,1024]{1,0:T(8,128)(2,1)S(1)} %get-tuple-element.17.one.own.unit, bf16[256,1024]{1,0:T(8,128)(2,1)S(1)} %collective-permute-done.other, bf16[256,1024]{1,0:T(8,128)(2,1)S(1)} %get-tuple-element.17.one.own.unit, bf16[256,1024]{1,0:T(8,128)(2,1)S(1)} %shard_map.34.one_a, ...), custom_call_target="tpu_custom_call" | custom-call | flops 800000000 | bytes 3145728 | tf_op jit(solution)/shard_map/pallas_call | solution.py:78
  68.0 0.4 collective-permute-done.10.got
  68.4 1.9 %collective-permute-start.12 = (bf16[128,1024]{1,0:T(8,128)(2,1)S(1)}, bf16[128,1024]{1,0:T(8,128)(2,1)S(1)}, u32[]{:S(2)}, u32[]{:S(2)}) collective-permute-start(bf16[128,1024]{1,0:T(8,128)(2,1)S(1)} %shard_map.40), channel_id=1, source_target_pairs={{0,256},{1,257},{2,258},{3,259},{4,260},{5,261},{6,262},{7,263},{8... | collective-permute-start | bytes 786440 | tf_op jit(solution)/shard_map/ppermute | solution.py:38
  70.4 0.7 shard_map.37
  71.1 2.1 %collective-permute-start.11 = (bf16[128,1024]{1,0:T(8,128)(2,1)S(1)}, bf16[128,1024]{1,0:T(8,128)(2,1)S(1)}, u32[]{:S(2)}, u32[]{:S(2)}) collective-permute-start(bf16[128,1024]{1,0:T(8,128)(2,1)S(1)} %get-tuple-element.28), channel_id=1, source_target_pairs={{0,128},{1,129},{2,130},{3,131},{4,132},{5,133},{6,134},{7,135},{8... | collective-permute-start | bytes 786440 | tf_op jit(solution)/shard_map/ppermute | solution.py:38
  73.1 5.0 %collective-permute-done.12.block = bf16[128,1024]{1,0:T(8,128)(2,1)S(1)} collective-permute-done((bf16[128,1024]{1,0:T(8,128)(2,1)S(1)}, bf16[128,1024]{1,0:T(8,128)(2,1)S(1)}, u32[]{:S(2)}, u32[]{:S(2)}) %collective-permute-start.12) | collective-permute-done | bytes 262176 | tf_op jit(solution)/shard_map/ppermute | solution.py:38
  78.1 0.0 collective-permute-done.11.got
  78.1 1.0 %shard_map.42 = bf16[128,1024]{1,0:T(8,128)(2,1)} custom-call(bf16[256,1024]{1,0:T(8,128)(2,1)S(1)} %get-tuple-element.17.one.own.unit, f32[128,1]{1,0:T(8,128)S(1)} %get-tuple-element.18.inv, f32[128,1024]{1,0:T(8,128)S(1)} %get-tuple-element.23.keep, bf16[128,1024]{1,0:T(8,128)(2,1)S(1)} %collective-permute-done.11.got, ...), custom_call_target="tpu_custom_call" | custom-call | flops 1048576 | bytes 1573376 | tf_op jit(solution)/shard_map/pallas_call | solution.py:78
  (7 shorter events, 0.2 us)
Async XLA Ops:
  0.0 0.9 %copy-start = (bf16[128,1024]{1,0:T(8,128)(2,1)S(1)}, bf16[128,1024]{1,0:T(8,128)(2,1)}, u32[]{:S(2)}) copy-start(bf16[128,1024]{1,0:T(8,128)(2,1)} %s_hbm.1) | copy-start | bytes 786436
  1.0 0.9 %copy-start.1 = (bf16[128,1024]{1,0:T(8,128)(2,1)S(1)}, bf16[128,1024]{1,0:T(8,128)(2,1)}, u32[]{:S(2)}) copy-start(bf16[128,1024]{1,0:T(8,128)(2,1)} %t_hbm.1) | copy-start | bytes 786436
  2.2 25.8 %collective-permute-start = (bf16[256,1024]{1,0:T(8,128)(2,1)S(1)}, bf16[256,1024]{1,0:T(8,128)(2,1)S(1)}, u32[]{:S(2)}, u32[]{:S(2)}) collective-permute-start(bf16[256,1024]{1,0:T(8,128)(2,1)S(1)} %get-tuple-element.17.one.own.unit), channel_id=1, source_target_pairs={{0,128},{1,129},{2,130},{3,131},{4,132},{5,133},{6,134},{7,135},{8... | collective-permute-start | bytes 1572872 | tf_op jit(solution)/shard_map/ppermute | solution.py:38
  11.0 18.3 %collective-permute-start.3 = (bf16[256,1024]{1,0:T(8,128)(2,1)S(1)}, bf16[256,1024]{1,0:T(8,128)(2,1)}, u32[]{:S(2)}, u32[]{:S(2)}) collective-permute-start(bf16[256,1024]{1,0:T(8,128)(2,1)S(1)} %get-tuple-element.17.one.own.unit), channel_id=1, source_target_pairs={{0,152},{1,153},{32,184},{33,185},{64,216},{65,217},{96,248},{97,2... | collective-permute-start | bytes 1572872 | tf_op jit(solution)/shard_map/ppermute | solution.py:38
  12.5 21.9 %collective-permute-start.7 = (bf16[256,1024]{1,0:T(8,128)(2,1)S(1)}, bf16[256,1024]{1,0:T(8,128)(2,1)S(1)}, u32[]{:S(2)}, u32[]{:S(2)}) collective-permute-start(bf16[256,1024]{1,0:T(8,128)(2,1)S(1)} %get-tuple-element.17.one.own.unit), channel_id=1, source_target_pairs={{0,1},{1,2},{2,3},{3,4},{4,5},{5,6},{6,7},{7,8},{8,9},{9,10},{10,1... | collective-permute-start | bytes 1572872 | tf_op jit(solution)/shard_map/ppermute | solution.py:38
  25.0 19.5 %collective-permute-start.2 = (bf16[256,1024]{1,0:T(8,128)(2,1)S(1)}, bf16[256,1024]{1,0:T(8,128)(2,1)S(1)}, u32[]{:S(2)}, u32[]{:S(2)}) collective-permute-start(bf16[256,1024]{1,0:T(8,128)(2,1)S(1)} %get-tuple-element.17.one.own.unit), channel_id=1, source_target_pairs={{0,256},{1,257},{2,258},{3,259},{4,260},{5,261},{6,262},{7,263},{8... | collective-permute-start | bytes 1572872 | tf_op jit(solution)/shard_map/ppermute | solution.py:38
  27.3 17.2 %collective-permute-start.5 = (bf16[256,1024]{1,0:T(8,128)(2,1)S(1)}, bf16[256,1024]{1,0:T(8,128)(2,1)S(1)}, u32[]{:S(2)}, u32[]{:S(2)}) collective-permute-start(bf16[256,1024]{1,0:T(8,128)(2,1)S(1)} %get-tuple-element.17.one.own.unit), channel_id=1, source_target_pairs={{30,32},{62,64},{94,96},{126,0},{129,255},{161,159},{193,191},{225... | collective-permute-start | bytes 1572872 | tf_op jit(solution)/shard_map/ppermute | solution.py:38
  28.1 17.1 %collective-permute-start.1 = (bf16[256,1024]{1,0:T(8,128)(2,1)S(1)}, bf16[256,1024]{1,0:T(8,128)(2,1)S(1)}, u32[]{:S(2)}, u32[]{:S(2)}) collective-permute-start(bf16[256,1024]{1,0:T(8,128)(2,1)S(1)} %collective-permute-done.other), channel_id=1, source_target_pairs={{0,1},{1,2},{2,3},{3,4},{4,5},{5,6},{6,7},{7,8},{8,9},{9,10},{10,1... | collective-permute-start | bytes 1572872 | tf_op jit(solution)/shard_map/ppermute | solution.py:38
  29.4 22.6 %collective-permute-start.4 = (bf16[256,1024]{1,0:T(8,128)(2,1)}, bf16[256,1024]{1,0:T(8,128)(2,1)}, u32[]{:S(2)}, u32[]{:S(2)}) collective-permute-start(bf16[256,1024]{1,0:T(8,128)(2,1)} %collective-permute-done.3), channel_id=1, source_target_pairs={{6,160},{7,32},{38,192},{39,64},{70,224},{71,96},{102,128},{103,0}... | collective-permute-start | bytes 1572872 | tf_op jit(solution)/shard_map/ppermute | solution.py:38
  34.5 22.3 %collective-permute-start.8 = (bf16[256,1024]{1,0:T(8,128)(2,1)S(1)}, bf16[256,1024]{1,0:T(8,128)(2,1)S(1)}, u32[]{:S(2)}, u32[]{:S(2)}) collective-permute-start(bf16[256,1024]{1,0:T(8,128)(2,1)S(1)} %shard_map.34.one_a), channel_id=1, source_target_pairs={{0,1},{1,2},{2,3},{3,4},{4,5},{5,6},{6,7},{7,8},{8,9},{9,10},{10,1... | collective-permute-start | bytes 1572872 | tf_op jit(solution)/shard_map/ppermute | solution.py:38
  53.2 9.9 %collective-permute-start.6 = (bf16[256,1024]{1,0:T(8,128)(2,1)S(1)}, bf16[256,1024]{1,0:T(8,128)(2,1)S(1)}, u32[]{:S(2)}, u32[]{:S(2)}) collective-permute-start(bf16[256,1024]{1,0:T(8,128)(2,1)S(1)} %get-tuple-element.22.one_b), channel_id=1, source_target_pairs={{0,1},{1,2},{2,3},{3,4},{4,5},{5,6},{6,7},{7,8},{8,9},{9,10},{10,1... | collective-permute-start | bytes 1572872 | tf_op jit(solution)/shard_map/ppermute | solution.py:38
  54.5 8.7 %collective-permute-start.9 = (bf16[256,1024]{1,0:T(8,128)(2,1)S(1)}, bf16[256,1024]{1,0:T(8,128)(2,1)S(1)}, u32[]{:S(2)}, u32[]{:S(2)}) collective-permute-start(bf16[256,1024]{1,0:T(8,128)(2,1)S(1)} %shard_map.29.one), channel_id=1, source_target_pairs={{0,128},{1,129},{2,130},{3,131},{4,132},{5,133},{6,134},{7,135},{8... | collective-permute-start | bytes 1572872 | tf_op jit(solution)/shard_map/ppermute | solution.py:38
  65.0 3.4 %collective-permute-start.10 = (bf16[128,1024]{1,0:T(8,128)(2,1)S(1)}, bf16[128,1024]{1,0:T(8,128)(2,1)S(1)}, u32[]{:S(2)}, u32[]{:S(2)}) collective-permute-start(bf16[128,1024]{1,0:T(8,128)(2,1)S(1)} %get-tuple-element.27), channel_id=1, source_target_pairs={{0,128},{1,129},{2,130},{3,131},{4,132},{5,133},{6,134},{7,135},{8... | collective-permute-start | bytes 786440 | tf_op jit(solution)/shard_map/ppermute | solution.py:38
  68.4 9.7 %collective-permute-start.12 = (bf16[128,1024]{1,0:T(8,128)(2,1)S(1)}, bf16[128,1024]{1,0:T(8,128)(2,1)S(1)}, u32[]{:S(2)}, u32[]{:S(2)}) collective-permute-start(bf16[128,1024]{1,0:T(8,128)(2,1)S(1)} %shard_map.40), channel_id=1, source_target_pairs={{0,256},{1,257},{2,258},{3,259},{4,260},{5,261},{6,262},{7,263},{8... | collective-permute-start | bytes 786440 | tf_op jit(solution)/shard_map/ppermute | solution.py:38
  71.1 7.1 %collective-permute-start.11 = (bf16[128,1024]{1,0:T(8,128)(2,1)S(1)}, bf16[128,1024]{1,0:T(8,128)(2,1)S(1)}, u32[]{:S(2)}, u32[]{:S(2)}) collective-permute-start(bf16[128,1024]{1,0:T(8,128)(2,1)S(1)} %get-tuple-element.28), channel_id=1, source_target_pairs={{0,128},{1,129},{2,130},{3,131},{4,132},{5,133},{6,134},{7,135},{8... | collective-permute-start | bytes 786440 | tf_op jit(solution)/shard_map/ppermute | solution.py:38

commit v3 on v2

--- a/solution.py
+++ b/solution.py
@@ -13,17 +13,20 @@
 F32 = jnp.float32
 BF16 = jnp.bfloat16
 C1 = 400000000
-C2 = 800000000
+C2 = 400000000
 C3 = 1
 C4 = 400000000
-C5 = 400000000
-C6 = 800000000
-C7 = 400000000
-C9 = 100000000
-C10 = 100000000
-C12 = 400000000
-C11 = 800000000
-C8 = 800000000
+C5 = 6400000000
+C6 = 100000000
+C7 = 800000000
+C9 = 400000000
+C10 = 200000000
+C15 = 1600000000
+C14 = 6400000000
+C13 = 400000000
+C12 = 200000000
+C11 = 400000000
+C8 = 400000000
 VMEM = pl.BlockSpec(memory_space=pltpu.VMEM)
 ROW_BY_ROW = (((1,), (1,)), ((), ()))
 
@@ -81,7 +84,7 @@
         in_specs=[pl.BlockSpec(memory_space=pltpu.SMEM) if x.ndim == 1 else VMEM for x in operands],
         out_specs=jax.tree.map(lambda _: VMEM, out_shape),
         cost_estimate=pl.CostEstimate(flops=flops, bytes_accessed=size, transcendentals=0),
-        compiler_params=pltpu.CompilerParams(vmem_limit_bytes=40 * 2**20),
+        compiler_params=pltpu.CompilerParams(vmem_limit_bytes=16 * 2**20),
     )(*operands)
 
 
@@ -109,7 +112,7 @@
         out_specs=(VMEM, VMEM),
         scratch_shapes=[pltpu.VMEM((ROWS, D), BF16)] * 2 + [pltpu.SemaphoreType.DMA((2,))],
         cost_estimate=pl.CostEstimate(flops=10 * ROWS * D, bytes_accessed=4 * ROWS * D, transcendentals=0),
-        compiler_params=pltpu.CompilerParams(vmem_limit_bytes=40 * 2**20),
+        compiler_params=pltpu.CompilerParams(vmem_limit_bytes=16 * 2**20),
     )(student, teacher)
 
 
@@ -130,11 +133,12 @@
     out_ref[...] = block[...]
 
 
-def mix_kernel(flag, one_b, near_b, direct, next_ref, extra_ref):
-    at_end = flag[0] == 1
-    none = jnp.zeros_like(near_b)
-    next_ref[...] = one_b[...] + jnp.where(at_end, near_b[...], none)
-    extra_ref[...] = direct[...] + jnp.where(at_end, none, near_b[...])
+def next_kernel(flag, one_b, near_b, rows_ref):
+    rows_ref[...] = one_b[...] + jnp.where(flag[0] == 1, near_b[...], jnp.zeros_like(near_b))
+
+
+def extra_kernel(flag, near_b, direct, rows_ref):
+    rows_ref[...] = direct[...] + jnp.where(flag[0] == 1, jnp.zeros_like(near_b), near_b[...])
 
 
 def first_kernel(one, other, own, one_a, one_b, two_a, sum_ref):
@@ -173,21 +177,22 @@
     gram = 2 * 3 * 2 * ROWS * ROWS * D
     own, inv = unit_rows(student, teacher)
     one_a = hold(route(own, along), C9)
-    spread = route(own, aside)
+    spread = hold(route(own, aside), C13)
     direct = hold(route(own, across), C11)
-    far = hold(route(own, to_y), C6)
+    far = hold(route(after(own, spread), to_y), C6)
     sib = route(own, to_core)
-    one_b = route(sib, along_inside)
-    near_b = hold(route(spread, from_aside), C12)
+    one_b = hold(route(sib, along_inside), C15)
+    near_b = route(spread, from_aside)
     core = lax.axis_index("section") % 2
     place = lax.axis_index("dp") % RUN
     flag = (place == core * (RUN - 1)).astype(jnp.int32).reshape(1)
-    one_b, extra = call(mix_kernel, (both, both), C1, flag, after(one_b, far), near_b, direct)
+    one_b = call(next_kernel, both, C1, flag, one_b, near_b)
+    extra = call(extra_kernel, both, C7, flag, near_b, direct)
     two_a = hold(route(one_a, along_inside), C5)
-    two_b = hold(route(one_b, along_inside), C2)
+    two_b = route(one_b, along_inside)
     near_sum = call(first_kernel, half, C8, own, sib, own, one_a, after(one_b, far), two_a)
-    cross = route(after(far, one_b), to_core)
-    away_sum = call(first_kernel, half, 0, far, cross, own, one_a, one_b, two_a)
+    cross = route(after(far, one_b, extra), to_core)
+    away_sum = call(first_kernel, half, C14, far, cross, own, one_a, one_b, two_a)
     keep_far, send_far = call(
         final_kernel, (quarter_f, quarter_h), C4, far, cross, two_b, extra, away_sum
     )

time: 79.6 us -> 74.8 us (0.940)
  waiting for transfers between devices: 31.5 us -> 24.1 us
  Pallas kernels: 6.32 us -> 8.22 us
    ppermute x13, waiting for transfers between devices: 31.5 us -> 24.1 us  [route(): return lax.ppermute(block, ('section', 'dp'), pairs)]
    pallas_call x14 -> x15, Pallas kernels: 5.99 us -> 7.89 us  [call(): pl.pallas_call(kernel, out_shape=out_shape, in_specs=[pl.BlockSpec(memory...]
  transfers between devices with their start and end apart: 13 -> 13, of which waited for: 7 -> 7; matrix products, arithmetic and copies ran while one was open for 0% -> 0% of each run, Pallas kernels for 4% -> 8%
where the time goes in v3:
time: 74.8 us; the launch traced here: 74.2 us
  starting transfers between devices  39.7 us (53%)
  waiting for transfers between devices  24.1 us (32%)
  Pallas kernels  8.22 us (11%)
  local copies, waits for them, and re-layouts  1.9 us (3%)
    ppermute x13, starting transfers between devices, route(): return lax.ppermute(block, ('section', 'dp'), pairs)  39.7 us
    ppermute x13, waiting for transfers between devices, route(): return lax.ppermute(block, ('section', 'dp'), pairs)  24.1 us
    pallas_call x15, Pallas kernels, call(): pl.pallas_call(kernel, out_shape=out_shape, in_specs=[pl.BlockSpec(memory...  7.89 us
    unnamed x4, local copies, waits for them, and re-layouts  1.9 us
  transfers between devices with their start and end apart: 13, of which 7 were waited for; matrix products, arithmetic and copies ran while one was open for 0% of the time, Pallas kernels for 8%

profile of v3, /device:TPU:1, one launch (start us, length us, event | category | flops | bytes accessed | tf_op | source)
XLA Modules:
  0.0 74.2 jit_solution(152353271237203258)
XLA Ops:
  0.0 0.0 copy-start
  0.0 0.9 %copy-done = bf16[128,1024]{1,0:T(8,128)(2,1)S(1)} copy-done((bf16[128,1024]{1,0:T(8,128)(2,1)S(1)}, bf16[128,1024]{1,0:T(8,128)(2,1)}, u32[]{:S(2)}) %copy-start) | copy-done | bytes 262168
  1.0 0.0 copy-start.1
  1.0 0.9 %copy-done.1 = bf16[128,1024]{1,0:T(8,128)(2,1)S(1)} copy-done((bf16[128,1024]{1,0:T(8,128)(2,1)S(1)}, bf16[128,1024]{1,0:T(8,128)(2,1)}, u32[]{:S(2)}) %copy-start.1) | copy-done | bytes 262168
  1.9 0.3 shard_map.28
  2.2 8.8 %collective-permute-start = (bf16[256,1024]{1,0:T(8,128)(2,1)S(1)}, bf16[256,1024]{1,0:T(8,128)(2,1)S(1)}, u32[]{:S(2)}, u32[]{:S(2)}) collective-permute-start(bf16[256,1024]{1,0:T(8,128)(2,1)S(1)} %get-tuple-element.17.one.own.unit), channel_id=1, source_target_pairs={{0,128},{1,129},{2,130},{3,131},{4,132},{5,133},{6,134},{7,135},{8... | collective-permute-start | bytes 1572872 | tf_op jit(solution)/shard_map/ppermute | solution.py:41
  11.0 0.7 collective-permute-start.2
  11.7 12.5 %collective-permute-start.6 = (bf16[256,1024]{1,0:T(8,128)(2,1)S(1)}, bf16[256,1024]{1,0:T(8,128)(2,1)S(1)}, u32[]{:S(2)}, u32[]{:S(2)}) collective-permute-start(bf16[256,1024]{1,0:T(8,128)(2,1)S(1)} %get-tuple-element.17.one.own.unit), channel_id=1, source_target_pairs={{0,1},{1,2},{2,3},{3,4},{4,5},{5,6},{6,7},{7,8},{8,9},{9,10},{10,1... | collective-permute-start | bytes 1572872 | tf_op jit(solution)/shard_map/ppermute | solution.py:41
  24.3 1.5 %collective-permute-start.5 = (bf16[256,1024]{1,0:T(8,128)(2,1)S(1)}, bf16[256,1024]{1,0:T(8,128)(2,1)}, u32[]{:S(2)}, u32[]{:S(2)}) collective-permute-start(bf16[256,1024]{1,0:T(8,128)(2,1)S(1)} %get-tuple-element.17.one.own.unit), channel_id=1, source_target_pairs={{30,32},{62,64},{94,96},{126,0},{129,255},{161,159},{193,191},{225... | collective-permute-start | bytes 1572872 | tf_op jit(solution)/shard_map/ppermute | solution.py:41
  25.8 0.0 collective-permute-done.other
  25.8 1.3 %collective-permute-start.1 = (bf16[256,1024]{1,0:T(8,128)(2,1)S(1)}, bf16[256,1024]{1,0:T(8,128)(2,1)}, u32[]{:S(2)}, u32[]{:S(2)}) collective-permute-start(bf16[256,1024]{1,0:T(8,128)(2,1)S(1)} %collective-permute-done.other), channel_id=1, source_target_pairs={{0,1},{1,2},{2,3},{3,4},{4,5},{5,6},{6,7},{7,8},{8,9},{9,10},{10,1... | collective-permute-start | bytes 1572872 | tf_op jit(solution)/shard_map/ppermute | solution.py:41
  27.0 0.0 collective-permute-done.2.block
  27.1 0.8 %shard_map.30 = bf16[256,1024]{1,0:T(8,128)(2,1)} custom-call(bf16[256,1024]{1,0:T(8,128)(2,1)S(1)} %collective-permute-done.2.block), custom_call_target="tpu_custom_call" | custom-call | flops 400000000 | bytes 524288 | tf_op jit(solution)/shard_map/pallas_call | solution.py:81
  27.9 1.3 %collective-permute-start.3 = (bf16[256,1024]{1,0:T(8,128)(2,1)}, bf16[256,1024]{1,0:T(8,128)(2,1)S(1)}, u32[]{:S(2)}, u32[]{:S(2)}) collective-permute-start(bf16[256,1024]{1,0:T(8,128)(2,1)} %shard_map.30), channel_id=1, source_target_pairs={{6,160},{7,32},{38,192},{39,64},{70,224},{71,96},{102,128},{103,0}... | collective-permute-start | bytes 1572872 | tf_op jit(solution)/shard_map/ppermute | solution.py:41
  29.2 2.3 %collective-permute-start.7 = (bf16[256,1024]{1,0:T(8,128)(2,1)S(1)}, bf16[256,1024]{1,0:T(8,128)(2,1)S(1)}, u32[]{:S(2)}, u32[]{:S(2)}) collective-permute-start(bf16[256,1024]{1,0:T(8,128)(2,1)S(1)} %get-tuple-element.17.one.own.unit), channel_id=1, source_target_pairs={{0,256},{1,257},{2,258},{3,259},{4,260},{5,261},{6,262},{7,263},{8... | collective-permute-start | bytes 1572872 | tf_op jit(solution)/shard_map/ppermute | solution.py:41
  31.5 1.0 %collective-permute-done.6.block = bf16[256,1024]{1,0:T(8,128)(2,1)S(1)} collective-permute-done((bf16[256,1024]{1,0:T(8,128)(2,1)S(1)}, bf16[256,1024]{1,0:T(8,128)(2,1)S(1)}, u32[]{:S(2)}, u32[]{:S(2)}) %collective-permute-start.6) | collective-permute-done | bytes 524320 | tf_op jit(solution)/shard_map/ppermute | solution.py:41
  32.6 1.3 %collective-permute-start.8 = (bf16[256,1024]{1,0:T(8,128)(2,1)S(1)}, bf16[256,1024]{1,0:T(8,128)(2,1)S(1)}, u32[]{:S(2)}, u32[]{:S(2)}) collective-permute-start(bf16[256,1024]{1,0:T(8,128)(2,1)S(1)} %shard_map.34.one_a), channel_id=1, source_target_pairs={{0,1},{1,2},{2,3},{3,4},{4,5},{5,6},{6,7},{7,8},{8,9},{9,10},{10,1... | collective-permute-start | bytes 1572872 | tf_op jit(solution)/shard_map/ppermute | solution.py:41
  33.9 0.0 collective-permute-done.5.block
  33.9 1.1 %shard_map.32.direct = bf16[256,1024]{1,0:T(8,128)(2,1)S(1)} custom-call(bf16[256,1024]{1,0:T(8,128)(2,1)} %collective-permute-done.5.block), custom_call_target="tpu_custom_call" | custom-call | flops 400000000 | bytes 524288 | tf_op jit(solution)/shard_map/pallas_call | solution.py:81
  35.0 5.1 %collective-permute-done.1.block = bf16[256,1024]{1,0:T(8,128)(2,1)} collective-permute-done((bf16[256,1024]{1,0:T(8,128)(2,1)S(1)}, bf16[256,1024]{1,0:T(8,128)(2,1)}, u32[]{:S(2)}, u32[]{:S(2)}) %collective-permute-start.1) | collective-permute-done | bytes 524320 | tf_op jit(solution)/shard_map/ppermute | solution.py:41
  40.0 1.1 %shard_map.29.one_b = bf16[256,1024]{1,0:T(8,128)(2,1)S(1)} custom-call(bf16[256,1024]{1,0:T(8,128)(2,1)} %collective-permute-done.1.block), custom_call_target="tpu_custom_call" | custom-call | flops 1600000000 | bytes 524288 | tf_op jit(solution)/shard_map/pallas_call | solution.py:81
  41.1 8.3 %collective-permute-done.3.near_b = bf16[256,1024]{1,0:T(8,128)(2,1)S(1)} collective-permute-done((bf16[256,1024]{1,0:T(8,128)(2,1)}, bf16[256,1024]{1,0:T(8,128)(2,1)S(1)}, u32[]{:S(2)}, u32[]{:S(2)}) %collective-permute-start.3) | collective-permute-done | bytes 524320 | tf_op jit(solution)/shard_map/ppermute | solution.py:41
  49.4 0.1 shard_map.31.one_b
  49.5 1.3 %collective-permute-start.4 = (bf16[256,1024]{1,0:T(8,128)(2,1)S(1)}, bf16[256,1024]{1,0:T(8,128)(2,1)S(1)}, u32[]{:S(2)}, u32[]{:S(2)}) collective-permute-start(bf16[256,1024]{1,0:T(8,128)(2,1)S(1)} %shard_map.31.one_b), channel_id=1, source_target_pairs={{0,1},{1,2},{2,3},{3,4},{4,5},{5,6},{6,7},{7,8},{8,9},{9,10},{10,1... | collective-permute-start | bytes 1572872 | tf_op jit(solution)/shard_map/ppermute | solution.py:41
  50.8 0.0 collective-permute-done.7.block
  50.8 0.1 shard_map.33.extra
  51.0 2.4 %collective-permute-start.9 = (bf16[256,1024]{1,0:T(8,128)(2,1)S(1)}, bf16[256,1024]{1,0:T(8,128)(2,1)S(1)}, u32[]{:S(2)}, u32[]{:S(2)}) collective-permute-start(bf16[256,1024]{1,0:T(8,128)(2,1)S(1)} %shard_map.35.one), channel_id=1, source_target_pairs={{0,128},{1,129},{2,130},{3,131},{4,132},{5,133},{6,134},{7,135},{8... | collective-permute-start | bytes 1572872 | tf_op jit(solution)/shard_map/ppermute | solution.py:41
  53.4 0.0 collective-permute-done.8.block
  53.4 1.5 %collective-permute-done.9.other = bf16[256,1024]{1,0:T(8,128)(2,1)S(1)} collective-permute-done((bf16[256,1024]{1,0:T(8,128)(2,1)S(1)}, bf16[256,1024]{1,0:T(8,128)(2,1)S(1)}, u32[]{:S(2)}, u32[]{:S(2)}) %collective-permute-start.9) | collective-permute-done | bytes 524320 | tf_op jit(solution)/shard_map/ppermute | solution.py:41
  54.9 1.1 %shard_map.39.old_ref = f32[256,1024]{1,0:T(8,128)S(1)} custom-call(bf16[256,1024]{1,0:T(8,128)(2,1)S(1)} %shard_map.35.one, bf16[256,1024]{1,0:T(8,128)(2,1)S(1)} %collective-permute-done.9.other, bf16[256,1024]{1,0:T(8,128)(2,1)S(1)} %get-tuple-element.17.one.own.unit, bf16[256,1024]{1,0:T(8,128)(2,1)S(1)} %shard_map.34.one_a, ...), custom_call_target="tpu_custom_call" | custom-call | flops 6400000000 | bytes 3145728 | tf_op jit(solution)/shard_map/pallas_call | solution.py:81
  56.0 3.4 %collective-permute-done.4.two = bf16[256,1024]{1,0:T(8,128)(2,1)S(1)} collective-permute-done((bf16[256,1024]{1,0:T(8,128)(2,1)S(1)}, bf16[256,1024]{1,0:T(8,128)(2,1)S(1)}, u32[]{:S(2)}, u32[]{:S(2)}) %collective-permute-start.4) | collective-permute-done | bytes 524320 | tf_op jit(solution)/shard_map/ppermute | solution.py:41
  59.4 0.7 shard_map.40
  60.1 1.9 %collective-permute-start.10 = (bf16[128,1024]{1,0:T(8,128)(2,1)S(1)}, bf16[128,1024]{1,0:T(8,128)(2,1)S(1)}, u32[]{:S(2)}, u32[]{:S(2)}) collective-permute-start(bf16[128,1024]{1,0:T(8,128)(2,1)S(1)} %get-tuple-element.23), channel_id=1, source_target_pairs={{0,128},{1,129},{2,130},{3,131},{4,132},{5,133},{6,134},{7,135},{8... | collective-permute-start | bytes 786440 | tf_op jit(solution)/shard_map/ppermute | solution.py:41
  62.0 1.1 %shard_map.37.old_ref = f32[256,1024]{1,0:T(8,128)S(1)} custom-call(bf16[256,1024]{1,0:T(8,128)(2,1)S(1)} %get-tuple-element.17.one.own.unit, bf16[256,1024]{1,0:T(8,128)(2,1)S(1)} %collective-permute-done.other, bf16[256,1024]{1,0:T(8,128)(2,1)S(1)} %get-tuple-element.17.one.own.unit, bf16[256,1024]{1,0:T(8,128)(2,1)S(1)} %shard_map.34.one_a, ...), custom_call_target="tpu_custom_call" | custom-call | flops 400000000 | bytes 3145728 | tf_op jit(solution)/shard_map/pallas_call | solution.py:81
  63.1 0.4 collective-permute-done.10.got
  63.6 2.1 %collective-permute-start.12 = (bf16[128,1024]{1,0:T(8,128)(2,1)S(1)}, bf16[128,1024]{1,0:T(8,128)(2,1)S(1)}, u32[]{:S(2)}, u32[]{:S(2)}) collective-permute-start(bf16[128,1024]{1,0:T(8,128)(2,1)S(1)} %shard_map.41), channel_id=1, source_target_pairs={{0,256},{1,257},{2,258},{3,259},{4,260},{5,261},{6,262},{7,263},{8... | collective-permute-start | bytes 786440 | tf_op jit(solution)/shard_map/ppermute | solution.py:41
  65.7 0.7 shard_map.38
  66.4 2.3 %collective-permute-start.11 = (bf16[128,1024]{1,0:T(8,128)(2,1)S(1)}, bf16[128,1024]{1,0:T(8,128)(2,1)S(1)}, u32[]{:S(2)}, u32[]{:S(2)}) collective-permute-start(bf16[128,1024]{1,0:T(8,128)(2,1)S(1)} %get-tuple-element.24), channel_id=1, source_target_pairs={{0,128},{1,129},{2,130},{3,131},{4,132},{5,133},{6,134},{7,135},{8... | collective-permute-start | bytes 786440 | tf_op jit(solution)/shard_map/ppermute | solution.py:41
  68.7 4.5 %collective-permute-done.12.block = bf16[128,1024]{1,0:T(8,128)(2,1)S(1)} collective-permute-done((bf16[128,1024]{1,0:T(8,128)(2,1)S(1)}, bf16[128,1024]{1,0:T(8,128)(2,1)S(1)}, u32[]{:S(2)}, u32[]{:S(2)}) %collective-permute-start.12) | collective-permute-done | bytes 262176 | tf_op jit(solution)/shard_map/ppermute | solution.py:41
  73.2 0.0 collective-permute-done.11.got
  73.2 1.0 %shard_map.43 = bf16[128,1024]{1,0:T(8,128)(2,1)} custom-call(bf16[256,1024]{1,0:T(8,128)(2,1)S(1)} %get-tuple-element.17.one.own.unit, f32[128,1]{1,0:T(8,128)S(1)} %get-tuple-element.16.inv, f32[128,1024]{1,0:T(8,128)S(1)} %get-tuple-element.19.keep, bf16[128,1024]{1,0:T(8,128)(2,1)S(1)} %collective-permute-done.11.got, ...), custom_call_target="tpu_custom_call" | custom-call | flops 1048576 | bytes 1573376 | tf_op jit(solution)/shard_map/pallas_call | solution.py:81
  (5 shorter events, 0.2 us)
Async XLA Ops:
  0.0 0.9 %copy-start = (bf16[128,1024]{1,0:T(8,128)(2,1)S(1)}, bf16[128,1024]{1,0:T(8,128)(2,1)}, u32[]{:S(2)}) copy-start(bf16[128,1024]{1,0:T(8,128)(2,1)} %s_hbm.1) | copy-start | bytes 786436
  1.0 0.9 %copy-start.1 = (bf16[128,1024]{1,0:T(8,128)(2,1)S(1)}, bf16[128,1024]{1,0:T(8,128)(2,1)}, u32[]{:S(2)}) copy-start(bf16[128,1024]{1,0:T(8,128)(2,1)} %t_hbm.1) | copy-start | bytes 786436
  2.2 23.5 %collective-permute-start = (bf16[256,1024]{1,0:T(8,128)(2,1)S(1)}, bf16[256,1024]{1,0:T(8,128)(2,1)S(1)}, u32[]{:S(2)}, u32[]{:S(2)}) collective-permute-start(bf16[256,1024]{1,0:T(8,128)(2,1)S(1)} %get-tuple-element.17.one.own.unit), channel_id=1, source_target_pairs={{0,128},{1,129},{2,130},{3,131},{4,132},{5,133},{6,134},{7,135},{8... | collective-permute-start | bytes 1572872 | tf_op jit(solution)/shard_map/ppermute | solution.py:41
  11.0 16.0 %collective-permute-start.2 = (bf16[256,1024]{1,0:T(8,128)(2,1)S(1)}, bf16[256,1024]{1,0:T(8,128)(2,1)S(1)}, u32[]{:S(2)}, u32[]{:S(2)}) collective-permute-start(bf16[256,1024]{1,0:T(8,128)(2,1)S(1)} %get-tuple-element.17.one.own.unit), channel_id=1, source_target_pairs={{0,152},{1,153},{32,184},{33,185},{64,216},{65,217},{96,248},{97,2... | collective-permute-start | bytes 1572872 | tf_op jit(solution)/shard_map/ppermute | solution.py:41
  11.7 20.8 %collective-permute-start.6 = (bf16[256,1024]{1,0:T(8,128)(2,1)S(1)}, bf16[256,1024]{1,0:T(8,128)(2,1)S(1)}, u32[]{:S(2)}, u32[]{:S(2)}) collective-permute-start(bf16[256,1024]{1,0:T(8,128)(2,1)S(1)} %get-tuple-element.17.one.own.unit), channel_id=1, source_target_pairs={{0,1},{1,2},{2,3},{3,4},{4,5},{5,6},{6,7},{7,8},{8,9},{9,10},{10,1... | collective-permute-start | bytes 1572872 | tf_op jit(solution)/shard_map/ppermute | solution.py:41
  24.3 9.6 %collective-permute-start.5 = (bf16[256,1024]{1,0:T(8,128)(2,1)S(1)}, bf16[256,1024]{1,0:T(8,128)(2,1)}, u32[]{:S(2)}, u32[]{:S(2)}) collective-permute-start(bf16[256,1024]{1,0:T(8,128)(2,1)S(1)} %get-tuple-element.17.one.own.unit), channel_id=1, source_target_pairs={{30,32},{62,64},{94,96},{126,0},{129,255},{161,159},{193,191},{225... | collective-permute-start | bytes 1572872 | tf_op jit(solution)/shard_map/ppermute | solution.py:41
  25.8 14.3 %collective-permute-start.1 = (bf16[256,1024]{1,0:T(8,128)(2,1)S(1)}, bf16[256,1024]{1,0:T(8,128)(2,1)}, u32[]{:S(2)}, u32[]{:S(2)}) collective-permute-start(bf16[256,1024]{1,0:T(8,128)(2,1)S(1)} %collective-permute-done.other), channel_id=1, source_target_pairs={{0,1},{1,2},{2,3},{3,4},{4,5},{5,6},{6,7},{7,8},{8,9},{9,10},{10,1... | collective-permute-start | bytes 1572872 | tf_op jit(solution)/shard_map/ppermute | solution.py:41
  27.9 21.5 %collective-permute-start.3 = (bf16[256,1024]{1,0:T(8,128)(2,1)}, bf16[256,1024]{1,0:T(8,128)(2,1)S(1)}, u32[]{:S(2)}, u32[]{:S(2)}) collective-permute-start(bf16[256,1024]{1,0:T(8,128)(2,1)} %shard_map.30), channel_id=1, source_target_pairs={{6,160},{7,32},{38,192},{39,64},{70,224},{71,96},{102,128},{103,0}... | collective-permute-start | bytes 1572872 | tf_op jit(solution)/shard_map/ppermute | solution.py:41
  29.2 21.6 %collective-permute-start.7 = (bf16[256,1024]{1,0:T(8,128)(2,1)S(1)}, bf16[256,1024]{1,0:T(8,128)(2,1)S(1)}, u32[]{:S(2)}, u32[]{:S(2)}) collective-permute-start(bf16[256,1024]{1,0:T(8,128)(2,1)S(1)} %get-tuple-element.17.one.own.unit), channel_id=1, source_target_pairs={{0,256},{1,257},{2,258},{3,259},{4,260},{5,261},{6,262},{7,263},{8... | collective-permute-start | bytes 1572872 | tf_op jit(solution)/shard_map/ppermute | solution.py:41
  32.6 20.8 %collective-permute-start.8 = (bf16[256,1024]{1,0:T(8,128)(2,1)S(1)}, bf16[256,1024]{1,0:T(8,128)(2,1)S(1)}, u32[]{:S(2)}, u32[]{:S(2)}) collective-permute-start(bf16[256,1024]{1,0:T(8,128)(2,1)S(1)} %shard_map.34.one_a), channel_id=1, source_target_pairs={{0,1},{1,2},{2,3},{3,4},{4,5},{5,6},{6,7},{7,8},{8,9},{9,10},{10,1... | collective-permute-start | bytes 1572872 | tf_op jit(solution)/shard_map/ppermute | solution.py:41
  49.5 9.9 %collective-permute-start.4 = (bf16[256,1024]{1,0:T(8,128)(2,1)S(1)}, bf16[256,1024]{1,0:T(8,128)(2,1)S(1)}, u32[]{:S(2)}, u32[]{:S(2)}) collective-permute-start(bf16[256,1024]{1,0:T(8,128)(2,1)S(1)} %shard_map.31.one_b), channel_id=1, source_target_pairs={{0,1},{1,2},{2,3},{3,4},{4,5},{5,6},{6,7},{7,8},{8,9},{9,10},{10,1... | collective-permute-start | bytes 1572872 | tf_op jit(solution)/shard_map/ppermute | solution.py:41
  51.0 3.9 %collective-permute-start.9 = (bf16[256,1024]{1,0:T(8,128)(2,1)S(1)}, bf16[256,1024]{1,0:T(8,128)(2,1)S(1)}, u32[]{:S(2)}, u32[]{:S(2)}) collective-permute-start(bf16[256,1024]{1,0:T(8,128)(2,1)S(1)} %shard_map.35.one), channel_id=1, source_target_pairs={{0,128},{1,129},{2,130},{3,131},{4,132},{5,133},{6,134},{7,135},{8... | collective-permute-start | bytes 1572872 | tf_op jit(solution)/shard_map/ppermute | solution.py:41
  60.1 3.4 %collective-permute-start.10 = (bf16[128,1024]{1,0:T(8,128)(2,1)S(1)}, bf16[128,1024]{1,0:T(8,128)(2,1)S(1)}, u32[]{:S(2)}, u32[]{:S(2)}) collective-permute-start(bf16[128,1024]{1,0:T(8,128)(2,1)S(1)} %get-tuple-element.23), channel_id=1, source_target_pairs={{0,128},{1,129},{2,130},{3,131},{4,132},{5,133},{6,134},{7,135},{8... | collective-permute-start | bytes 786440 | tf_op jit(solution)/shard_map/ppermute | solution.py:41
  63.6 9.7 %collective-permute-start.12 = (bf16[128,1024]{1,0:T(8,128)(2,1)S(1)}, bf16[128,1024]{1,0:T(8,128)(2,1)S(1)}, u32[]{:S(2)}, u32[]{:S(2)}) collective-permute-start(bf16[128,1024]{1,0:T(8,128)(2,1)S(1)} %shard_map.41), channel_id=1, source_target_pairs={{0,256},{1,257},{2,258},{3,259},{4,260},{5,261},{6,262},{7,263},{8... | collective-permute-start | bytes 786440 | tf_op jit(solution)/shard_map/ppermute | solution.py:41
  66.4 6.9 %collective-permute-start.11 = (bf16[128,1024]{1,0:T(8,128)(2,1)S(1)}, bf16[128,1024]{1,0:T(8,128)(2,1)S(1)}, u32[]{:S(2)}, u32[]{:S(2)}) collective-permute-start(bf16[128,1024]{1,0:T(8,128)(2,1)S(1)} %get-tuple-element.24), channel_id=1, source_target_pairs={{0,128},{1,129},{2,130},{3,131},{4,132},{5,133},{6,134},{7,135},{8... | collective-permute-start | bytes 786440 | tf_op jit(solution)/shard_map/ppermute | solution.py:41

commit v4 on v3

--- a/solution.py
+++ b/solution.py
@@ -65,15 +65,25 @@
 
 
 def aside(q, d):
+    step = 24 if q < 2 else 7
     if q % 2 == 1:
-        return (q ^ 1, d - 24) if d % RUN in (RUN - 2, RUN - 1) else None
-    return (q ^ 1, d + 24) if d % RUN in (0, 1) else None
+        steps = {RUN - 1: -step, RUN - 2: -24}
+        return (q, d + steps[d % RUN]) if d % RUN in steps else None
+    steps = {0: step, 1: 24}
+    return (q ^ 1, d + steps[d % RUN]) if d % RUN in steps else None
 
 
 def from_aside(q, d):
     if q % 2 == 0:
-        return {7: (q, d + 25), 6: (q ^ 1, d + 26)}.get(d % RUN)
-    return {RUN - 8: (q, d - 25), RUN - 7: (q ^ 1, d - 26)}.get(d % RUN)
+        return None
+    step = 24 if q < 2 else 7
+    goals = {
+        RUN - 1 - step: (q ^ 1, d + step + 1),
+        step: (q, d - step - 1),
+        6: (q, d + 26),
+        25: (q ^ 1, d - 26),
+    }
+    return goals.get(d % RUN)
 
 
 def call(kernel, out_shape, flops, *operands):

time: 74.8 us -> 73.2 us (0.979)
  starting transfers between devices: 39.7 us -> 38.5 us
    ppermute x13, starting transfers between devices: 39.7 us -> 38.5 us  [route(): return lax.ppermute(block, ('section', 'dp'), pairs)]
  transfers between devices with their start and end apart: 13 -> 13, of which waited for: 7 -> 7; matrix products, arithmetic and copies ran while one was open for 0% -> 0% of each run, Pallas kernels for 8% -> 9%
where the time goes in v4:
time: 73.2 us; the launch traced here: 72.6 us
  starting transfers between devices  38.5 us (53%)
  waiting for transfers between devices  23.8 us (33%)
  Pallas kernels  8.22 us (11%)
  local copies, waits for them, and re-layouts  1.9 us (3%)
    ppermute x13, starting transfers between devices, route(): return lax.ppermute(block, ('section', 'dp'), pairs)  38.5 us
    ppermute x13, waiting for transfers between devices, route(): return lax.ppermute(block, ('section', 'dp'), pairs)  23.8 us
    pallas_call x15, Pallas kernels, call(): pl.pallas_call(kernel, out_shape=out_shape, in_specs=[pl.BlockSpec(memory...  7.88 us
    unnamed x4, local copies, waits for them, and re-layouts  1.9 us
  transfers between devices with their start and end apart: 13, of which 7 were waited for; matrix products, arithmetic and copies ran while one was open for 0% of the time, Pallas kernels for 9%

profile of v4, /device:TPU:1, one launch (start us, length us, event | category | flops | bytes accessed | tf_op | source)
XLA Modules:
  0.0 72.6 jit_solution(16130713616059385610)
XLA Ops:
  0.0 0.0 copy-start
  0.0 0.9 %copy-done = bf16[128,1024]{1,0:T(8,128)(2,1)S(1)} copy-done((bf16[128,1024]{1,0:T(8,128)(2,1)S(1)}, bf16[128,1024]{1,0:T(8,128)(2,1)}, u32[]{:S(2)}) %copy-start) | copy-done | bytes 262168
  1.0 0.0 copy-start.1
  1.0 0.9 %copy-done.1 = bf16[128,1024]{1,0:T(8,128)(2,1)S(1)} copy-done((bf16[128,1024]{1,0:T(8,128)(2,1)S(1)}, bf16[128,1024]{1,0:T(8,128)(2,1)}, u32[]{:S(2)}) %copy-start.1) | copy-done | bytes 262168
  1.9 0.3 shard_map.28
  2.2 8.8 %collective-permute-start = (bf16[256,1024]{1,0:T(8,128)(2,1)S(1)}, bf16[256,1024]{1,0:T(8,128)(2,1)S(1)}, u32[]{:S(2)}, u32[]{:S(2)}) collective-permute-start(bf16[256,1024]{1,0:T(8,128)(2,1)S(1)} %get-tuple-element.17.one.own.unit), channel_id=1, source_target_pairs={{0,128},{1,129},{2,130},{3,131},{4,132},{5,133},{6,134},{7,135},{8... | collective-permute-start | bytes 1572872 | tf_op jit(solution)/shard_map/ppermute | solution.py:41
  11.0 0.7 collective-permute-start.2
  11.7 12.6 %collective-permute-start.6 = (bf16[256,1024]{1,0:T(8,128)(2,1)S(1)}, bf16[256,1024]{1,0:T(8,128)(2,1)S(1)}, u32[]{:S(2)}, u32[]{:S(2)}) collective-permute-start(bf16[256,1024]{1,0:T(8,128)(2,1)S(1)} %get-tuple-element.17.one.own.unit), channel_id=1, source_target_pairs={{0,1},{1,2},{2,3},{3,4},{4,5},{5,6},{6,7},{7,8},{8,9},{9,10},{10,1... | collective-permute-start | bytes 1572872 | tf_op jit(solution)/shard_map/ppermute | solution.py:41
  24.4 1.5 %collective-permute-start.5 = (bf16[256,1024]{1,0:T(8,128)(2,1)S(1)}, bf16[256,1024]{1,0:T(8,128)(2,1)}, u32[]{:S(2)}, u32[]{:S(2)}) collective-permute-start(bf16[256,1024]{1,0:T(8,128)(2,1)S(1)} %get-tuple-element.17.one.own.unit), channel_id=1, source_target_pairs={{30,32},{62,64},{94,96},{126,0},{129,255},{161,159},{193,191},{225... | collective-permute-start | bytes 1572872 | tf_op jit(solution)/shard_map/ppermute | solution.py:41
  25.9 0.0 collective-permute-done.other
  25.9 1.3 %collective-permute-start.1 = (bf16[256,1024]{1,0:T(8,128)(2,1)S(1)}, bf16[256,1024]{1,0:T(8,128)(2,1)}, u32[]{:S(2)}, u32[]{:S(2)}) collective-permute-start(bf16[256,1024]{1,0:T(8,128)(2,1)S(1)} %collective-permute-done.other), channel_id=1, source_target_pairs={{0,1},{1,2},{2,3},{3,4},{4,5},{5,6},{6,7},{7,8},{8,9},{9,10},{10,1... | collective-permute-start | bytes 1572872 | tf_op jit(solution)/shard_map/ppermute | solution.py:41
  27.1 0.0 collective-permute-done.2.block
  27.2 0.8 %shard_map.30 = bf16[256,1024]{1,0:T(8,128)(2,1)} custom-call(bf16[256,1024]{1,0:T(8,128)(2,1)S(1)} %collective-permute-done.2.block), custom_call_target="tpu_custom_call" | custom-call | flops 400000000 | bytes 524288 | tf_op jit(solution)/shard_map/pallas_call | solution.py:91
  28.0 1.3 %collective-permute-start.3 = (bf16[256,1024]{1,0:T(8,128)(2,1)}, bf16[256,1024]{1,0:T(8,128)(2,1)S(1)}, u32[]{:S(2)}, u32[]{:S(2)}) collective-permute-start(bf16[256,1024]{1,0:T(8,128)(2,1)} %shard_map.30), channel_id=1, source_target_pairs={{134,160},{135,32},{152,255},{153,127},{166,192},{167,64},{184,159... | collective-permute-start | bytes 1572872 | tf_op jit(solution)/shard_map/ppermute | solution.py:41
  29.3 1.9 %collective-permute-start.7 = (bf16[256,1024]{1,0:T(8,128)(2,1)S(1)}, bf16[256,1024]{1,0:T(8,128)(2,1)S(1)}, u32[]{:S(2)}, u32[]{:S(2)}) collective-permute-start(bf16[256,1024]{1,0:T(8,128)(2,1)S(1)} %get-tuple-element.17.one.own.unit), channel_id=1, source_target_pairs={{0,256},{1,257},{2,258},{3,259},{4,260},{5,261},{6,262},{7,263},{8... | collective-permute-start | bytes 1572872 | tf_op jit(solution)/shard_map/ppermute | solution.py:41
  31.2 5.4 %collective-permute-done.6.block = bf16[256,1024]{1,0:T(8,128)(2,1)S(1)} collective-permute-done((bf16[256,1024]{1,0:T(8,128)(2,1)S(1)}, bf16[256,1024]{1,0:T(8,128)(2,1)S(1)}, u32[]{:S(2)}, u32[]{:S(2)}) %collective-permute-start.6) | collective-permute-done | bytes 524320 | tf_op jit(solution)/shard_map/ppermute | solution.py:41
  36.7 1.3 %collective-permute-start.8 = (bf16[256,1024]{1,0:T(8,128)(2,1)S(1)}, bf16[256,1024]{1,0:T(8,128)(2,1)S(1)}, u32[]{:S(2)}, u32[]{:S(2)}) collective-permute-start(bf16[256,1024]{1,0:T(8,128)(2,1)S(1)} %shard_map.34.one_a), channel_id=1, source_target_pairs={{0,1},{1,2},{2,3},{3,4},{4,5},{5,6},{6,7},{7,8},{8,9},{9,10},{10,1... | collective-permute-start | bytes 1572872 | tf_op jit(solution)/shard_map/ppermute | solution.py:41
  38.0 0.0 collective-permute-done.5.block
  38.0 1.1 %shard_map.32.direct = bf16[256,1024]{1,0:T(8,128)(2,1)S(1)} custom-call(bf16[256,1024]{1,0:T(8,128)(2,1)} %collective-permute-done.5.block), custom_call_target="tpu_custom_call" | custom-call | flops 400000000 | bytes 524288 | tf_op jit(solution)/shard_map/pallas_call | solution.py:91
  39.1 0.5 collective-permute-done.1.block
  39.6 1.1 %shard_map.29.one_b = bf16[256,1024]{1,0:T(8,128)(2,1)S(1)} custom-call(bf16[256,1024]{1,0:T(8,128)(2,1)} %collective-permute-done.1.block), custom_call_target="tpu_custom_call" | custom-call | flops 1600000000 | bytes 524288 | tf_op jit(solution)/shard_map/pallas_call | solution.py:91
  40.7 7.1 %collective-permute-done.3.near_b = bf16[256,1024]{1,0:T(8,128)(2,1)S(1)} collective-permute-done((bf16[256,1024]{1,0:T(8,128)(2,1)}, bf16[256,1024]{1,0:T(8,128)(2,1)S(1)}, u32[]{:S(2)}, u32[]{:S(2)}) %collective-permute-start.3) | collective-permute-done | bytes 524320 | tf_op jit(solution)/shard_map/ppermute | solution.py:41
  47.8 0.1 shard_map.31.one_b
  47.9 1.3 %collective-permute-start.4 = (bf16[256,1024]{1,0:T(8,128)(2,1)S(1)}, bf16[256,1024]{1,0:T(8,128)(2,1)S(1)}, u32[]{:S(2)}, u32[]{:S(2)}) collective-permute-start(bf16[256,1024]{1,0:T(8,128)(2,1)S(1)} %shard_map.31.one_b), channel_id=1, source_target_pairs={{0,1},{1,2},{2,3},{3,4},{4,5},{5,6},{6,7},{7,8},{8,9},{9,10},{10,1... | collective-permute-start | bytes 1572872 | tf_op jit(solution)/shard_map/ppermute | solution.py:41
  49.2 0.0 collective-permute-done.7.block
  49.2 0.1 shard_map.33.extra
  49.4 1.9 %collective-permute-start.9 = (bf16[256,1024]{1,0:T(8,128)(2,1)S(1)}, bf16[256,1024]{1,0:T(8,128)(2,1)S(1)}, u32[]{:S(2)}, u32[]{:S(2)}) collective-permute-start(bf16[256,1024]{1,0:T(8,128)(2,1)S(1)} %shard_map.35.one), channel_id=1, source_target_pairs={{0,128},{1,129},{2,130},{3,131},{4,132},{5,133},{6,134},{7,135},{8... | collective-permute-start | bytes 1572872 | tf_op jit(solution)/shard_map/ppermute | solution.py:41
  51.3 0.0 collective-permute-done.8.block
  51.4 1.8 %collective-permute-done.9.other = bf16[256,1024]{1,0:T(8,128)(2,1)S(1)} collective-permute-done((bf16[256,1024]{1,0:T(8,128)(2,1)S(1)}, bf16[256,1024]{1,0:T(8,128)(2,1)S(1)}, u32[]{:S(2)}, u32[]{:S(2)}) %collective-permute-start.9) | collective-permute-done | bytes 524320 | tf_op jit(solution)/shard_map/ppermute | solution.py:41
  53.2 1.1 %shard_map.39.old_ref = f32[256,1024]{1,0:T(8,128)S(1)} custom-call(bf16[256,1024]{1,0:T(8,128)(2,1)S(1)} %shard_map.35.one, bf16[256,1024]{1,0:T(8,128)(2,1)S(1)} %collective-permute-done.9.other, bf16[256,1024]{1,0:T(8,128)(2,1)S(1)} %get-tuple-element.17.one.own.unit, bf16[256,1024]{1,0:T(8,128)(2,1)S(1)} %shard_map.34.one_a, ...), custom_call_target="tpu_custom_call" | custom-call | flops 6400000000 | bytes 3145728 | tf_op jit(solution)/shard_map/pallas_call | solution.py:91
  54.3 3.5 %collective-permute-done.4.two = bf16[256,1024]{1,0:T(8,128)(2,1)S(1)} collective-permute-done((bf16[256,1024]{1,0:T(8,128)(2,1)S(1)}, bf16[256,1024]{1,0:T(8,128)(2,1)S(1)}, u32[]{:S(2)}, u32[]{:S(2)}) %collective-permute-start.4) | collective-permute-done | bytes 524320 | tf_op jit(solution)/shard_map/ppermute | solution.py:41
  57.8 0.7 shard_map.40
  58.5 1.9 %collective-permute-start.10 = (bf16[128,1024]{1,0:T(8,128)(2,1)S(1)}, bf16[128,1024]{1,0:T(8,128)(2,1)S(1)}, u32[]{:S(2)}, u32[]{:S(2)}) collective-permute-start(bf16[128,1024]{1,0:T(8,128)(2,1)S(1)} %get-tuple-element.23), channel_id=1, source_target_pairs={{0,128},{1,129},{2,130},{3,131},{4,132},{5,133},{6,134},{7,135},{8... | collective-permute-start | bytes 786440 | tf_op jit(solution)/shard_map/ppermute | solution.py:41
  60.4 1.1 %shard_map.37.old_ref = f32[256,1024]{1,0:T(8,128)S(1)} custom-call(bf16[256,1024]{1,0:T(8,128)(2,1)S(1)} %get-tuple-element.17.one.own.unit, bf16[256,1024]{1,0:T(8,128)(2,1)S(1)} %collective-permute-done.other, bf16[256,1024]{1,0:T(8,128)(2,1)S(1)} %get-tuple-element.17.one.own.unit, bf16[256,1024]{1,0:T(8,128)(2,1)S(1)} %shard_map.34.one_a, ...), custom_call_target="tpu_custom_call" | custom-call | flops 400000000 | bytes 3145728 | tf_op jit(solution)/shard_map/pallas_call | solution.py:91
  61.5 0.4 collective-permute-done.10.got
  62.0 1.9 %collective-permute-start.12 = (bf16[128,1024]{1,0:T(8,128)(2,1)S(1)}, bf16[128,1024]{1,0:T(8,128)(2,1)S(1)}, u32[]{:S(2)}, u32[]{:S(2)}) collective-permute-start(bf16[128,1024]{1,0:T(8,128)(2,1)S(1)} %shard_map.41), channel_id=1, source_target_pairs={{0,256},{1,257},{2,258},{3,259},{4,260},{5,261},{6,262},{7,263},{8... | collective-permute-start | bytes 786440 | tf_op jit(solution)/shard_map/ppermute | solution.py:41
  63.9 0.7 shard_map.38
  64.6 2.0 %collective-permute-start.11 = (bf16[128,1024]{1,0:T(8,128)(2,1)S(1)}, bf16[128,1024]{1,0:T(8,128)(2,1)S(1)}, u32[]{:S(2)}, u32[]{:S(2)}) collective-permute-start(bf16[128,1024]{1,0:T(8,128)(2,1)S(1)} %get-tuple-element.24), channel_id=1, source_target_pairs={{0,128},{1,129},{2,130},{3,131},{4,132},{5,133},{6,134},{7,135},{8... | collective-permute-start | bytes 786440 | tf_op jit(solution)/shard_map/ppermute | solution.py:41
  66.7 5.0 %collective-permute-done.12.block = bf16[128,1024]{1,0:T(8,128)(2,1)S(1)} collective-permute-done((bf16[128,1024]{1,0:T(8,128)(2,1)S(1)}, bf16[128,1024]{1,0:T(8,128)(2,1)S(1)}, u32[]{:S(2)}, u32[]{:S(2)}) %collective-permute-start.12) | collective-permute-done | bytes 262176 | tf_op jit(solution)/shard_map/ppermute | solution.py:41
  71.7 0.0 collective-permute-done.11.got
  71.7 1.0 %shard_map.43 = bf16[128,1024]{1,0:T(8,128)(2,1)} custom-call(bf16[256,1024]{1,0:T(8,128)(2,1)S(1)} %get-tuple-element.17.one.own.unit, f32[128,1]{1,0:T(8,128)S(1)} %get-tuple-element.16.inv, f32[128,1024]{1,0:T(8,128)S(1)} %get-tuple-element.19.keep, bf16[128,1024]{1,0:T(8,128)(2,1)S(1)} %collective-permute-done.11.got, ...), custom_call_target="tpu_custom_call" | custom-call | flops 1048576 | bytes 1573376 | tf_op jit(solution)/shard_map/pallas_call | solution.py:91
  (5 shorter events, 0.2 us)
Async XLA Ops:
  0.0 0.9 %copy-start = (bf16[128,1024]{1,0:T(8,128)(2,1)S(1)}, bf16[128,1024]{1,0:T(8,128)(2,1)}, u32[]{:S(2)}) copy-start(bf16[128,1024]{1,0:T(8,128)(2,1)} %s_hbm.1) | copy-start | bytes 786436
  1.0 0.9 %copy-start.1 = (bf16[128,1024]{1,0:T(8,128)(2,1)S(1)}, bf16[128,1024]{1,0:T(8,128)(2,1)}, u32[]{:S(2)}) copy-start(bf16[128,1024]{1,0:T(8,128)(2,1)} %t_hbm.1) | copy-start | bytes 786436
  2.2 23.6 %collective-permute-start = (bf16[256,1024]{1,0:T(8,128)(2,1)S(1)}, bf16[256,1024]{1,0:T(8,128)(2,1)S(1)}, u32[]{:S(2)}, u32[]{:S(2)}) collective-permute-start(bf16[256,1024]{1,0:T(8,128)(2,1)S(1)} %get-tuple-element.17.one.own.unit), channel_id=1, source_target_pairs={{0,128},{1,129},{2,130},{3,131},{4,132},{5,133},{6,134},{7,135},{8... | collective-permute-start | bytes 1572872 | tf_op jit(solution)/shard_map/ppermute | solution.py:41
  11.0 16.1 %collective-permute-start.2 = (bf16[256,1024]{1,0:T(8,128)(2,1)S(1)}, bf16[256,1024]{1,0:T(8,128)(2,1)S(1)}, u32[]{:S(2)}, u32[]{:S(2)}) collective-permute-start(bf16[256,1024]{1,0:T(8,128)(2,1)S(1)} %get-tuple-element.17.one.own.unit), channel_id=1, source_target_pairs={{0,152},{1,153},{32,184},{33,185},{64,216},{65,217},{96,248},{97,2... | collective-permute-start | bytes 1572872 | tf_op jit(solution)/shard_map/ppermute | solution.py:41
  11.7 24.9 %collective-permute-start.6 = (bf16[256,1024]{1,0:T(8,128)(2,1)S(1)}, bf16[256,1024]{1,0:T(8,128)(2,1)S(1)}, u32[]{:S(2)}, u32[]{:S(2)}) collective-permute-start(bf16[256,1024]{1,0:T(8,128)(2,1)S(1)} %get-tuple-element.17.one.own.unit), channel_id=1, source_target_pairs={{0,1},{1,2},{2,3},{3,4},{4,5},{5,6},{6,7},{7,8},{8,9},{9,10},{10,1... | collective-permute-start | bytes 1572872 | tf_op jit(solution)/shard_map/ppermute | solution.py:41
  24.4 13.7 %collective-permute-start.5 = (bf16[256,1024]{1,0:T(8,128)(2,1)S(1)}, bf16[256,1024]{1,0:T(8,128)(2,1)}, u32[]{:S(2)}, u32[]{:S(2)}) collective-permute-start(bf16[256,1024]{1,0:T(8,128)(2,1)S(1)} %get-tuple-element.17.one.own.unit), channel_id=1, source_target_pairs={{30,32},{62,64},{94,96},{126,0},{129,255},{161,159},{193,191},{225... | collective-permute-start | bytes 1572872 | tf_op jit(solution)/shard_map/ppermute | solution.py:41
  25.9 13.7 %collective-permute-start.1 = (bf16[256,1024]{1,0:T(8,128)(2,1)S(1)}, bf16[256,1024]{1,0:T(8,128)(2,1)}, u32[]{:S(2)}, u32[]{:S(2)}) collective-permute-start(bf16[256,1024]{1,0:T(8,128)(2,1)S(1)} %collective-permute-done.other), channel_id=1, source_target_pairs={{0,1},{1,2},{2,3},{3,4},{4,5},{5,6},{6,7},{7,8},{8,9},{9,10},{10,1... | collective-permute-start | bytes 1572872 | tf_op jit(solution)/shard_map/ppermute | solution.py:41
  28.0 19.8 %collective-permute-start.3 = (bf16[256,1024]{1,0:T(8,128)(2,1)}, bf16[256,1024]{1,0:T(8,128)(2,1)S(1)}, u32[]{:S(2)}, u32[]{:S(2)}) collective-permute-start(bf16[256,1024]{1,0:T(8,128)(2,1)} %shard_map.30), channel_id=1, source_target_pairs={{134,160},{135,32},{152,255},{153,127},{166,192},{167,64},{184,159... | collective-permute-start | bytes 1572872 | tf_op jit(solution)/shard_map/ppermute | solution.py:41
  29.3 19.9 %collective-permute-start.7 = (bf16[256,1024]{1,0:T(8,128)(2,1)S(1)}, bf16[256,1024]{1,0:T(8,128)(2,1)S(1)}, u32[]{:S(2)}, u32[]{:S(2)}) collective-permute-start(bf16[256,1024]{1,0:T(8,128)(2,1)S(1)} %get-tuple-element.17.one.own.unit), channel_id=1, source_target_pairs={{0,256},{1,257},{2,258},{3,259},{4,260},{5,261},{6,262},{7,263},{8... | collective-permute-start | bytes 1572872 | tf_op jit(solution)/shard_map/ppermute | solution.py:41
  36.7 14.6 %collective-permute-start.8 = (bf16[256,1024]{1,0:T(8,128)(2,1)S(1)}, bf16[256,1024]{1,0:T(8,128)(2,1)S(1)}, u32[]{:S(2)}, u32[]{:S(2)}) collective-permute-start(bf16[256,1024]{1,0:T(8,128)(2,1)S(1)} %shard_map.34.one_a), channel_id=1, source_target_pairs={{0,1},{1,2},{2,3},{3,4},{4,5},{5,6},{6,7},{7,8},{8,9},{9,10},{10,1... | collective-permute-start | bytes 1572872 | tf_op jit(solution)/shard_map/ppermute | solution.py:41
  47.9 9.9 %collective-permute-start.4 = (bf16[256,1024]{1,0:T(8,128)(2,1)S(1)}, bf16[256,1024]{1,0:T(8,128)(2,1)S(1)}, u32[]{:S(2)}, u32[]{:S(2)}) collective-permute-start(bf16[256,1024]{1,0:T(8,128)(2,1)S(1)} %shard_map.31.one_b), channel_id=1, source_target_pairs={{0,1},{1,2},{2,3},{3,4},{4,5},{5,6},{6,7},{7,8},{8,9},{9,10},{10,1... | collective-permute-start | bytes 1572872 | tf_op jit(solution)/shard_map/ppermute | solution.py:41
  49.4 3.8 %collective-permute-start.9 = (bf16[256,1024]{1,0:T(8,128)(2,1)S(1)}, bf16[256,1024]{1,0:T(8,128)(2,1)S(1)}, u32[]{:S(2)}, u32[]{:S(2)}) collective-permute-start(bf16[256,1024]{1,0:T(8,128)(2,1)S(1)} %shard_map.35.one), channel_id=1, source_target_pairs={{0,128},{1,129},{2,130},{3,131},{4,132},{5,133},{6,134},{7,135},{8... | collective-permute-start | bytes 1572872 | tf_op jit(solution)/shard_map/ppermute | solution.py:41
  58.5 3.4 %collective-permute-start.10 = (bf16[128,1024]{1,0:T(8,128)(2,1)S(1)}, bf16[128,1024]{1,0:T(8,128)(2,1)S(1)}, u32[]{:S(2)}, u32[]{:S(2)}) collective-permute-start(bf16[128,1024]{1,0:T(8,128)(2,1)S(1)} %get-tuple-element.23), channel_id=1, source_target_pairs={{0,128},{1,129},{2,130},{3,131},{4,132},{5,133},{6,134},{7,135},{8... | collective-permute-start | bytes 786440 | tf_op jit(solution)/shard_map/ppermute | solution.py:41
  62.0 9.7 %collective-permute-start.12 = (bf16[128,1024]{1,0:T(8,128)(2,1)S(1)}, bf16[128,1024]{1,0:T(8,128)(2,1)S(1)}, u32[]{:S(2)}, u32[]{:S(2)}) collective-permute-start(bf16[128,1024]{1,0:T(8,128)(2,1)S(1)} %shard_map.41), channel_id=1, source_target_pairs={{0,256},{1,257},{2,258},{3,259},{4,260},{5,261},{6,262},{7,263},{8... | collective-permute-start | bytes 786440 | tf_op jit(solution)/shard_map/ppermute | solution.py:41
  64.6 7.1 %collective-permute-start.11 = (bf16[128,1024]{1,0:T(8,128)(2,1)S(1)}, bf16[128,1024]{1,0:T(8,128)(2,1)S(1)}, u32[]{:S(2)}, u32[]{:S(2)}) collective-permute-start(bf16[128,1024]{1,0:T(8,128)(2,1)S(1)} %get-tuple-element.24), channel_id=1, source_target_pairs={{0,128},{1,129},{2,130},{3,131},{4,132},{5,133},{6,134},{7,135},{8... | collective-permute-start | bytes 786440 | tf_op jit(solution)/shard_map/ppermute | solution.py:41

commit v5 on v4

--- a/solution.py
+++ b/solution.py
@@ -12,21 +12,17 @@
 RUN = 32
 F32 = jnp.float32
 BF16 = jnp.bfloat16
-C1 = 400000000
-C2 = 400000000
-C3 = 1
-C4 = 400000000
-C5 = 6400000000
-C6 = 100000000
-C7 = 800000000
-C9 = 400000000
-C10 = 200000000
-C15 = 1600000000
-C14 = 6400000000
-C13 = 400000000
-C12 = 200000000
-C11 = 400000000
-C8 = 400000000
+NEXT_COST = 400_000_000
+FINAL_COST = 400_000_000
+TWO_A_COST = 6_400_000_000
+FAR_COST = 100_000_000
+EXTRA_COST = 800_000_000
+ONE_A_COST = 400_000_000
+TAIL_COST = 200_000_000
+AWAY_COST = 6_400_000_000
+SPREAD_COST = 400_000_000
+DIRECT_COST = 400_000_000
+NEAR_COST = 400_000_000
 VMEM = pl.BlockSpec(memory_space=pltpu.VMEM)
 ROW_BY_ROW = (((1,), (1,)), ((), ()))
 
@@ -186,29 +182,29 @@
     half, both = shape((2 * ROWS, D), F32), shape((2 * ROWS, D), BF16)
     gram = 2 * 3 * 2 * ROWS * ROWS * D
     own, inv = unit_rows(student, teacher)
-    one_a = hold(route(own, along), C9)
-    spread = hold(route(own, aside), C13)
-    direct = hold(route(own, across), C11)
-    far = hold(route(after(own, spread), to_y), C6)
+    one_a = hold(route(own, along), ONE_A_COST)
+    spread = hold(route(own, aside), SPREAD_COST)
+    direct = hold(route(own, across), DIRECT_COST)
+    far = hold(route(after(own, spread), to_y), FAR_COST)
     sib = route(own, to_core)
-    one_b = hold(route(sib, along_inside), C15)
+    one_b = route(sib, along_inside)
     near_b = route(spread, from_aside)
     core = lax.axis_index("section") % 2
     place = lax.axis_index("dp") % RUN
     flag = (place == core * (RUN - 1)).astype(jnp.int32).reshape(1)
-    one_b = call(next_kernel, both, C1, flag, one_b, near_b)
-    extra = call(extra_kernel, both, C7, flag, near_b, direct)
-    two_a = hold(route(one_a, along_inside), C5)
+    one_b = call(next_kernel, both, NEXT_COST, flag, one_b, near_b)
+    extra = call(extra_kernel, both, EXTRA_COST, flag, near_b, direct)
+    two_a = hold(route(one_a, along_inside), TWO_A_COST)
     two_b = route(one_b, along_inside)
-    near_sum = call(first_kernel, half, C8, own, sib, own, one_a, after(one_b, far), two_a)
+    near_sum = call(first_kernel, half, NEAR_COST, own, sib, own, one_a, after(one_b, far), two_a)
     cross = route(after(far, one_b, extra), to_core)
-    away_sum = call(first_kernel, half, C14, far, cross, own, one_a, one_b, two_a)
+    away_sum = call(first_kernel, half, AWAY_COST, far, cross, own, one_a, one_b, two_a)
     keep_far, send_far = call(
-        final_kernel, (quarter_f, quarter_h), C4, far, cross, two_b, extra, away_sum
+        final_kernel, (quarter_f, quarter_h), FINAL_COST, far, cross, two_b, extra, away_sum
     )
     got_far = route(send_far, to_core)
     send_far = call(far_kernel, quarter_h, ROWS * D, keep_far, got_far)
-    got_far = hold(route(send_far, to_y), C10)
+    got_far = hold(route(send_far, to_y), TAIL_COST)
     keep, send = call(final_kernel, (quarter_f, quarter_h), gram, own, sib, two_b, extra, near_sum)
     got = route(after(send, send_far), to_core)
     return call(last_kernel, quarter_h, 8 * ROWS * D, own, inv, keep, got, got_far)

time: 73.2 us -> 73.1 us (level)
    pallas_call x15 -> x14, Pallas kernels: 7.88 us -> 7.78 us  [call(): pl.pallas_call(kernel, out_shape=out_shape, in_specs=[pl.BlockSpec(memory...]
  transfers between devices with their start and end apart: 13 -> 13, of which waited for: 7 -> 7; matrix products, arithmetic and copies ran while one was open for 0% -> 0% of each run, Pallas kernels for 9% -> 8%
where the time goes in v5:
time: 73.1 us; the launch traced here: 72.6 us
  starting transfers between devices  38.4 us (53%)
  waiting for transfers between devices  23.9 us (33%)
  Pallas kernels  8.11 us (11%)
  local copies, waits for them, and re-layouts  1.9 us (3%)
    ppermute x13, starting transfers between devices, route(): return lax.ppermute(block, ('section', 'dp'), pairs)  38.4 us
    ppermute x13, waiting for transfers between devices, route(): return lax.ppermute(block, ('section', 'dp'), pairs)  23.9 us
    pallas_call x14, Pallas kernels, call(): pl.pallas_call(kernel, out_shape=out_shape, in_specs=[pl.BlockSpec(memory...  7.78 us
    unnamed x4, local copies, waits for them, and re-layouts  1.9 us
  transfers between devices with their start and end apart: 13, of which 7 were waited for; matrix products, arithmetic and copies ran while one was open for 0% of the time, Pallas kernels for 8%

profile of v5, /device:TPU:1, one launch (start us, length us, event | category | flops | bytes accessed | tf_op | source)
XLA Modules:
  0.0 72.6 jit_solution(9620916146024804901)
XLA Ops:
  0.0 0.0 copy-start
  0.0 0.9 %copy-done = bf16[128,1024]{1,0:T(8,128)(2,1)S(1)} copy-done((bf16[128,1024]{1,0:T(8,128)(2,1)S(1)}, bf16[128,1024]{1,0:T(8,128)(2,1)}, u32[]{:S(2)}) %copy-start) | copy-done | bytes 262168
  1.0 0.0 copy-start.1
  1.0 0.9 %copy-done.1 = bf16[128,1024]{1,0:T(8,128)(2,1)S(1)} copy-done((bf16[128,1024]{1,0:T(8,128)(2,1)S(1)}, bf16[128,1024]{1,0:T(8,128)(2,1)}, u32[]{:S(2)}) %copy-start.1) | copy-done | bytes 262168
  1.9 0.3 shard_map.28
  2.2 8.8 %collective-permute-start = (bf16[256,1024]{1,0:T(8,128)(2,1)S(1)}, bf16[256,1024]{1,0:T(8,128)(2,1)S(1)}, u32[]{:S(2)}, u32[]{:S(2)}) collective-permute-start(bf16[256,1024]{1,0:T(8,128)(2,1)S(1)} %get-tuple-element.17.one.own.unit), channel_id=1, source_target_pairs={{0,128},{1,129},{2,130},{3,131},{4,132},{5,133},{6,134},{7,135},{8... | collective-permute-start | bytes 1572872 | tf_op jit(solution)/shard_map/ppermute | solution.py:37
  11.0 0.7 collective-permute-start.2
  11.7 12.6 %collective-permute-start.6 = (bf16[256,1024]{1,0:T(8,128)(2,1)S(1)}, bf16[256,1024]{1,0:T(8,128)(2,1)S(1)}, u32[]{:S(2)}, u32[]{:S(2)}) collective-permute-start(bf16[256,1024]{1,0:T(8,128)(2,1)S(1)} %get-tuple-element.17.one.own.unit), channel_id=1, source_target_pairs={{0,1},{1,2},{2,3},{3,4},{4,5},{5,6},{6,7},{7,8},{8,9},{9,10},{10,1... | collective-permute-start | bytes 1572872 | tf_op jit(solution)/shard_map/ppermute | solution.py:37
  24.4 1.5 %collective-permute-start.5 = (bf16[256,1024]{1,0:T(8,128)(2,1)S(1)}, bf16[256,1024]{1,0:T(8,128)(2,1)}, u32[]{:S(2)}, u32[]{:S(2)}) collective-permute-start(bf16[256,1024]{1,0:T(8,128)(2,1)S(1)} %get-tuple-element.17.one.own.unit), channel_id=1, source_target_pairs={{30,32},{62,64},{94,96},{126,0},{129,255},{161,159},{193,191},{225... | collective-permute-start | bytes 1572872 | tf_op jit(solution)/shard_map/ppermute | solution.py:37
  25.8 0.0 collective-permute-done.other
  25.8 1.3 %collective-permute-start.1 = (bf16[256,1024]{1,0:T(8,128)(2,1)S(1)}, bf16[256,1024]{1,0:T(8,128)(2,1)S(1)}, u32[]{:S(2)}, u32[]{:S(2)}) collective-permute-start(bf16[256,1024]{1,0:T(8,128)(2,1)S(1)} %collective-permute-done.other), channel_id=1, source_target_pairs={{0,1},{1,2},{2,3},{3,4},{4,5},{5,6},{6,7},{7,8},{8,9},{9,10},{10,1... | collective-permute-start | bytes 1572872 | tf_op jit(solution)/shard_map/ppermute | solution.py:37
  27.1 0.0 collective-permute-done.2.block
  27.1 0.8 %shard_map.29 = bf16[256,1024]{1,0:T(8,128)(2,1)} custom-call(bf16[256,1024]{1,0:T(8,128)(2,1)S(1)} %collective-permute-done.2.block), custom_call_target="tpu_custom_call" | custom-call | flops 400000000 | bytes 524288 | tf_op jit(solution)/shard_map/pallas_call | solution.py:87
  28.0 1.3 %collective-permute-start.3 = (bf16[256,1024]{1,0:T(8,128)(2,1)}, bf16[256,1024]{1,0:T(8,128)(2,1)S(1)}, u32[]{:S(2)}, u32[]{:S(2)}) collective-permute-start(bf16[256,1024]{1,0:T(8,128)(2,1)} %shard_map.29), channel_id=1, source_target_pairs={{134,160},{135,32},{152,255},{153,127},{166,192},{167,64},{184,159... | collective-permute-start | bytes 1572872 | tf_op jit(solution)/shard_map/ppermute | solution.py:37
  29.3 1.9 %collective-permute-start.7 = (bf16[256,1024]{1,0:T(8,128)(2,1)S(1)}, bf16[256,1024]{1,0:T(8,128)(2,1)S(1)}, u32[]{:S(2)}, u32[]{:S(2)}) collective-permute-start(bf16[256,1024]{1,0:T(8,128)(2,1)S(1)} %get-tuple-element.17.one.own.unit), channel_id=1, source_target_pairs={{0,256},{1,257},{2,258},{3,259},{4,260},{5,261},{6,262},{7,263},{8... | collective-permute-start | bytes 1572872 | tf_op jit(solution)/shard_map/ppermute | solution.py:37
  31.2 5.4 %collective-permute-done.6.block = bf16[256,1024]{1,0:T(8,128)(2,1)S(1)} collective-permute-done((bf16[256,1024]{1,0:T(8,128)(2,1)S(1)}, bf16[256,1024]{1,0:T(8,128)(2,1)S(1)}, u32[]{:S(2)}, u32[]{:S(2)}) %collective-permute-start.6) | collective-permute-done | bytes 524320 | tf_op jit(solution)/shard_map/ppermute | solution.py:37
  36.7 1.3 %collective-permute-start.8 = (bf16[256,1024]{1,0:T(8,128)(2,1)S(1)}, bf16[256,1024]{1,0:T(8,128)(2,1)}, u32[]{:S(2)}, u32[]{:S(2)}) collective-permute-start(bf16[256,1024]{1,0:T(8,128)(2,1)S(1)} %shard_map.33.one_a), channel_id=1, source_target_pairs={{0,1},{1,2},{2,3},{3,4},{4,5},{5,6},{6,7},{7,8},{8,9},{9,10},{10,1... | collective-permute-start | bytes 1572872 | tf_op jit(solution)/shard_map/ppermute | solution.py:37
  38.0 0.0 collective-permute-done.5.block
  38.0 1.1 %shard_map.31.direct = bf16[256,1024]{1,0:T(8,128)(2,1)S(1)} custom-call(bf16[256,1024]{1,0:T(8,128)(2,1)} %collective-permute-done.5.block), custom_call_target="tpu_custom_call" | custom-call | flops 400000000 | bytes 524288 | tf_op jit(solution)/shard_map/pallas_call | solution.py:87
  39.1 0.5 collective-permute-done.1.one_b
  39.6 8.2 %collective-permute-done.3.near_b = bf16[256,1024]{1,0:T(8,128)(2,1)S(1)} collective-permute-done((bf16[256,1024]{1,0:T(8,128)(2,1)}, bf16[256,1024]{1,0:T(8,128)(2,1)S(1)}, u32[]{:S(2)}, u32[]{:S(2)}) %collective-permute-start.3) | collective-permute-done | bytes 524320 | tf_op jit(solution)/shard_map/ppermute | solution.py:37
  47.8 0.1 shard_map.30.one_b
  47.9 1.3 %collective-permute-start.4 = (bf16[256,1024]{1,0:T(8,128)(2,1)S(1)}, bf16[256,1024]{1,0:T(8,128)(2,1)S(1)}, u32[]{:S(2)}, u32[]{:S(2)}) collective-permute-start(bf16[256,1024]{1,0:T(8,128)(2,1)S(1)} %shard_map.30.one_b), channel_id=1, source_target_pairs={{0,1},{1,2},{2,3},{3,4},{4,5},{5,6},{6,7},{7,8},{8,9},{9,10},{10,1... | collective-permute-start | bytes 1572872 | tf_op jit(solution)/shard_map/ppermute | solution.py:37
  49.2 0.0 collective-permute-done.7.block
  49.2 0.1 shard_map.32.extra
  49.3 1.9 %collective-permute-start.9 = (bf16[256,1024]{1,0:T(8,128)(2,1)S(1)}, bf16[256,1024]{1,0:T(8,128)(2,1)S(1)}, u32[]{:S(2)}, u32[]{:S(2)}) collective-permute-start(bf16[256,1024]{1,0:T(8,128)(2,1)S(1)} %shard_map.34.one), channel_id=1, source_target_pairs={{0,128},{1,129},{2,130},{3,131},{4,132},{5,133},{6,134},{7,135},{8... | collective-permute-start | bytes 1572872 | tf_op jit(solution)/shard_map/ppermute | solution.py:37
  51.2 0.0 collective-permute-done.8.block
  51.2 1.1 %shard_map.35.two_a = bf16[256,1024]{1,0:T(8,128)(2,1)S(1)} custom-call(bf16[256,1024]{1,0:T(8,128)(2,1)} %collective-permute-done.8.block), custom_call_target="tpu_custom_call" | custom-call | flops 6400000000 | bytes 524288 | tf_op jit(solution)/shard_map/pallas_call | solution.py:87
  52.3 0.8 %collective-permute-done.9.other = bf16[256,1024]{1,0:T(8,128)(2,1)S(1)} collective-permute-done((bf16[256,1024]{1,0:T(8,128)(2,1)S(1)}, bf16[256,1024]{1,0:T(8,128)(2,1)S(1)}, u32[]{:S(2)}, u32[]{:S(2)}) %collective-permute-start.9) | collective-permute-done | bytes 524320 | tf_op jit(solution)/shard_map/ppermute | solution.py:37
  53.1 1.1 %shard_map.38.old_ref = f32[256,1024]{1,0:T(8,128)S(1)} custom-call(bf16[256,1024]{1,0:T(8,128)(2,1)S(1)} %shard_map.34.one, bf16[256,1024]{1,0:T(8,128)(2,1)S(1)} %collective-permute-done.9.other, bf16[256,1024]{1,0:T(8,128)(2,1)S(1)} %get-tuple-element.17.one.own.unit, bf16[256,1024]{1,0:T(8,128)(2,1)S(1)} %shard_map.33.one_a, ...), custom_call_target="tpu_custom_call" | custom-call | flops 6400000000 | bytes 3145728 | tf_op jit(solution)/shard_map/pallas_call | solution.py:87
  54.2 3.6 %collective-permute-done.4.two = bf16[256,1024]{1,0:T(8,128)(2,1)S(1)} collective-permute-done((bf16[256,1024]{1,0:T(8,128)(2,1)S(1)}, bf16[256,1024]{1,0:T(8,128)(2,1)S(1)}, u32[]{:S(2)}, u32[]{:S(2)}) %collective-permute-start.4) | collective-permute-done | bytes 524320 | tf_op jit(solution)/shard_map/ppermute | solution.py:37
  57.8 0.7 shard_map.39
  58.5 1.9 %collective-permute-start.10 = (bf16[128,1024]{1,0:T(8,128)(2,1)S(1)}, bf16[128,1024]{1,0:T(8,128)(2,1)S(1)}, u32[]{:S(2)}, u32[]{:S(2)}) collective-permute-start(bf16[128,1024]{1,0:T(8,128)(2,1)S(1)} %get-tuple-element.23), channel_id=1, source_target_pairs={{0,128},{1,129},{2,130},{3,131},{4,132},{5,133},{6,134},{7,135},{8... | collective-permute-start | bytes 786440 | tf_op jit(solution)/shard_map/ppermute | solution.py:37
  60.4 1.1 %shard_map.36.old_ref = f32[256,1024]{1,0:T(8,128)S(1)} custom-call(bf16[256,1024]{1,0:T(8,128)(2,1)S(1)} %get-tuple-element.17.one.own.unit, bf16[256,1024]{1,0:T(8,128)(2,1)S(1)} %collective-permute-done.other, bf16[256,1024]{1,0:T(8,128)(2,1)S(1)} %get-tuple-element.17.one.own.unit, bf16[256,1024]{1,0:T(8,128)(2,1)S(1)} %shard_map.33.one_a, ...), custom_call_target="tpu_custom_call" | custom-call | flops 400000000 | bytes 3145728 | tf_op jit(solution)/shard_map/pallas_call | solution.py:87
  61.5 0.4 collective-permute-done.10.got
  61.9 1.9 %collective-permute-start.12 = (bf16[128,1024]{1,0:T(8,128)(2,1)S(1)}, bf16[128,1024]{1,0:T(8,128)(2,1)S(1)}, u32[]{:S(2)}, u32[]{:S(2)}) collective-permute-start(bf16[128,1024]{1,0:T(8,128)(2,1)S(1)} %shard_map.40), channel_id=1, source_target_pairs={{0,256},{1,257},{2,258},{3,259},{4,260},{5,261},{6,262},{7,263},{8... | collective-permute-start | bytes 786440 | tf_op jit(solution)/shard_map/ppermute | solution.py:37
  63.9 0.7 shard_map.37
  64.6 2.0 %collective-permute-start.11 = (bf16[128,1024]{1,0:T(8,128)(2,1)S(1)}, bf16[128,1024]{1,0:T(8,128)(2,1)S(1)}, u32[]{:S(2)}, u32[]{:S(2)}) collective-permute-start(bf16[128,1024]{1,0:T(8,128)(2,1)S(1)} %get-tuple-element.24), channel_id=1, source_target_pairs={{0,128},{1,129},{2,130},{3,131},{4,132},{5,133},{6,134},{7,135},{8... | collective-permute-start | bytes 786440 | tf_op jit(solution)/shard_map/ppermute | solution.py:37
  66.6 5.0 %collective-permute-done.12.block = bf16[128,1024]{1,0:T(8,128)(2,1)S(1)} collective-permute-done((bf16[128,1024]{1,0:T(8,128)(2,1)S(1)}, bf16[128,1024]{1,0:T(8,128)(2,1)S(1)}, u32[]{:S(2)}, u32[]{:S(2)}) %collective-permute-start.12) | collective-permute-done | bytes 262176 | tf_op jit(solution)/shard_map/ppermute | solution.py:37
  71.6 0.0 collective-permute-done.11.got
  71.6 1.0 %shard_map.42 = bf16[128,1024]{1,0:T(8,128)(2,1)} custom-call(bf16[256,1024]{1,0:T(8,128)(2,1)S(1)} %get-tuple-element.17.one.own.unit, f32[128,1]{1,0:T(8,128)S(1)} %get-tuple-element.16.inv, f32[128,1024]{1,0:T(8,128)S(1)} %get-tuple-element.19.keep, bf16[128,1024]{1,0:T(8,128)(2,1)S(1)} %collective-permute-done.11.got, ...), custom_call_target="tpu_custom_call" | custom-call | flops 1048576 | bytes 1573376 | tf_op jit(solution)/shard_map/pallas_call | solution.py:87
  (4 shorter events, 0.1 us)
Async XLA Ops:
  0.0 0.9 %copy-start = (bf16[128,1024]{1,0:T(8,128)(2,1)S(1)}, bf16[128,1024]{1,0:T(8,128)(2,1)}, u32[]{:S(2)}) copy-start(bf16[128,1024]{1,0:T(8,128)(2,1)} %s_hbm.1) | copy-start | bytes 786436
  1.0 0.9 %copy-start.1 = (bf16[128,1024]{1,0:T(8,128)(2,1)S(1)}, bf16[128,1024]{1,0:T(8,128)(2,1)}, u32[]{:S(2)}) copy-start(bf16[128,1024]{1,0:T(8,128)(2,1)} %t_hbm.1) | copy-start | bytes 786436
  2.2 23.6 %collective-permute-start = (bf16[256,1024]{1,0:T(8,128)(2,1)S(1)}, bf16[256,1024]{1,0:T(8,128)(2,1)S(1)}, u32[]{:S(2)}, u32[]{:S(2)}) collective-permute-start(bf16[256,1024]{1,0:T(8,128)(2,1)S(1)} %get-tuple-element.17.one.own.unit), channel_id=1, source_target_pairs={{0,128},{1,129},{2,130},{3,131},{4,132},{5,133},{6,134},{7,135},{8... | collective-permute-start | bytes 1572872 | tf_op jit(solution)/shard_map/ppermute | solution.py:37
  11.0 16.1 %collective-permute-start.2 = (bf16[256,1024]{1,0:T(8,128)(2,1)S(1)}, bf16[256,1024]{1,0:T(8,128)(2,1)S(1)}, u32[]{:S(2)}, u32[]{:S(2)}) collective-permute-start(bf16[256,1024]{1,0:T(8,128)(2,1)S(1)} %get-tuple-element.17.one.own.unit), channel_id=1, source_target_pairs={{0,152},{1,153},{32,184},{33,185},{64,216},{65,217},{96,248},{97,2... | collective-permute-start | bytes 1572872 | tf_op jit(solution)/shard_map/ppermute | solution.py:37
  11.7 24.9 %collective-permute-start.6 = (bf16[256,1024]{1,0:T(8,128)(2,1)S(1)}, bf16[256,1024]{1,0:T(8,128)(2,1)S(1)}, u32[]{:S(2)}, u32[]{:S(2)}) collective-permute-start(bf16[256,1024]{1,0:T(8,128)(2,1)S(1)} %get-tuple-element.17.one.own.unit), channel_id=1, source_target_pairs={{0,1},{1,2},{2,3},{3,4},{4,5},{5,6},{6,7},{7,8},{8,9},{9,10},{10,1... | collective-permute-start | bytes 1572872 | tf_op jit(solution)/shard_map/ppermute | solution.py:37
  24.4 13.6 %collective-permute-start.5 = (bf16[256,1024]{1,0:T(8,128)(2,1)S(1)}, bf16[256,1024]{1,0:T(8,128)(2,1)}, u32[]{:S(2)}, u32[]{:S(2)}) collective-permute-start(bf16[256,1024]{1,0:T(8,128)(2,1)S(1)} %get-tuple-element.17.one.own.unit), channel_id=1, source_target_pairs={{30,32},{62,64},{94,96},{126,0},{129,255},{161,159},{193,191},{225... | collective-permute-start | bytes 1572872 | tf_op jit(solution)/shard_map/ppermute | solution.py:37
  25.8 13.8 %collective-permute-start.1 = (bf16[256,1024]{1,0:T(8,128)(2,1)S(1)}, bf16[256,1024]{1,0:T(8,128)(2,1)S(1)}, u32[]{:S(2)}, u32[]{:S(2)}) collective-permute-start(bf16[256,1024]{1,0:T(8,128)(2,1)S(1)} %collective-permute-done.other), channel_id=1, source_target_pairs={{0,1},{1,2},{2,3},{3,4},{4,5},{5,6},{6,7},{7,8},{8,9},{9,10},{10,1... | collective-permute-start | bytes 1572872 | tf_op jit(solution)/shard_map/ppermute | solution.py:37
  28.0 19.8 %collective-permute-start.3 = (bf16[256,1024]{1,0:T(8,128)(2,1)}, bf16[256,1024]{1,0:T(8,128)(2,1)S(1)}, u32[]{:S(2)}, u32[]{:S(2)}) collective-permute-start(bf16[256,1024]{1,0:T(8,128)(2,1)} %shard_map.29), channel_id=1, source_target_pairs={{134,160},{135,32},{152,255},{153,127},{166,192},{167,64},{184,159... | collective-permute-start | bytes 1572872 | tf_op jit(solution)/shard_map/ppermute | solution.py:37
  29.3 19.9 %collective-permute-start.7 = (bf16[256,1024]{1,0:T(8,128)(2,1)S(1)}, bf16[256,1024]{1,0:T(8,128)(2,1)S(1)}, u32[]{:S(2)}, u32[]{:S(2)}) collective-permute-start(bf16[256,1024]{1,0:T(8,128)(2,1)S(1)} %get-tuple-element.17.one.own.unit), channel_id=1, source_target_pairs={{0,256},{1,257},{2,258},{3,259},{4,260},{5,261},{6,262},{7,263},{8... | collective-permute-start | bytes 1572872 | tf_op jit(solution)/shard_map/ppermute | solution.py:37
  36.7 14.6 %collective-permute-start.8 = (bf16[256,1024]{1,0:T(8,128)(2,1)S(1)}, bf16[256,1024]{1,0:T(8,128)(2,1)}, u32[]{:S(2)}, u32[]{:S(2)}) collective-permute-start(bf16[256,1024]{1,0:T(8,128)(2,1)S(1)} %shard_map.33.one_a), channel_id=1, source_target_pairs={{0,1},{1,2},{2,3},{3,4},{4,5},{5,6},{6,7},{7,8},{8,9},{9,10},{10,1... | collective-permute-start | bytes 1572872 | tf_op jit(solution)/shard_map/ppermute | solution.py:37
  47.9 9.9 %collective-permute-start.4 = (bf16[256,1024]{1,0:T(8,128)(2,1)S(1)}, bf16[256,1024]{1,0:T(8,128)(2,1)S(1)}, u32[]{:S(2)}, u32[]{:S(2)}) collective-permute-start(bf16[256,1024]{1,0:T(8,128)(2,1)S(1)} %shard_map.30.one_b), channel_id=1, source_target_pairs={{0,1},{1,2},{2,3},{3,4},{4,5},{5,6},{6,7},{7,8},{8,9},{9,10},{10,1... | collective-permute-start | bytes 1572872 | tf_op jit(solution)/shard_map/ppermute | solution.py:37
  49.3 3.8 %collective-permute-start.9 = (bf16[256,1024]{1,0:T(8,128)(2,1)S(1)}, bf16[256,1024]{1,0:T(8,128)(2,1)S(1)}, u32[]{:S(2)}, u32[]{:S(2)}) collective-permute-start(bf16[256,1024]{1,0:T(8,128)(2,1)S(1)} %shard_map.34.one), channel_id=1, source_target_pairs={{0,128},{1,129},{2,130},{3,131},{4,132},{5,133},{6,134},{7,135},{8... | collective-permute-start | bytes 1572872 | tf_op jit(solution)/shard_map/ppermute | solution.py:37
  58.5 3.4 %collective-permute-start.10 = (bf16[128,1024]{1,0:T(8,128)(2,1)S(1)}, bf16[128,1024]{1,0:T(8,128)(2,1)S(1)}, u32[]{:S(2)}, u32[]{:S(2)}) collective-permute-start(bf16[128,1024]{1,0:T(8,128)(2,1)S(1)} %get-tuple-element.23), channel_id=1, source_target_pairs={{0,128},{1,129},{2,130},{3,131},{4,132},{5,133},{6,134},{7,135},{8... | collective-permute-start | bytes 786440 | tf_op jit(solution)/shard_map/ppermute | solution.py:37
  61.9 9.7 %collective-permute-start.12 = (bf16[128,1024]{1,0:T(8,128)(2,1)S(1)}, bf16[128,1024]{1,0:T(8,128)(2,1)S(1)}, u32[]{:S(2)}, u32[]{:S(2)}) collective-permute-start(bf16[128,1024]{1,0:T(8,128)(2,1)S(1)} %shard_map.40), channel_id=1, source_target_pairs={{0,256},{1,257},{2,258},{3,259},{4,260},{5,261},{6,262},{7,263},{8... | collective-permute-start | bytes 786440 | tf_op jit(solution)/shard_map/ppermute | solution.py:37
  64.6 7.1 %collective-permute-start.11 = (bf16[128,1024]{1,0:T(8,128)(2,1)S(1)}, bf16[128,1024]{1,0:T(8,128)(2,1)S(1)}, u32[]{:S(2)}, u32[]{:S(2)}) collective-permute-start(bf16[128,1024]{1,0:T(8,128)(2,1)S(1)} %get-tuple-element.24), channel_id=1, source_target_pairs={{0,128},{1,129},{2,130},{3,131},{4,132},{5,133},{6,134},{7,135},{8... | collective-permute-start | bytes 786440 | tf_op jit(solution)/shard_map/ppermute | solution.py:37

commit v6 on v5

--- a/solution.py
+++ b/solution.py
@@ -10,8 +10,10 @@
 N_SECTION = 4
 N_DP = 128
 RUN = 32
+PARTS = 4
 F32 = jnp.float32
 BF16 = jnp.bfloat16
+START_COST = 1
 NEXT_COST = 400_000_000
 FINAL_COST = 400_000_000
 TWO_A_COST = 6_400_000_000
@@ -94,32 +96,26 @@
     )(*operands)
 
 
-def unit_kernel(s_hbm, t_hbm, unit_ref, inv_ref, s_ref, t_ref, sems):
-    copies = [
-        pltpu.make_async_copy(src, dst, sems.at[i])
-        for i, (src, dst) in enumerate(((s_hbm, s_ref), (t_hbm, t_ref)))
-    ]
-    for copy in copies:
-        copy.start()
-    for i, ref in enumerate((s_ref, t_ref)):
-        copies[i].wait()
-        values = ref[...].astype(F32)
-        inverse = lax.rsqrt(jnp.sum(values * values, axis=1, keepdims=True) + 1e-06)
-        unit_ref[i * ROWS : (i + 1) * ROWS, :] = (values * inverse).astype(BF16)
-        if i == 0:
-            inv_ref[...] = inverse
+def normalise(rows):
+    values = rows.astype(F32)
+    inverse = lax.rsqrt(jnp.sum(values * values, axis=1, keepdims=True) + 1e-06)
+    return (values * inverse).astype(BF16), inverse
+
+
+def student_kernel(s_ref, unit_ref, inv_ref):
+    unit_ref[...], inv_ref[...] = normalise(s_ref[...])
+
+
+def both_kernel(unit_s, t_ref, unit_ref):
+    unit_ref[:ROWS, :] = unit_s[...]
+    unit_ref[ROWS:, :] = normalise(t_ref[...])[0]
 
 
 def unit_rows(student, teacher):
-    return pl.pallas_call(
-        unit_kernel,
-        out_shape=(jax.ShapeDtypeStruct((2 * ROWS, D), BF16), jax.ShapeDtypeStruct((ROWS, 1), F32)),
-        in_specs=[pl.BlockSpec(memory_space=pl.ANY)] * 2,
-        out_specs=(VMEM, VMEM),
-        scratch_shapes=[pltpu.VMEM((ROWS, D), BF16)] * 2 + [pltpu.SemaphoreType.DMA((2,))],
-        cost_estimate=pl.CostEstimate(flops=10 * ROWS * D, bytes_accessed=4 * ROWS * D, transcendentals=0),
-        compiler_params=pltpu.CompilerParams(vmem_limit_bytes=16 * 2**20),
-    )(student, teacher)
+    shape = jax.ShapeDtypeStruct
+    outs = (shape((ROWS, D), BF16), shape((ROWS, 1), F32))
+    unit_s, inv = call(student_kernel, outs, START_COST, student)
+    return call(both_kernel, shape((2 * ROWS, D), BF16), 5 * ROWS * D, unit_s, teacher), inv
 
 
 def stack(blocks, part):
@@ -161,11 +157,31 @@
     send_ref[...] = (keep[...] + got[...].astype(F32)).astype(BF16)
 
 
-def last_kernel(unit, inv, keep, got, got_far, out_ref):
-    total = keep[...] + got[...].astype(F32) + got_far[...].astype(F32)
-    unit_f = unit[:ROWS, :].astype(F32)
-    along_unit = jnp.sum(unit_f * total, axis=1, keepdims=True)
-    out_ref[...] = (D / 2.0 * inv[...] * (total - unit_f * along_unit)).astype(BF16)
+def last_kernel(unit, inv, keep, got, got_far, out_hbm, out_ref, sems):
+    part = ROWS // PARTS
+    copies = []
+    for i in range(PARTS):
+        here = pl.ds(i * part, part)
+        total = keep[here, :] + got[here, :].astype(F32) + got_far[here, :].astype(F32)
+        unit_f = unit[here, :].astype(F32)
+        along_unit = jnp.sum(unit_f * total, axis=1, keepdims=True)
+        out_ref[here, :] = (D / 2.0 * inv[here, :] * (total - unit_f * along_unit)).astype(BF16)
+        copies.append(pltpu.make_async_copy(out_ref.at[here], out_hbm.at[here], sems.at[i]))
+        copies[i].start()
+    for copy in copies:
+        copy.wait()
+
+
+def last(*operands):
+    return pl.pallas_call(
+        last_kernel,
+        out_shape=jax.ShapeDtypeStruct((ROWS, D), BF16),
+        in_specs=[VMEM] * len(operands),
+        out_specs=pl.BlockSpec(memory_space=pl.ANY),
+        scratch_shapes=[pltpu.VMEM((ROWS, D), BF16), pltpu.SemaphoreType.DMA((PARTS,))],
+        cost_estimate=pl.CostEstimate(flops=8 * ROWS * D, bytes_accessed=12 * ROWS * D, transcendentals=0),
+        compiler_params=pltpu.CompilerParams(vmem_limit_bytes=16 * 2**20),
+    )(*operands)
 
 
 def after(block, *others):
@@ -207,7 +223,7 @@
     got_far = hold(route(send_far, to_y), TAIL_COST)
     keep, send = call(final_kernel, (quarter_f, quarter_h), gram, own, sib, two_b, extra, near_sum)
     got = route(after(send, send_far), to_core)
-    return call(last_kernel, quarter_h, 8 * ROWS * D, own, inv, keep, got, got_far)
+    return last(own, inv, keep, got, got_far)
 
 
 def solution(mesh):

time: 73.1 us -> 73 us (level)
    pallas_call x14 -> x15, Pallas kernels: 7.78 us -> 7.1 us  [call(): pl.pallas_call(kernel, out_shape=out_shape, in_specs=[pl.BlockSpec(memory...]
where the time goes in v6:
time: 73 us; the launch traced here: 72.4 us
  starting transfers between devices  38.4 us (53%)
  waiting for transfers between devices  23.9 us (33%)
  Pallas kernels  8.07 us (11%)
  local copies, waits for them, and re-layouts  1.76 us (2%)
    ppermute x13, starting transfers between devices, route(): return lax.ppermute(block, ('section', 'dp'), pairs)  38.4 us
    ppermute x13, waiting for transfers between devices, route(): return lax.ppermute(block, ('section', 'dp'), pairs)  23.9 us
    pallas_call x15, Pallas kernels, call(): pl.pallas_call(kernel, out_shape=out_shape, in_specs=[pl.BlockSpec(memory...  7.1 us
    unnamed x4, local copies, waits for them, and re-layouts  1.76 us
  transfers between devices with their start and end apart: 13, of which 7 were waited for; matrix products, arithmetic and copies ran while one was open for 0% of the time, Pallas kernels for 8%

profile of v6, /device:TPU:1, one launch (start us, length us, event | category | flops | bytes accessed | tf_op | source)
XLA Modules:
  0.0 72.4 jit_solution(7582111702806606031)
XLA Ops:
  0.0 0.0 copy-start
  0.0 0.9 %copy-done = bf16[128,1024]{1,0:T(8,128)(2,1)S(1)} copy-done((bf16[128,1024]{1,0:T(8,128)(2,1)S(1)}, bf16[128,1024]{1,0:T(8,128)(2,1)}, u32[]{:S(2)}) %copy-start) | copy-done | bytes 262168
  1.0 0.0 copy-start.1
  1.0 0.1 shard_map.28
  1.1 0.8 %copy-done.1 = bf16[128,1024]{1,0:T(8,128)(2,1)S(1)} copy-done((bf16[128,1024]{1,0:T(8,128)(2,1)S(1)}, bf16[128,1024]{1,0:T(8,128)(2,1)}, u32[]{:S(2)}) %copy-start.1) | copy-done | bytes 262168
  1.9 0.1 shard_map.29.one.own.unit
  2.0 8.8 %collective-permute-start = (bf16[256,1024]{1,0:T(8,128)(2,1)S(1)}, bf16[256,1024]{1,0:T(8,128)(2,1)S(1)}, u32[]{:S(2)}, u32[]{:S(2)}) collective-permute-start(bf16[256,1024]{1,0:T(8,128)(2,1)S(1)} %shard_map.29.one.own.unit), channel_id=1, source_target_pairs={{0,128},{1,129},{2,130},{3,131},{4,132},{5,133},{6,134},{7,135},{8... | collective-permute-start | bytes 1572872 | tf_op jit(solution)/shard_map/ppermute | solution.py:39
  10.8 0.7 collective-permute-start.2
  11.5 12.6 %collective-permute-start.6 = (bf16[256,1024]{1,0:T(8,128)(2,1)S(1)}, bf16[256,1024]{1,0:T(8,128)(2,1)S(1)}, u32[]{:S(2)}, u32[]{:S(2)}) collective-permute-start(bf16[256,1024]{1,0:T(8,128)(2,1)S(1)} %shard_map.29.one.own.unit), channel_id=1, source_target_pairs={{0,1},{1,2},{2,3},{3,4},{4,5},{5,6},{6,7},{7,8},{8,9},{9,10},{10,1... | collective-permute-start | bytes 1572872 | tf_op jit(solution)/shard_map/ppermute | solution.py:39
  24.2 1.5 %collective-permute-start.5 = (bf16[256,1024]{1,0:T(8,128)(2,1)S(1)}, bf16[256,1024]{1,0:T(8,128)(2,1)}, u32[]{:S(2)}, u32[]{:S(2)}) collective-permute-start(bf16[256,1024]{1,0:T(8,128)(2,1)S(1)} %shard_map.29.one.own.unit), channel_id=1, source_target_pairs={{30,32},{62,64},{94,96},{126,0},{129,255},{161,159},{193,191},{225... | collective-permute-start | bytes 1572872 | tf_op jit(solution)/shard_map/ppermute | solution.py:39
  25.6 0.0 collective-permute-done.other
  25.6 1.3 %collective-permute-start.1 = (bf16[256,1024]{1,0:T(8,128)(2,1)S(1)}, bf16[256,1024]{1,0:T(8,128)(2,1)S(1)}, u32[]{:S(2)}, u32[]{:S(2)}) collective-permute-start(bf16[256,1024]{1,0:T(8,128)(2,1)S(1)} %collective-permute-done.other), channel_id=1, source_target_pairs={{0,1},{1,2},{2,3},{3,4},{4,5},{5,6},{6,7},{7,8},{8,9},{9,10},{10,1... | collective-permute-start | bytes 1572872 | tf_op jit(solution)/shard_map/ppermute | solution.py:39
  26.9 0.0 collective-permute-done.2.block
  26.9 0.8 %shard_map.30 = bf16[256,1024]{1,0:T(8,128)(2,1)} custom-call(bf16[256,1024]{1,0:T(8,128)(2,1)S(1)} %collective-permute-done.2.block), custom_call_target="tpu_custom_call" | custom-call | flops 400000000 | bytes 524288 | tf_op jit(solution)/shard_map/pallas_call | solution.py:89
  27.8 1.3 %collective-permute-start.3 = (bf16[256,1024]{1,0:T(8,128)(2,1)}, bf16[256,1024]{1,0:T(8,128)(2,1)S(1)}, u32[]{:S(2)}, u32[]{:S(2)}) collective-permute-start(bf16[256,1024]{1,0:T(8,128)(2,1)} %shard_map.30), channel_id=1, source_target_pairs={{134,160},{135,32},{152,255},{153,127},{166,192},{167,64},{184,159... | collective-permute-start | bytes 1572872 | tf_op jit(solution)/shard_map/ppermute | solution.py:39
  29.1 1.9 %collective-permute-start.7 = (bf16[256,1024]{1,0:T(8,128)(2,1)S(1)}, bf16[256,1024]{1,0:T(8,128)(2,1)S(1)}, u32[]{:S(2)}, u32[]{:S(2)}) collective-permute-start(bf16[256,1024]{1,0:T(8,128)(2,1)S(1)} %shard_map.29.one.own.unit), channel_id=1, source_target_pairs={{0,256},{1,257},{2,258},{3,259},{4,260},{5,261},{6,262},{7,263},{8... | collective-permute-start | bytes 1572872 | tf_op jit(solution)/shard_map/ppermute | solution.py:39
  31.0 5.4 %collective-permute-done.6.block = bf16[256,1024]{1,0:T(8,128)(2,1)S(1)} collective-permute-done((bf16[256,1024]{1,0:T(8,128)(2,1)S(1)}, bf16[256,1024]{1,0:T(8,128)(2,1)S(1)}, u32[]{:S(2)}, u32[]{:S(2)}) %collective-permute-start.6) | collective-permute-done | bytes 524320 | tf_op jit(solution)/shard_map/ppermute | solution.py:39
  36.5 1.3 %collective-permute-start.8 = (bf16[256,1024]{1,0:T(8,128)(2,1)S(1)}, bf16[256,1024]{1,0:T(8,128)(2,1)}, u32[]{:S(2)}, u32[]{:S(2)}) collective-permute-start(bf16[256,1024]{1,0:T(8,128)(2,1)S(1)} %shard_map.34.one_a), channel_id=1, source_target_pairs={{0,1},{1,2},{2,3},{3,4},{4,5},{5,6},{6,7},{7,8},{8,9},{9,10},{10,1... | collective-permute-start | bytes 1572872 | tf_op jit(solution)/shard_map/ppermute | solution.py:39
  37.8 0.0 collective-permute-done.5.block
  37.8 1.1 %shard_map.32.direct = bf16[256,1024]{1,0:T(8,128)(2,1)S(1)} custom-call(bf16[256,1024]{1,0:T(8,128)(2,1)} %collective-permute-done.5.block), custom_call_target="tpu_custom_call" | custom-call | flops 400000000 | bytes 524288 | tf_op jit(solution)/shard_map/pallas_call | solution.py:89
  38.9 0.5 collective-permute-done.1.one_b
  39.4 8.2 %collective-permute-done.3.near_b = bf16[256,1024]{1,0:T(8,128)(2,1)S(1)} collective-permute-done((bf16[256,1024]{1,0:T(8,128)(2,1)}, bf16[256,1024]{1,0:T(8,128)(2,1)S(1)}, u32[]{:S(2)}, u32[]{:S(2)}) %collective-permute-start.3) | collective-permute-done | bytes 524320 | tf_op jit(solution)/shard_map/ppermute | solution.py:39
  47.6 0.1 shard_map.31.one_b
  47.7 1.3 %collective-permute-start.4 = (bf16[256,1024]{1,0:T(8,128)(2,1)S(1)}, bf16[256,1024]{1,0:T(8,128)(2,1)S(1)}, u32[]{:S(2)}, u32[]{:S(2)}) collective-permute-start(bf16[256,1024]{1,0:T(8,128)(2,1)S(1)} %shard_map.31.one_b), channel_id=1, source_target_pairs={{0,1},{1,2},{2,3},{3,4},{4,5},{5,6},{6,7},{7,8},{8,9},{9,10},{10,1... | collective-permute-start | bytes 1572872 | tf_op jit(solution)/shard_map/ppermute | solution.py:39
  49.0 0.0 collective-permute-done.7.block
  49.0 0.1 shard_map.33.extra
  49.1 1.9 %collective-permute-start.9 = (bf16[256,1024]{1,0:T(8,128)(2,1)S(1)}, bf16[256,1024]{1,0:T(8,128)(2,1)S(1)}, u32[]{:S(2)}, u32[]{:S(2)}) collective-permute-start(bf16[256,1024]{1,0:T(8,128)(2,1)S(1)} %shard_map.35.one), channel_id=1, source_target_pairs={{0,128},{1,129},{2,130},{3,131},{4,132},{5,133},{6,134},{7,135},{8... | collective-permute-start | bytes 1572872 | tf_op jit(solution)/shard_map/ppermute | solution.py:39
  51.0 0.0 collective-permute-done.8.block
  51.0 1.1 %shard_map.36.two_a = bf16[256,1024]{1,0:T(8,128)(2,1)S(1)} custom-call(bf16[256,1024]{1,0:T(8,128)(2,1)} %collective-permute-done.8.block), custom_call_target="tpu_custom_call" | custom-call | flops 6400000000 | bytes 524288 | tf_op jit(solution)/shard_map/pallas_call | solution.py:89
  52.1 0.8 %collective-permute-done.9.other = bf16[256,1024]{1,0:T(8,128)(2,1)S(1)} collective-permute-done((bf16[256,1024]{1,0:T(8,128)(2,1)S(1)}, bf16[256,1024]{1,0:T(8,128)(2,1)S(1)}, u32[]{:S(2)}, u32[]{:S(2)}) %collective-permute-start.9) | collective-permute-done | bytes 524320 | tf_op jit(solution)/shard_map/ppermute | solution.py:39
  52.9 1.1 %shard_map.39.old_ref = f32[256,1024]{1,0:T(8,128)S(1)} custom-call(bf16[256,1024]{1,0:T(8,128)(2,1)S(1)} %shard_map.35.one, bf16[256,1024]{1,0:T(8,128)(2,1)S(1)} %collective-permute-done.9.other, bf16[256,1024]{1,0:T(8,128)(2,1)S(1)} %shard_map.29.one.own.unit, bf16[256,1024]{1,0:T(8,128)(2,1)S(1)} %shard_map.34.one_a, ...), custom_call_target="tpu_custom_call" | custom-call | flops 6400000000 | bytes 3145728 | tf_op jit(solution)/shard_map/pallas_call | solution.py:89
  54.0 3.6 %collective-permute-done.4.two = bf16[256,1024]{1,0:T(8,128)(2,1)S(1)} collective-permute-done((bf16[256,1024]{1,0:T(8,128)(2,1)S(1)}, bf16[256,1024]{1,0:T(8,128)(2,1)S(1)}, u32[]{:S(2)}, u32[]{:S(2)}) %collective-permute-start.4) | collective-permute-done | bytes 524320 | tf_op jit(solution)/shard_map/ppermute | solution.py:39
  57.6 0.7 shard_map.40
  58.3 1.9 %collective-permute-start.10 = (bf16[128,1024]{1,0:T(8,128)(2,1)S(1)}, bf16[128,1024]{1,0:T(8,128)(2,1)S(1)}, u32[]{:S(2)}, u32[]{:S(2)}) collective-permute-start(bf16[128,1024]{1,0:T(8,128)(2,1)S(1)} %get-tuple-element.23), channel_id=1, source_target_pairs={{0,128},{1,129},{2,130},{3,131},{4,132},{5,133},{6,134},{7,135},{8... | collective-permute-start | bytes 786440 | tf_op jit(solution)/shard_map/ppermute | solution.py:39
  60.2 1.1 %shard_map.37.old_ref = f32[256,1024]{1,0:T(8,128)S(1)} custom-call(bf16[256,1024]{1,0:T(8,128)(2,1)S(1)} %shard_map.29.one.own.unit, bf16[256,1024]{1,0:T(8,128)(2,1)S(1)} %collective-permute-done.other, bf16[256,1024]{1,0:T(8,128)(2,1)S(1)} %shard_map.29.one.own.unit, bf16[256,1024]{1,0:T(8,128)(2,1)S(1)} %shard_map.34.one_a, ...), custom_call_target="tpu_custom_call" | custom-call | flops 400000000 | bytes 3145728 | tf_op jit(solution)/shard_map/pallas_call | solution.py:89
  61.3 0.4 collective-permute-done.10.got
  61.8 1.9 %collective-permute-start.12 = (bf16[128,1024]{1,0:T(8,128)(2,1)S(1)}, bf16[128,1024]{1,0:T(8,128)(2,1)S(1)}, u32[]{:S(2)}, u32[]{:S(2)}) collective-permute-start(bf16[128,1024]{1,0:T(8,128)(2,1)S(1)} %shard_map.41), channel_id=1, source_target_pairs={{0,256},{1,257},{2,258},{3,259},{4,260},{5,261},{6,262},{7,263},{8... | collective-permute-start | bytes 786440 | tf_op jit(solution)/shard_map/ppermute | solution.py:39
  63.7 0.7 shard_map.38
  64.4 2.0 %collective-permute-start.11 = (bf16[128,1024]{1,0:T(8,128)(2,1)S(1)}, bf16[128,1024]{1,0:T(8,128)(2,1)S(1)}, u32[]{:S(2)}, u32[]{:S(2)}) collective-permute-start(bf16[128,1024]{1,0:T(8,128)(2,1)S(1)} %get-tuple-element.24), channel_id=1, source_target_pairs={{0,128},{1,129},{2,130},{3,131},{4,132},{5,133},{6,134},{7,135},{8... | collective-permute-start | bytes 786440 | tf_op jit(solution)/shard_map/ppermute | solution.py:39
  66.4 5.0 %collective-permute-done.12.block = bf16[128,1024]{1,0:T(8,128)(2,1)S(1)} collective-permute-done((bf16[128,1024]{1,0:T(8,128)(2,1)S(1)}, bf16[128,1024]{1,0:T(8,128)(2,1)S(1)}, u32[]{:S(2)}, u32[]{:S(2)}) %collective-permute-start.12) | collective-permute-done | bytes 262176 | tf_op jit(solution)/shard_map/ppermute | solution.py:39
  71.4 0.0 collective-permute-done.11.got
  71.4 1.0 %shard_map.43 = bf16[128,1024]{1,0:T(8,128)(2,1)} custom-call(bf16[256,1024]{1,0:T(8,128)(2,1)S(1)} %shard_map.29.one.own.unit, f32[128,1]{1,0:T(8,128)S(1)} %get-tuple-element.16.inv, f32[128,1024]{1,0:T(8,128)S(1)} %get-tuple-element.19.keep, bf16[128,1024]{1,0:T(8,128)(2,1)S(1)} %collective-permute-done.11.got, bf16[128,1024]{1,0:T(8,128)(2,1)S(1)} %shard_map.42.got_far), custom_call_target="tpu_custom_call" | custom-call | flops 1048576 | bytes 1572864 | tf_op jit(solution)/shard_map/pallas_call | solution.py:176
  (4 shorter events, 0.1 us)
Async XLA Ops:
  0.0 0.9 %copy-start = (bf16[128,1024]{1,0:T(8,128)(2,1)S(1)}, bf16[128,1024]{1,0:T(8,128)(2,1)}, u32[]{:S(2)}) copy-start(bf16[128,1024]{1,0:T(8,128)(2,1)} %s_ref.1) | copy-start | bytes 786436
  1.0 0.9 %copy-start.1 = (bf16[128,1024]{1,0:T(8,128)(2,1)S(1)}, bf16[128,1024]{1,0:T(8,128)(2,1)}, u32[]{:S(2)}) copy-start(bf16[128,1024]{1,0:T(8,128)(2,1)} %t_ref.1) | copy-start | bytes 786436
  2.0 23.6 %collective-permute-start = (bf16[256,1024]{1,0:T(8,128)(2,1)S(1)}, bf16[256,1024]{1,0:T(8,128)(2,1)S(1)}, u32[]{:S(2)}, u32[]{:S(2)}) collective-permute-start(bf16[256,1024]{1,0:T(8,128)(2,1)S(1)} %shard_map.29.one.own.unit), channel_id=1, source_target_pairs={{0,128},{1,129},{2,130},{3,131},{4,132},{5,133},{6,134},{7,135},{8... | collective-permute-start | bytes 1572872 | tf_op jit(solution)/shard_map/ppermute | solution.py:39
  10.8 16.1 %collective-permute-start.2 = (bf16[256,1024]{1,0:T(8,128)(2,1)S(1)}, bf16[256,1024]{1,0:T(8,128)(2,1)S(1)}, u32[]{:S(2)}, u32[]{:S(2)}) collective-permute-start(bf16[256,1024]{1,0:T(8,128)(2,1)S(1)} %shard_map.29.one.own.unit), channel_id=1, source_target_pairs={{0,152},{1,153},{32,184},{33,185},{64,216},{65,217},{96,248},{97,2... | collective-permute-start | bytes 1572872 | tf_op jit(solution)/shard_map/ppermute | solution.py:39
  11.5 24.9 %collective-permute-start.6 = (bf16[256,1024]{1,0:T(8,128)(2,1)S(1)}, bf16[256,1024]{1,0:T(8,128)(2,1)S(1)}, u32[]{:S(2)}, u32[]{:S(2)}) collective-permute-start(bf16[256,1024]{1,0:T(8,128)(2,1)S(1)} %shard_map.29.one.own.unit), channel_id=1, source_target_pairs={{0,1},{1,2},{2,3},{3,4},{4,5},{5,6},{6,7},{7,8},{8,9},{9,10},{10,1... | collective-permute-start | bytes 1572872 | tf_op jit(solution)/shard_map/ppermute | solution.py:39
  24.2 13.6 %collective-permute-start.5 = (bf16[256,1024]{1,0:T(8,128)(2,1)S(1)}, bf16[256,1024]{1,0:T(8,128)(2,1)}, u32[]{:S(2)}, u32[]{:S(2)}) collective-permute-start(bf16[256,1024]{1,0:T(8,128)(2,1)S(1)} %shard_map.29.one.own.unit), channel_id=1, source_target_pairs={{30,32},{62,64},{94,96},{126,0},{129,255},{161,159},{193,191},{225... | collective-permute-start | bytes 1572872 | tf_op jit(solution)/shard_map/ppermute | solution.py:39
  25.6 13.8 %collective-permute-start.1 = (bf16[256,1024]{1,0:T(8,128)(2,1)S(1)}, bf16[256,1024]{1,0:T(8,128)(2,1)S(1)}, u32[]{:S(2)}, u32[]{:S(2)}) collective-permute-start(bf16[256,1024]{1,0:T(8,128)(2,1)S(1)} %collective-permute-done.other), channel_id=1, source_target_pairs={{0,1},{1,2},{2,3},{3,4},{4,5},{5,6},{6,7},{7,8},{8,9},{9,10},{10,1... | collective-permute-start | bytes 1572872 | tf_op jit(solution)/shard_map/ppermute | solution.py:39
  27.8 19.8 %collective-permute-start.3 = (bf16[256,1024]{1,0:T(8,128)(2,1)}, bf16[256,1024]{1,0:T(8,128)(2,1)S(1)}, u32[]{:S(2)}, u32[]{:S(2)}) collective-permute-start(bf16[256,1024]{1,0:T(8,128)(2,1)} %shard_map.30), channel_id=1, source_target_pairs={{134,160},{135,32},{152,255},{153,127},{166,192},{167,64},{184,159... | collective-permute-start | bytes 1572872 | tf_op jit(solution)/shard_map/ppermute | solution.py:39
  29.1 19.9 %collective-permute-start.7 = (bf16[256,1024]{1,0:T(8,128)(2,1)S(1)}, bf16[256,1024]{1,0:T(8,128)(2,1)S(1)}, u32[]{:S(2)}, u32[]{:S(2)}) collective-permute-start(bf16[256,1024]{1,0:T(8,128)(2,1)S(1)} %shard_map.29.one.own.unit), channel_id=1, source_target_pairs={{0,256},{1,257},{2,258},{3,259},{4,260},{5,261},{6,262},{7,263},{8... | collective-permute-start | bytes 1572872 | tf_op jit(solution)/shard_map/ppermute | solution.py:39
  36.5 14.6 %collective-permute-start.8 = (bf16[256,1024]{1,0:T(8,128)(2,1)S(1)}, bf16[256,1024]{1,0:T(8,128)(2,1)}, u32[]{:S(2)}, u32[]{:S(2)}) collective-permute-start(bf16[256,1024]{1,0:T(8,128)(2,1)S(1)} %shard_map.34.one_a), channel_id=1, source_target_pairs={{0,1},{1,2},{2,3},{3,4},{4,5},{5,6},{6,7},{7,8},{8,9},{9,10},{10,1... | collective-permute-start | bytes 1572872 | tf_op jit(solution)/shard_map/ppermute | solution.py:39
  47.7 9.9 %collective-permute-start.4 = (bf16[256,1024]{1,0:T(8,128)(2,1)S(1)}, bf16[256,1024]{1,0:T(8,128)(2,1)S(1)}, u32[]{:S(2)}, u32[]{:S(2)}) collective-permute-start(bf16[256,1024]{1,0:T(8,128)(2,1)S(1)} %shard_map.31.one_b), channel_id=1, source_target_pairs={{0,1},{1,2},{2,3},{3,4},{4,5},{5,6},{6,7},{7,8},{8,9},{9,10},{10,1... | collective-permute-start | bytes 1572872 | tf_op jit(solution)/shard_map/ppermute | solution.py:39
  49.1 3.8 %collective-permute-start.9 = (bf16[256,1024]{1,0:T(8,128)(2,1)S(1)}, bf16[256,1024]{1,0:T(8,128)(2,1)S(1)}, u32[]{:S(2)}, u32[]{:S(2)}) collective-permute-start(bf16[256,1024]{1,0:T(8,128)(2,1)S(1)} %shard_map.35.one), channel_id=1, source_target_pairs={{0,128},{1,129},{2,130},{3,131},{4,132},{5,133},{6,134},{7,135},{8... | collective-permute-start | bytes 1572872 | tf_op jit(solution)/shard_map/ppermute | solution.py:39
  58.3 3.4 %collective-permute-start.10 = (bf16[128,1024]{1,0:T(8,128)(2,1)S(1)}, bf16[128,1024]{1,0:T(8,128)(2,1)S(1)}, u32[]{:S(2)}, u32[]{:S(2)}) collective-permute-start(bf16[128,1024]{1,0:T(8,128)(2,1)S(1)} %get-tuple-element.23), channel_id=1, source_target_pairs={{0,128},{1,129},{2,130},{3,131},{4,132},{5,133},{6,134},{7,135},{8... | collective-permute-start | bytes 786440 | tf_op jit(solution)/shard_map/ppermute | solution.py:39
  61.8 9.7 %collective-permute-start.12 = (bf16[128,1024]{1,0:T(8,128)(2,1)S(1)}, bf16[128,1024]{1,0:T(8,128)(2,1)S(1)}, u32[]{:S(2)}, u32[]{:S(2)}) collective-permute-start(bf16[128,1024]{1,0:T(8,128)(2,1)S(1)} %shard_map.41), channel_id=1, source_target_pairs={{0,256},{1,257},{2,258},{3,259},{4,260},{5,261},{6,262},{7,263},{8... | collective-permute-start | bytes 786440 | tf_op jit(solution)/shard_map/ppermute | solution.py:39
  64.4 7.1 %collective-permute-start.11 = (bf16[128,1024]{1,0:T(8,128)(2,1)S(1)}, bf16[128,1024]{1,0:T(8,128)(2,1)S(1)}, u32[]{:S(2)}, u32[]{:S(2)}) collective-permute-start(bf16[128,1024]{1,0:T(8,128)(2,1)S(1)} %get-tuple-element.24), channel_id=1, source_target_pairs={{0,128},{1,129},{2,130},{3,131},{4,132},{5,133},{6,134},{7,135},{8... | collective-permute-start | bytes 786440 | tf_op jit(solution)/shard_map/ppermute | solution.py:39

commit v7 on v6

--- a/solution.py
+++ b/solution.py
@@ -22,7 +22,6 @@
 ONE_A_COST = 400_000_000
 TAIL_COST = 200_000_000
 AWAY_COST = 6_400_000_000
-SPREAD_COST = 400_000_000
 DIRECT_COST = 400_000_000
 NEAR_COST = 400_000_000
 VMEM = pl.BlockSpec(memory_space=pltpu.VMEM)
@@ -199,7 +198,7 @@
     gram = 2 * 3 * 2 * ROWS * ROWS * D
     own, inv = unit_rows(student, teacher)
     one_a = hold(route(own, along), ONE_A_COST)
-    spread = hold(route(own, aside), SPREAD_COST)
+    spread = route(own, aside)
     direct = hold(route(own, across), DIRECT_COST)
     far = hold(route(after(own, spread), to_y), FAR_COST)
     sib = route(own, to_core)

time: 73 us -> 72.9 us (level)
  starting transfers between devices: 38.4 us -> 40.9 us
  waiting for transfers between devices: 23.9 us -> 22.2 us
  Pallas kernels: 8.07 us -> 7.24 us
    ppermute x13, starting transfers between devices: 38.4 us -> 40.9 us  [route(): return lax.ppermute(block, ('section', 'dp'), pairs)]
    ppermute x13, waiting for transfers between devices: 23.9 us -> 22.2 us  [route(): return lax.ppermute(block, ('section', 'dp'), pairs)]
    pallas_call x15 -> x14, Pallas kernels: 7.1 us -> 6.27 us  [call(): pl.pallas_call(kernel, out_shape=out_shape, in_specs=[pl.BlockSpec(memory...]
  transfers between devices with their start and end apart: 13 -> 13, of which waited for: 7 -> 7; matrix products, arithmetic and copies ran while one was open for 0% -> 0% of each run, Pallas kernels for 8% -> 7%
where the time goes in v7:
time: 72.9 us; the launch traced here: 72.4 us
  starting transfers between devices  40.9 us (56%)
  waiting for transfers between devices  22.2 us (30%)
  Pallas kernels  7.24 us (10%)
  local copies, waits for them, and re-layouts  1.76 us (2%)
    ppermute x13, starting transfers between devices, route(): return lax.ppermute(block, ('section', 'dp'), pairs)  40.9 us
    ppermute x13, waiting for transfers between devices, route(): return lax.ppermute(block, ('section', 'dp'), pairs)  22.2 us
    pallas_call x14, Pallas kernels, call(): pl.pallas_call(kernel, out_shape=out_shape, in_specs=[pl.BlockSpec(memory...  6.27 us
    unnamed x4, local copies, waits for them, and re-layouts  1.76 us
  transfers between devices with their start and end apart: 13, of which 7 were waited for; matrix products, arithmetic and copies ran while one was open for 0% of the time, Pallas kernels for 7%

profile of v7, /device:TPU:1, one launch (start us, length us, event | category | flops | bytes accessed | tf_op | source)
XLA Modules:
  0.0 72.4 jit_solution(11159577318653009006)
XLA Ops:
  0.0 0.0 copy-start
  0.0 0.9 %copy-done = bf16[128,1024]{1,0:T(8,128)(2,1)S(1)} copy-done((bf16[128,1024]{1,0:T(8,128)(2,1)S(1)}, bf16[128,1024]{1,0:T(8,128)(2,1)}, u32[]{:S(2)}) %copy-start) | copy-done | bytes 262168
  1.0 0.0 copy-start.1
  1.0 0.1 shard_map.28
  1.1 0.8 %copy-done.1 = bf16[128,1024]{1,0:T(8,128)(2,1)S(1)} copy-done((bf16[128,1024]{1,0:T(8,128)(2,1)S(1)}, bf16[128,1024]{1,0:T(8,128)(2,1)}, u32[]{:S(2)}) %copy-start.1) | copy-done | bytes 262168
  1.9 0.1 shard_map.29.one.own.unit
  2.0 8.8 %collective-permute-start = (bf16[256,1024]{1,0:T(8,128)(2,1)S(1)}, bf16[256,1024]{1,0:T(8,128)(2,1)S(1)}, u32[]{:S(2)}, u32[]{:S(2)}) collective-permute-start(bf16[256,1024]{1,0:T(8,128)(2,1)S(1)} %shard_map.29.one.own.unit), channel_id=1, source_target_pairs={{0,128},{1,129},{2,130},{3,131},{4,132},{5,133},{6,134},{7,135},{8... | collective-permute-start | bytes 1572872 | tf_op jit(solution)/shard_map/ppermute | solution.py:38
  10.8 1.5 %collective-permute-start.2 = (bf16[256,1024]{1,0:T(8,128)(2,1)S(1)}, bf16[256,1024]{1,0:T(8,128)(2,1)}, u32[]{:S(2)}, u32[]{:S(2)}) collective-permute-start(bf16[256,1024]{1,0:T(8,128)(2,1)S(1)} %shard_map.29.one.own.unit), channel_id=1, source_target_pairs={{0,152},{1,153},{32,184},{33,185},{64,216},{65,217},{96,248},{97,2... | collective-permute-start | bytes 1572872 | tf_op jit(solution)/shard_map/ppermute | solution.py:38
  12.3 12.6 %collective-permute-start.6 = (bf16[256,1024]{1,0:T(8,128)(2,1)S(1)}, bf16[256,1024]{1,0:T(8,128)(2,1)S(1)}, u32[]{:S(2)}, u32[]{:S(2)}) collective-permute-start(bf16[256,1024]{1,0:T(8,128)(2,1)S(1)} %shard_map.29.one.own.unit), channel_id=1, source_target_pairs={{0,1},{1,2},{2,3},{3,4},{4,5},{5,6},{6,7},{7,8},{8,9},{9,10},{10,1... | collective-permute-start | bytes 1572872 | tf_op jit(solution)/shard_map/ppermute | solution.py:38
  24.9 1.5 %collective-permute-start.5 = (bf16[256,1024]{1,0:T(8,128)(2,1)S(1)}, bf16[256,1024]{1,0:T(8,128)(2,1)}, u32[]{:S(2)}, u32[]{:S(2)}) collective-permute-start(bf16[256,1024]{1,0:T(8,128)(2,1)S(1)} %shard_map.29.one.own.unit), channel_id=1, source_target_pairs={{30,32},{62,64},{94,96},{126,0},{129,255},{161,159},{193,191},{225... | collective-permute-start | bytes 1572872 | tf_op jit(solution)/shard_map/ppermute | solution.py:38
  26.4 0.0 collective-permute-done.other
  26.4 1.3 %collective-permute-start.1 = (bf16[256,1024]{1,0:T(8,128)(2,1)S(1)}, bf16[256,1024]{1,0:T(8,128)(2,1)S(1)}, u32[]{:S(2)}, u32[]{:S(2)}) collective-permute-start(bf16[256,1024]{1,0:T(8,128)(2,1)S(1)} %collective-permute-done.other), channel_id=1, source_target_pairs={{0,1},{1,2},{2,3},{3,4},{4,5},{5,6},{6,7},{7,8},{8,9},{9,10},{10,1... | collective-permute-start | bytes 1572872 | tf_op jit(solution)/shard_map/ppermute | solution.py:38
  27.7 0.0 collective-permute-done.2
  27.7 1.3 %collective-permute-start.3 = (bf16[256,1024]{1,0:T(8,128)(2,1)}, bf16[256,1024]{1,0:T(8,128)(2,1)S(1)}, u32[]{:S(2)}, u32[]{:S(2)}) collective-permute-start(bf16[256,1024]{1,0:T(8,128)(2,1)} %collective-permute-done.2), channel_id=1, source_target_pairs={{134,160},{135,32},{152,255},{153,127},{166,192},{167,64},{184,159... | collective-permute-start | bytes 1572872 | tf_op jit(solution)/shard_map/ppermute | solution.py:38
  29.0 1.9 %collective-permute-start.7 = (bf16[256,1024]{1,0:T(8,128)(2,1)S(1)}, bf16[256,1024]{1,0:T(8,128)(2,1)S(1)}, u32[]{:S(2)}, u32[]{:S(2)}) collective-permute-start(bf16[256,1024]{1,0:T(8,128)(2,1)S(1)} %shard_map.29.one.own.unit), channel_id=1, source_target_pairs={{0,256},{1,257},{2,258},{3,259},{4,260},{5,261},{6,262},{7,263},{8... | collective-permute-start | bytes 1572872 | tf_op jit(solution)/shard_map/ppermute | solution.py:38
  30.9 5.0 %collective-permute-done.6.block = bf16[256,1024]{1,0:T(8,128)(2,1)S(1)} collective-permute-done((bf16[256,1024]{1,0:T(8,128)(2,1)S(1)}, bf16[256,1024]{1,0:T(8,128)(2,1)S(1)}, u32[]{:S(2)}, u32[]{:S(2)}) %collective-permute-start.6) | collective-permute-done | bytes 524320 | tf_op jit(solution)/shard_map/ppermute | solution.py:38
  36.0 1.3 %collective-permute-start.8 = (bf16[256,1024]{1,0:T(8,128)(2,1)S(1)}, bf16[256,1024]{1,0:T(8,128)(2,1)}, u32[]{:S(2)}, u32[]{:S(2)}) collective-permute-start(bf16[256,1024]{1,0:T(8,128)(2,1)S(1)} %shard_map.33.one_a), channel_id=1, source_target_pairs={{0,1},{1,2},{2,3},{3,4},{4,5},{5,6},{6,7},{7,8},{8,9},{9,10},{10,1... | collective-permute-start | bytes 1572872 | tf_op jit(solution)/shard_map/ppermute | solution.py:38
  37.3 0.0 collective-permute-done.5.block
  37.3 1.1 %shard_map.31.direct = bf16[256,1024]{1,0:T(8,128)(2,1)S(1)} custom-call(bf16[256,1024]{1,0:T(8,128)(2,1)} %collective-permute-done.5.block), custom_call_target="tpu_custom_call" | custom-call | flops 400000000 | bytes 524288 | tf_op jit(solution)/shard_map/pallas_call | solution.py:88
  38.4 1.7 %collective-permute-done.1.one_b = bf16[256,1024]{1,0:T(8,128)(2,1)S(1)} collective-permute-done((bf16[256,1024]{1,0:T(8,128)(2,1)S(1)}, bf16[256,1024]{1,0:T(8,128)(2,1)S(1)}, u32[]{:S(2)}, u32[]{:S(2)}) %collective-permute-start.1) | collective-permute-done | bytes 524320 | tf_op jit(solution)/shard_map/ppermute | solution.py:38
  40.1 7.5 %collective-permute-done.3.near_b = bf16[256,1024]{1,0:T(8,128)(2,1)S(1)} collective-permute-done((bf16[256,1024]{1,0:T(8,128)(2,1)}, bf16[256,1024]{1,0:T(8,128)(2,1)S(1)}, u32[]{:S(2)}, u32[]{:S(2)}) %collective-permute-start.3) | collective-permute-done | bytes 524320 | tf_op jit(solution)/shard_map/ppermute | solution.py:38
  47.5 0.1 shard_map.30.one_b
  47.6 1.3 %collective-permute-start.4 = (bf16[256,1024]{1,0:T(8,128)(2,1)S(1)}, bf16[256,1024]{1,0:T(8,128)(2,1)S(1)}, u32[]{:S(2)}, u32[]{:S(2)}) collective-permute-start(bf16[256,1024]{1,0:T(8,128)(2,1)S(1)} %shard_map.30.one_b), channel_id=1, source_target_pairs={{0,1},{1,2},{2,3},{3,4},{4,5},{5,6},{6,7},{7,8},{8,9},{9,10},{10,1... | collective-permute-start | bytes 1572872 | tf_op jit(solution)/shard_map/ppermute | solution.py:38
  48.9 0.0 collective-permute-done.7.block
  49.0 0.1 shard_map.32.extra
  49.0 1.9 %collective-permute-start.9 = (bf16[256,1024]{1,0:T(8,128)(2,1)S(1)}, bf16[256,1024]{1,0:T(8,128)(2,1)S(1)}, u32[]{:S(2)}, u32[]{:S(2)}) collective-permute-start(bf16[256,1024]{1,0:T(8,128)(2,1)S(1)} %shard_map.34.one), channel_id=1, source_target_pairs={{0,128},{1,129},{2,130},{3,131},{4,132},{5,133},{6,134},{7,135},{8... | collective-permute-start | bytes 1572872 | tf_op jit(solution)/shard_map/ppermute | solution.py:38
  51.0 0.0 collective-permute-done.8.block
  51.0 1.1 %shard_map.35.two_a = bf16[256,1024]{1,0:T(8,128)(2,1)S(1)} custom-call(bf16[256,1024]{1,0:T(8,128)(2,1)} %collective-permute-done.8.block), custom_call_target="tpu_custom_call" | custom-call | flops 6400000000 | bytes 524288 | tf_op jit(solution)/shard_map/pallas_call | solution.py:88
  52.1 0.8 %collective-permute-done.9.other = bf16[256,1024]{1,0:T(8,128)(2,1)S(1)} collective-permute-done((bf16[256,1024]{1,0:T(8,128)(2,1)S(1)}, bf16[256,1024]{1,0:T(8,128)(2,1)S(1)}, u32[]{:S(2)}, u32[]{:S(2)}) %collective-permute-start.9) | collective-permute-done | bytes 524320 | tf_op jit(solution)/shard_map/ppermute | solution.py:38
  52.9 1.1 %shard_map.38.old_ref = f32[256,1024]{1,0:T(8,128)S(1)} custom-call(bf16[256,1024]{1,0:T(8,128)(2,1)S(1)} %shard_map.34.one, bf16[256,1024]{1,0:T(8,128)(2,1)S(1)} %collective-permute-done.9.other, bf16[256,1024]{1,0:T(8,128)(2,1)S(1)} %shard_map.29.one.own.unit, bf16[256,1024]{1,0:T(8,128)(2,1)S(1)} %shard_map.33.one_a, ...), custom_call_target="tpu_custom_call" | custom-call | flops 6400000000 | bytes 3145728 | tf_op jit(solution)/shard_map/pallas_call | solution.py:88
  54.0 3.6 %collective-permute-done.4.two = bf16[256,1024]{1,0:T(8,128)(2,1)S(1)} collective-permute-done((bf16[256,1024]{1,0:T(8,128)(2,1)S(1)}, bf16[256,1024]{1,0:T(8,128)(2,1)S(1)}, u32[]{:S(2)}, u32[]{:S(2)}) %collective-permute-start.4) | collective-permute-done | bytes 524320 | tf_op jit(solution)/shard_map/ppermute | solution.py:38
  57.5 0.7 shard_map.39
  58.2 1.9 %collective-permute-start.10 = (bf16[128,1024]{1,0:T(8,128)(2,1)S(1)}, bf16[128,1024]{1,0:T(8,128)(2,1)S(1)}, u32[]{:S(2)}, u32[]{:S(2)}) collective-permute-start(bf16[128,1024]{1,0:T(8,128)(2,1)S(1)} %get-tuple-element.23), channel_id=1, source_target_pairs={{0,128},{1,129},{2,130},{3,131},{4,132},{5,133},{6,134},{7,135},{8... | collective-permute-start | bytes 786440 | tf_op jit(solution)/shard_map/ppermute | solution.py:38
  60.2 1.1 %shard_map.36.old_ref = f32[256,1024]{1,0:T(8,128)S(1)} custom-call(bf16[256,1024]{1,0:T(8,128)(2,1)S(1)} %shard_map.29.one.own.unit, bf16[256,1024]{1,0:T(8,128)(2,1)S(1)} %collective-permute-done.other, bf16[256,1024]{1,0:T(8,128)(2,1)S(1)} %shard_map.29.one.own.unit, bf16[256,1024]{1,0:T(8,128)(2,1)S(1)} %shard_map.33.one_a, ...), custom_call_target="tpu_custom_call" | custom-call | flops 400000000 | bytes 3145728 | tf_op jit(solution)/shard_map/pallas_call | solution.py:88
  61.3 0.4 collective-permute-done.10.got
  61.7 3.1 %collective-permute-start.12 = (bf16[128,1024]{1,0:T(8,128)(2,1)S(1)}, bf16[128,1024]{1,0:T(8,128)(2,1)S(1)}, u32[]{:S(2)}, u32[]{:S(2)}) collective-permute-start(bf16[128,1024]{1,0:T(8,128)(2,1)S(1)} %shard_map.40), channel_id=1, source_target_pairs={{0,256},{1,257},{2,258},{3,259},{4,260},{5,261},{6,262},{7,263},{8... | collective-permute-start | bytes 786440 | tf_op jit(solution)/shard_map/ppermute | solution.py:38
  64.8 0.7 shard_map.37
  65.5 2.6 %collective-permute-start.11 = (bf16[128,1024]{1,0:T(8,128)(2,1)S(1)}, bf16[128,1024]{1,0:T(8,128)(2,1)S(1)}, u32[]{:S(2)}, u32[]{:S(2)}) collective-permute-start(bf16[128,1024]{1,0:T(8,128)(2,1)S(1)} %get-tuple-element.24), channel_id=1, source_target_pairs={{0,128},{1,129},{2,130},{3,131},{4,132},{5,133},{6,134},{7,135},{8... | collective-permute-start | bytes 786440 | tf_op jit(solution)/shard_map/ppermute | solution.py:38
  68.1 3.3 %collective-permute-done.12.block = bf16[128,1024]{1,0:T(8,128)(2,1)S(1)} collective-permute-done((bf16[128,1024]{1,0:T(8,128)(2,1)S(1)}, bf16[128,1024]{1,0:T(8,128)(2,1)S(1)}, u32[]{:S(2)}, u32[]{:S(2)}) %collective-permute-start.12) | collective-permute-done | bytes 262176 | tf_op jit(solution)/shard_map/ppermute | solution.py:38
  71.4 0.0 collective-permute-done.11.got
  71.4 1.0 %shard_map.42 = bf16[128,1024]{1,0:T(8,128)(2,1)} custom-call(bf16[256,1024]{1,0:T(8,128)(2,1)S(1)} %shard_map.29.one.own.unit, f32[128,1]{1,0:T(8,128)S(1)} %get-tuple-element.16.inv, f32[128,1024]{1,0:T(8,128)S(1)} %get-tuple-element.19.keep, bf16[128,1024]{1,0:T(8,128)(2,1)S(1)} %collective-permute-done.11.got, bf16[128,1024]{1,0:T(8,128)(2,1)S(1)} %shard_map.41.got_far), custom_call_target="tpu_custom_call" | custom-call | flops 1048576 | bytes 1572864 | tf_op jit(solution)/shard_map/pallas_call | solution.py:175
  (4 shorter events, 0.1 us)
Async XLA Ops:
  0.0 0.9 %copy-start = (bf16[128,1024]{1,0:T(8,128)(2,1)S(1)}, bf16[128,1024]{1,0:T(8,128)(2,1)}, u32[]{:S(2)}) copy-start(bf16[128,1024]{1,0:T(8,128)(2,1)} %s_ref.1) | copy-start | bytes 786436
  1.0 0.9 %copy-start.1 = (bf16[128,1024]{1,0:T(8,128)(2,1)S(1)}, bf16[128,1024]{1,0:T(8,128)(2,1)}, u32[]{:S(2)}) copy-start(bf16[128,1024]{1,0:T(8,128)(2,1)} %t_ref.1) | copy-start | bytes 786436
  2.0 24.4 %collective-permute-start = (bf16[256,1024]{1,0:T(8,128)(2,1)S(1)}, bf16[256,1024]{1,0:T(8,128)(2,1)S(1)}, u32[]{:S(2)}, u32[]{:S(2)}) collective-permute-start(bf16[256,1024]{1,0:T(8,128)(2,1)S(1)} %shard_map.29.one.own.unit), channel_id=1, source_target_pairs={{0,128},{1,129},{2,130},{3,131},{4,132},{5,133},{6,134},{7,135},{8... | collective-permute-start | bytes 1572872 | tf_op jit(solution)/shard_map/ppermute | solution.py:38
  10.8 16.9 %collective-permute-start.2 = (bf16[256,1024]{1,0:T(8,128)(2,1)S(1)}, bf16[256,1024]{1,0:T(8,128)(2,1)}, u32[]{:S(2)}, u32[]{:S(2)}) collective-permute-start(bf16[256,1024]{1,0:T(8,128)(2,1)S(1)} %shard_map.29.one.own.unit), channel_id=1, source_target_pairs={{0,152},{1,153},{32,184},{33,185},{64,216},{65,217},{96,248},{97,2... | collective-permute-start | bytes 1572872 | tf_op jit(solution)/shard_map/ppermute | solution.py:38
  12.3 23.6 %collective-permute-start.6 = (bf16[256,1024]{1,0:T(8,128)(2,1)S(1)}, bf16[256,1024]{1,0:T(8,128)(2,1)S(1)}, u32[]{:S(2)}, u32[]{:S(2)}) collective-permute-start(bf16[256,1024]{1,0:T(8,128)(2,1)S(1)} %shard_map.29.one.own.unit), channel_id=1, source_target_pairs={{0,1},{1,2},{2,3},{3,4},{4,5},{5,6},{6,7},{7,8},{8,9},{9,10},{10,1... | collective-permute-start | bytes 1572872 | tf_op jit(solution)/shard_map/ppermute | solution.py:38
  24.9 12.4 %collective-permute-start.5 = (bf16[256,1024]{1,0:T(8,128)(2,1)S(1)}, bf16[256,1024]{1,0:T(8,128)(2,1)}, u32[]{:S(2)}, u32[]{:S(2)}) collective-permute-start(bf16[256,1024]{1,0:T(8,128)(2,1)S(1)} %shard_map.29.one.own.unit), channel_id=1, source_target_pairs={{30,32},{62,64},{94,96},{126,0},{129,255},{161,159},{193,191},{225... | collective-permute-start | bytes 1572872 | tf_op jit(solution)/shard_map/ppermute | solution.py:38
  26.4 13.7 %collective-permute-start.1 = (bf16[256,1024]{1,0:T(8,128)(2,1)S(1)}, bf16[256,1024]{1,0:T(8,128)(2,1)S(1)}, u32[]{:S(2)}, u32[]{:S(2)}) collective-permute-start(bf16[256,1024]{1,0:T(8,128)(2,1)S(1)} %collective-permute-done.other), channel_id=1, source_target_pairs={{0,1},{1,2},{2,3},{3,4},{4,5},{5,6},{6,7},{7,8},{8,9},{9,10},{10,1... | collective-permute-start | bytes 1572872 | tf_op jit(solution)/shard_map/ppermute | solution.py:38
  27.7 19.8 %collective-permute-start.3 = (bf16[256,1024]{1,0:T(8,128)(2,1)}, bf16[256,1024]{1,0:T(8,128)(2,1)S(1)}, u32[]{:S(2)}, u32[]{:S(2)}) collective-permute-start(bf16[256,1024]{1,0:T(8,128)(2,1)} %collective-permute-done.2), channel_id=1, source_target_pairs={{134,160},{135,32},{152,255},{153,127},{166,192},{167,64},{184,159... | collective-permute-start | bytes 1572872 | tf_op jit(solution)/shard_map/ppermute | solution.py:38
  29.0 19.9 %collective-permute-start.7 = (bf16[256,1024]{1,0:T(8,128)(2,1)S(1)}, bf16[256,1024]{1,0:T(8,128)(2,1)S(1)}, u32[]{:S(2)}, u32[]{:S(2)}) collective-permute-start(bf16[256,1024]{1,0:T(8,128)(2,1)S(1)} %shard_map.29.one.own.unit), channel_id=1, source_target_pairs={{0,256},{1,257},{2,258},{3,259},{4,260},{5,261},{6,262},{7,263},{8... | collective-permute-start | bytes 1572872 | tf_op jit(solution)/shard_map/ppermute | solution.py:38
  36.0 15.0 %collective-permute-start.8 = (bf16[256,1024]{1,0:T(8,128)(2,1)S(1)}, bf16[256,1024]{1,0:T(8,128)(2,1)}, u32[]{:S(2)}, u32[]{:S(2)}) collective-permute-start(bf16[256,1024]{1,0:T(8,128)(2,1)S(1)} %shard_map.33.one_a), channel_id=1, source_target_pairs={{0,1},{1,2},{2,3},{3,4},{4,5},{5,6},{6,7},{7,8},{8,9},{9,10},{10,1... | collective-permute-start | bytes 1572872 | tf_op jit(solution)/shard_map/ppermute | solution.py:38
  47.6 9.9 %collective-permute-start.4 = (bf16[256,1024]{1,0:T(8,128)(2,1)S(1)}, bf16[256,1024]{1,0:T(8,128)(2,1)S(1)}, u32[]{:S(2)}, u32[]{:S(2)}) collective-permute-start(bf16[256,1024]{1,0:T(8,128)(2,1)S(1)} %shard_map.30.one_b), channel_id=1, source_target_pairs={{0,1},{1,2},{2,3},{3,4},{4,5},{5,6},{6,7},{7,8},{8,9},{9,10},{10,1... | collective-permute-start | bytes 1572872 | tf_op jit(solution)/shard_map/ppermute | solution.py:38
  49.0 3.8 %collective-permute-start.9 = (bf16[256,1024]{1,0:T(8,128)(2,1)S(1)}, bf16[256,1024]{1,0:T(8,128)(2,1)S(1)}, u32[]{:S(2)}, u32[]{:S(2)}) collective-permute-start(bf16[256,1024]{1,0:T(8,128)(2,1)S(1)} %shard_map.34.one), channel_id=1, source_target_pairs={{0,128},{1,129},{2,130},{3,131},{4,132},{5,133},{6,134},{7,135},{8... | collective-permute-start | bytes 1572872 | tf_op jit(solution)/shard_map/ppermute | solution.py:38
  58.2 3.4 %collective-permute-start.10 = (bf16[128,1024]{1,0:T(8,128)(2,1)S(1)}, bf16[128,1024]{1,0:T(8,128)(2,1)S(1)}, u32[]{:S(2)}, u32[]{:S(2)}) collective-permute-start(bf16[128,1024]{1,0:T(8,128)(2,1)S(1)} %get-tuple-element.23), channel_id=1, source_target_pairs={{0,128},{1,129},{2,130},{3,131},{4,132},{5,133},{6,134},{7,135},{8... | collective-permute-start | bytes 786440 | tf_op jit(solution)/shard_map/ppermute | solution.py:38
  61.7 9.7 %collective-permute-start.12 = (bf16[128,1024]{1,0:T(8,128)(2,1)S(1)}, bf16[128,1024]{1,0:T(8,128)(2,1)S(1)}, u32[]{:S(2)}, u32[]{:S(2)}) collective-permute-start(bf16[128,1024]{1,0:T(8,128)(2,1)S(1)} %shard_map.40), channel_id=1, source_target_pairs={{0,256},{1,257},{2,258},{3,259},{4,260},{5,261},{6,262},{7,263},{8... | collective-permute-start | bytes 786440 | tf_op jit(solution)/shard_map/ppermute | solution.py:38
  65.5 5.9 %collective-permute-start.11 = (bf16[128,1024]{1,0:T(8,128)(2,1)S(1)}, bf16[128,1024]{1,0:T(8,128)(2,1)S(1)}, u32[]{:S(2)}, u32[]{:S(2)}) collective-permute-start(bf16[128,1024]{1,0:T(8,128)(2,1)S(1)} %get-tuple-element.24), channel_id=1, source_target_pairs={{0,128},{1,129},{2,130},{3,131},{4,132},{5,133},{6,134},{7,135},{8... | collective-permute-start | bytes 786440 | tf_op jit(solution)/shard_map/ppermute | solution.py:38
